TPU v7x, 32 devices: a whole 2x2x4 slice. The times are simulated.
32 devices in a mesh: fsdp: 8 (over y, x, core), head: 4 (over z).
Axes of the slice: x: 2, y: 2, z: 4, core: 2. Of those that a mesh axis runs over, the one named last changes fastest.
Arguments:
- images: bfloat16 [16, 577, 1024], P('fsdp'), may hold values from -6 to 6
- cotangent: bfloat16 [16, 577, 1024], P('fsdp'), may hold values from -6 to 6
- w_qkv: bfloat16 [2, 3, 1024, 1024], P(None, None, 'fsdp', 'head'), may hold values from -0.1875 to 0.1875
- w_out: bfloat16 [2, 1024, 1024], P(None, 'head', 'fsdp'), may hold values from -0.75 to 0.75
- w_in: bfloat16 [2, 1024, 4096], P(None, 'fsdp', 'head'), may hold values from -0.1875 to 0.1875
- w_down: bfloat16 [2, 4096, 1024], P(None, 'head', 'fsdp'), may hold values from -0.09375 to 0.09375
- qv_bias: bfloat16 [2, 2, 128, 8], P(None, None, 'head', 'fsdp'), may hold values from -3 to 3
- in_bias: bfloat16 [2, 512, 8], P(None, 'head', 'fsdp'), may hold values from -3 to 3
- gains: bfloat16 [2, 2, 1024], P(None, None, 'fsdp'), may hold values from 0.25 to 1.75
- shifts: bfloat16 [2, 4, 1024], P(None, None, 'fsdp'), may hold values from -2 to 2
Outputs:
- block_out: float32 [16, 577, 1024], P('fsdp')
- input_grad: float32 [16, 577, 1024], P('fsdp')
- grad_qkv: float32 [2, 3, 1024, 1024], P(None, None, 'fsdp', 'head')
- grad_out_proj: float32 [2, 1024, 1024], P(None, 'head', 'fsdp')
- grad_in_proj: float32 [2, 1024, 4096], P(None, 'fsdp', 'head')
- grad_down_proj: float32 [2, 4096, 1024], P(None, 'head', 'fsdp')
- grad_qv_bias: float32 [2, 2, 128, 8], P(None, None, 'head', 'fsdp')
- grad_in_bias: float32 [2, 512, 8], P(None, 'head', 'fsdp')
- grad_gains: float32 [2, 2, 1024], P(None, None, 'fsdp')
- grad_shifts: float32 [2, 4, 1024], P(None, None, 'fsdp')
All inputs are finite; a program needn't handle non-finite values.
Results may differ from a plain program's by a relative error of at most 0.019.
Values may be sent and summed in bfloat16 or wider, within the bound.
A program may use at most 256 MiB of HBM per device.

v0:
```python
from functools import partial

import jax
import jax.numpy as jnp
from jax import lax
from jax.sharding import PartitionSpec as P

D = 1024
HD = 64
LAYERS = 2


epsilon = 1e-06


def unpack(pieces):
    w_qkv, w_out, w_in, w_down, qv_bias, in_bias, gains, shifts = pieces
    local_width = w_qkv.shape[-1]
    hidden_width = w_in.shape[-1]
    return (
        w_qkv,
        w_out,
        w_in,
        w_down,
        qv_bias.astype(jnp.float32).reshape(2, local_width),
        in_bias.astype(jnp.float32).reshape(hidden_width),
        gains.astype(jnp.float32),
        shifts.astype(jnp.float32),
    )


def norm_rows(stream, gain, shift):
    average = jnp.mean(stream, axis=-1, keepdims=True)
    centred = stream - average
    inverse = lax.rsqrt(jnp.mean(centred * centred, axis=-1, keepdims=True) + epsilon)
    unit = centred * inverse
    return (unit * gain + shift, unit, inverse)


def norm_back(upstream, unit, inverse, gain):
    scaled = upstream * gain
    return inverse * (
        scaled
        - jnp.mean(scaled, axis=-1, keepdims=True)
        - unit * jnp.mean(scaled * unit, axis=-1, keepdims=True)
    )


def product(left, right, form):
    return jnp.einsum(form, left, right, preferred_element_type=jnp.float32)


def split_heads(rows):
    return rows.reshape(rows.shape[0], rows.shape[1] // HD, HD)


def layer_forward(stream, weights):
    w_qkv, w_out, w_in, w_down, qv_bias, in_bias, gains, shifts = weights
    normed, unit_first, inverse_first = norm_rows(stream, gains[0], shifts[0])
    normed = normed.astype(jnp.bfloat16)
    queries = (product(normed, w_qkv[0], "sd,da->sa") + qv_bias[0]).astype(jnp.bfloat16)
    key_rows = product(normed, w_qkv[1], "sd,da->sa").astype(jnp.bfloat16)
    value_rows = (product(normed, w_qkv[2], "sd,da->sa") + qv_bias[1]).astype(jnp.bfloat16)
    scores = product(split_heads(queries), split_heads(key_rows), "qhd,khd->hqk") * HD ** (-0.5)
    largest = jnp.max(scores, axis=-1, keepdims=True)
    logsum = largest + jnp.log(jnp.sum(jnp.exp(scores - largest), axis=-1, keepdims=True))
    soft_low = jnp.exp(scores - logsum).astype(jnp.bfloat16)
    attended = product(soft_low, split_heads(value_rows), "hqk,khd->qhd")
    attended = attended.reshape(queries.shape).astype(jnp.bfloat16)
    partial_rows = product(attended, w_out, "sa,ad->sd")
    branch = lax.psum(partial_rows.astype(jnp.bfloat16), "head").astype(jnp.float32)
    stream = stream + branch + shifts[2]
    normed_second, unit_second, inverse_second = norm_rows(stream, gains[1], shifts[1])
    normed_second = normed_second.astype(jnp.bfloat16)
    hidden = product(normed_second, w_in, "sd,df->sf") + in_bias
    active = jax.nn.gelu(hidden, approximate=False).astype(jnp.bfloat16)
    partial_rows = product(active, w_down, "sf,fd->sd")
    branch = lax.psum(partial_rows.astype(jnp.bfloat16), "head").astype(jnp.float32)
    stream = stream + branch + shifts[3]
    stored = (
        unit_first,
        inverse_first,
        normed,
        queries,
        key_rows,
        value_rows,
        logsum,
        attended,
        unit_second,
        inverse_second,
        normed_second,
        hidden,
        active,
    )
    return (stream, stored)


def layer_backward(upstream, weights, stored):
    w_qkv, w_out, w_in, w_down, qv_bias, in_bias, gains, shifts = weights
    (
        unit_first,
        inverse_first,
        normed,
        queries,
        key_rows,
        value_rows,
        logsum,
        attended,
        unit_second,
        inverse_second,
        normed_second,
        hidden,
        active,
    ) = stored
    shift_down = jnp.sum(upstream, axis=0)
    upstream_low = upstream.astype(jnp.bfloat16)
    grad_down = product(active, upstream_low, "sf,sd->fd")
    grad_active = product(upstream_low, w_down, "sd,fd->sf")
    unused, gelu_back = jax.vjp(partial(jax.nn.gelu, approximate=False), hidden)
    grad_hidden = gelu_back(grad_active)[0].astype(jnp.bfloat16)
    grad_in_bias = jnp.sum(grad_hidden.astype(jnp.float32), axis=0)
    grad_in = product(normed_second, grad_hidden, "sd,sf->df")
    partial_rows = product(grad_hidden, w_in, "sf,df->sd")
    grad_normed_second = lax.psum(partial_rows.astype(jnp.bfloat16), "head").astype(jnp.float32)
    gain_second = jnp.sum(grad_normed_second * unit_second, axis=0)
    shift_second = jnp.sum(grad_normed_second, axis=0)
    grad_mid = upstream + norm_back(grad_normed_second, unit_second, inverse_second, gains[1])
    shift_out = jnp.sum(grad_mid, axis=0)
    mid_low = grad_mid.astype(jnp.bfloat16)
    grad_out = product(attended, mid_low, "sa,sd->ad")
    grad_attended = product(mid_low, w_out, "sd,ad->sa").astype(jnp.bfloat16)
    query_heads = split_heads(queries)
    key_heads = split_heads(key_rows)
    value_heads = split_heads(value_rows)
    factor = HD ** (-0.5)
    soft = jnp.exp(product(query_heads, key_heads, "qhd,khd->hqk") * factor - logsum)
    soft_low = soft.astype(jnp.bfloat16)
    attended_heads = split_heads(grad_attended)
    grad_values = (
        product(soft_low, attended_heads, "hqk,qhd->khd")
        .reshape(queries.shape)
        .astype(jnp.bfloat16)
    )
    grad_soft = product(attended_heads, value_heads, "qhd,khd->hqk")
    grad_scores = (soft * (grad_soft - jnp.sum(grad_soft * soft, axis=-1, keepdims=True))).astype(
        jnp.bfloat16
    )
    grad_queries = (
        (product(grad_scores, key_heads, "hqk,khd->qhd") * factor)
        .reshape(queries.shape)
        .astype(jnp.bfloat16)
    )
    grad_keys = (
        (product(grad_scores, query_heads, "hqk,qhd->khd") * factor)
        .reshape(queries.shape)
        .astype(jnp.bfloat16)
    )
    grad_qv = jnp.stack(
        [
            jnp.sum(grad_queries.astype(jnp.float32), axis=0),
            jnp.sum(grad_values.astype(jnp.float32), axis=0),
        ]
    )
    grad_qkv = jnp.stack(
        [
            product(normed, grad_queries, "sd,sa->da"),
            product(normed, grad_keys, "sd,sa->da"),
            product(normed, grad_values, "sd,sa->da"),
        ]
    )
    partial_sum = (
        product(grad_queries, w_qkv[0], "sa,da->sd")
        + product(grad_keys, w_qkv[1], "sa,da->sd")
        + product(grad_values, w_qkv[2], "sa,da->sd")
    )
    grad_normed_first = lax.psum(partial_sum.astype(jnp.bfloat16), "head").astype(jnp.float32)
    gain_first = jnp.sum(grad_normed_first * unit_first, axis=0)
    shift_first = jnp.sum(grad_normed_first, axis=0)
    upstream = grad_mid + norm_back(grad_normed_first, unit_first, inverse_first, gains[0])
    layer_grads = (
        grad_qkv,
        grad_out,
        grad_in,
        grad_down,
        grad_qv,
        grad_in_bias,
        jnp.stack([gain_first, gain_second]),
        jnp.stack([shift_first, shift_second, shift_out, shift_down]),
    )
    return (upstream, layer_grads)


def body(images, cotangent, w_qkv, w_out, w_in, w_down, qv_bias, in_bias, gains, shifts):

    def fetch_forward(layer_index):
        return unpack(
            (
                lax.all_gather(w_qkv[layer_index], "fsdp", axis=1, tiled=True),
                lax.all_gather(w_out[layer_index], "fsdp", axis=1, tiled=True),
                lax.all_gather(w_in[layer_index], "fsdp", axis=0, tiled=True),
                lax.all_gather(w_down[layer_index], "fsdp", axis=1, tiled=True),
                lax.all_gather(qv_bias[layer_index], "fsdp", axis=2, tiled=True),
                lax.all_gather(in_bias[layer_index], "fsdp", axis=1, tiled=True),
                lax.all_gather(gains[layer_index], "fsdp", axis=1, tiled=True),
                lax.all_gather(shifts[layer_index], "fsdp", axis=1, tiled=True),
            )
        )

    def fetch_backward(layer_index):
        return unpack(
            (
                lax.all_gather(w_qkv[layer_index], "fsdp", axis=1, tiled=True),
                lax.all_gather(w_out[layer_index], "fsdp", axis=1, tiled=True),
                lax.all_gather(w_in[layer_index], "fsdp", axis=0, tiled=True),
                lax.all_gather(w_down[layer_index], "fsdp", axis=1, tiled=True),
                lax.all_gather(qv_bias[layer_index], "fsdp", axis=2, tiled=True),
                lax.all_gather(in_bias[layer_index], "fsdp", axis=1, tiled=True),
                lax.all_gather(gains[layer_index], "fsdp", axis=1, tiled=True),
                lax.all_gather(shifts[layer_index], "fsdp", axis=1, tiled=True),
            )
        )

    local_width = w_qkv.shape[3]
    hidden_width = w_in.shape[2]
    initial = (
        jnp.zeros((LAYERS, 3, D, local_width), jnp.float32),
        jnp.zeros((LAYERS, local_width, D), jnp.float32),
        jnp.zeros((LAYERS, D, hidden_width), jnp.float32),
        jnp.zeros((LAYERS, hidden_width, D), jnp.float32),
        jnp.zeros((LAYERS, 2, local_width), jnp.float32),
        jnp.zeros((LAYERS, hidden_width), jnp.float32),
        jnp.zeros((LAYERS, 2, D), jnp.float32),
        jnp.zeros((LAYERS, 4, D), jnp.float32),
    )

    def image_step(totals, inputs):
        one_image, grad_image = inputs
        stream = one_image.astype(jnp.float32)
        upstream = grad_image.astype(jnp.float32)
        stored_list = []
        for layer_index in range(LAYERS):
            stream, stored = layer_forward(stream, fetch_forward(layer_index))
            stored_list.append(stored)
        for layer_index in reversed(range(LAYERS)):
            upstream, layer_grads = layer_backward(
                upstream, fetch_backward(layer_index), stored_list[layer_index]
            )
            totals = tuple(
                (total.at[layer_index].add(term) for total, term in zip(totals, layer_grads))
            )
        return (totals, (stream, upstream))

    totals, (block_out, input_grad) = lax.scan(image_step, initial, (images, cotangent))
    fsdp_count = lax.axis_size("fsdp")
    grad_qv = totals[4].reshape(LAYERS, 2, qv_bias.shape[2], fsdp_count)
    grad_bias = totals[5].reshape(LAYERS, in_bias.shape[1], fsdp_count)
    summed = (
        lax.psum_scatter(
            totals[0].astype(jnp.bfloat16), "fsdp", scatter_dimension=2, tiled=True
        ).astype(jnp.float32),
        lax.psum_scatter(
            totals[1].astype(jnp.bfloat16), "fsdp", scatter_dimension=2, tiled=True
        ).astype(jnp.float32),
        lax.psum_scatter(
            totals[2].astype(jnp.bfloat16), "fsdp", scatter_dimension=1, tiled=True
        ).astype(jnp.float32),
        lax.psum_scatter(
            totals[3].astype(jnp.bfloat16), "fsdp", scatter_dimension=2, tiled=True
        ).astype(jnp.float32),
        lax.psum_scatter(
            grad_qv.astype(jnp.bfloat16), "fsdp", scatter_dimension=3, tiled=True
        ).astype(jnp.float32),
        lax.psum_scatter(
            grad_bias.astype(jnp.bfloat16), "fsdp", scatter_dimension=2, tiled=True
        ).astype(jnp.float32),
        lax.psum_scatter(
            totals[6].astype(jnp.bfloat16), "fsdp", scatter_dimension=2, tiled=True
        ).astype(jnp.float32),
        lax.psum_scatter(
            totals[7].astype(jnp.bfloat16), "fsdp", scatter_dimension=2, tiled=True
        ).astype(jnp.float32),
    )
    return (
        block_out,
        input_grad,
        summed[0],
        summed[1],
        summed[2],
        summed[3],
        summed[4],
        summed[5],
        summed[6],
        summed[7],
    )


def solution(mesh):
    placed = (
        P("fsdp", None, None),
        P("fsdp", None, None),
        P(None, None, "fsdp", "head"),
        P(None, "head", "fsdp"),
        P(None, "fsdp", "head"),
        P(None, "head", "fsdp"),
        P(None, None, "head", "fsdp"),
        P(None, "head", "fsdp"),
        P(None, None, "fsdp"),
        P(None, None, "fsdp"),
    )
    return jax.shard_map(
        body,
        mesh=mesh,
        in_specs=placed,
        out_specs=(
            P("fsdp", None, None),
            P("fsdp", None, None),
            P(None, None, "fsdp", "head"),
            P(None, "head", "fsdp"),
            P(None, "fsdp", "head"),
            P(None, "head", "fsdp"),
            P(None, None, "head", "fsdp"),
            P(None, "head", "fsdp"),
            P(None, None, "fsdp"),
            P(None, None, "fsdp"),
        ),
        check_vma=False,
    )
```

profile of v0, /device:TPU:1, one launch (start us, length us, event | category | flops | bytes accessed | tf_op | source)
XLA Modules:
  0.0 1987.0 jit_solution(9658690383721035021)
XLA Ops:
  28.6 1676.1 %while.47 = (s32[]{:T(128)}, f32[2,3,1024,256]{3,2,1,0:T(8,128)}, f32[2,256,1024]{2,1,0:T(8,128)}, f32[2,1024,1024]{2,1,0:T(8,128)}, f32[2,1024,1024]{2,1,0:T(8,...) while((s32[]{:T(128)}, f32[2,3,1024,256]{3,2,1,0:T(8,128)}, ...), condition=%wide.region_49.0_spmd, body=%wide.region_0.49_spmd.sunk | while | flops 24107284480 | bytes 845762304 | solution.py:253
  30.4 10.1 all-gather.37
  59.4 10.0 all-gather.38
  99.9 45.7 %all-reduce.14.cloned.1.call-done = bf16[577,1024]{1,0:T(8,128)(2,1)} async-done(((bf16[577,1024]{1,0:T(8,128)(2,1)}), bf16[577,1024]{1,0:T(8,128)(2,1)}) %all-reduce.14.cloned.1.call-update) | async-done | bytes 1181712 | tf_op jit(solution)/shard_map/while/body/eval_jaxpr/psum | solution.py:71
  148.1 27.7 %all-gather.55.cloned.1.call-done = bf16[1,1024,1024]{2,1,0:T(8,128)(2,1)} async-done(((bf16[1,128,1024]{2,1,0:T(8,128)(2,1)}), bf16[1,1024,1024]{2,1,0:T(8,128)(2,1)}) %all-gather.55.cloned.1.call-update) | async-done | bytes 2097168 | tf_op jit(solution)/shard_map/while/body/eval_jaxpr/all_gather | solution.py:200
  175.7 10.8 multiply_convert_fusion.8
  186.5 19.2 all-gather.59.cloned.1.call-done
  227.8 8.8 all-gather.40
  236.6 9.6 all-gather.46
  247.4 19.4 all-reduce.16.cloned.1.call-done
  271.4 22.9 %all-gather.63.cloned.1.call-done = bf16[1,3,1024,256]{3,2,1,0:T(8,128)(2,1)} async-done(((bf16[1,3,128,256]{3,2,1,0:T(8,128)(2,1)}), bf16[1,3,1024,256]{3,2,1,0:T(8,128)(2,1)}) %all-gather.63.cloned.1.call-update) | async-done | bytes 1572880 | tf_op jit(solution)/shard_map/while/body/eval_jaxpr/all_gather | solution.py:198
  317.6 8.9 all-gather.42
  328.6 44.1 %all-reduce.18.cloned.1.call-done = bf16[577,1024]{1,0:T(8,128)(2,1)} async-done(((bf16[577,1024]{1,0:T(8,128)(2,1)}), bf16[577,1024]{1,0:T(8,128)(2,1)}) %all-reduce.18.cloned.1.call-update) | async-done | bytes 1181712 | tf_op jit(solution)/shard_map/while/body/eval_jaxpr/psum | solution.py:71
  376.3 26.7 %all-gather.61.cloned.1.call-done = bf16[1,1024,1024]{2,1,0:T(8,128)(2,1)} async-done(((bf16[1,128,1024]{2,1,0:T(8,128)(2,1)}), bf16[1,1024,1024]{2,1,0:T(8,128)(2,1)}) %all-gather.61.cloned.1.call-update) | async-done | bytes 2097168 | tf_op jit(solution)/shard_map/while/body/eval_jaxpr/all_gather | solution.py:200
  402.9 10.5 multiply_convert_fusion.9
  413.4 19.6 all-gather.65.cloned.1.call-done
  460.4 38.5 %all-reduce.20.cloned.1.call-done = bf16[577,1024]{1,0:T(8,128)(2,1)} async-done(((bf16[577,1024]{1,0:T(8,128)(2,1)}), bf16[577,1024]{1,0:T(8,128)(2,1)}) %all-reduce.20.cloned.1.call-update) | async-done | bytes 1181712 | tf_op jit(solution)/shard_map/while/body/eval_jaxpr/psum | solution.py:124
  538.3 42.3 %all-reduce.22.cloned.1.call-done = bf16[577,1024]{1,0:T(8,128)(2,1)} async-done(((bf16[577,1024]{1,0:T(8,128)(2,1)}), bf16[577,1024]{1,0:T(8,128)(2,1)}) %all-reduce.22.cloned.1.call-update) | async-done | bytes 1181712 | tf_op jit(solution)/shard_map/while/body/eval_jaxpr/psum | solution.py:176
  600.2 49.0 %all-reduce.24.cloned.1.call-done = bf16[577,1024]{1,0:T(8,128)(2,1)} async-done(((bf16[577,1024]{1,0:T(8,128)(2,1)}), bf16[577,1024]{1,0:T(8,128)(2,1)}) %all-reduce.24.cloned.1.call-update) | async-done | bytes 1181712 | tf_op jit(solution)/shard_map/while/body/eval_jaxpr/psum | solution.py:124
  691.1 77.8 %all-reduce.26.cloned.1.call-done = (bf16[577,1024]{1,0:T(8,128)(2,1)}, bf16[577,1024]{1,0:T(8,128)(2,1)}) async-done(((bf16[577,1024]{1,0:T(8,128)(2,1)}, bf16[577,1024]{1,0:T(8,128)(2,1)}), (bf16[577,1024]{1,0:T(8,128)(2,1)}, bf16[577,1024]{1,0:T(8,128)(2,1)})) %all-reduce.26.cloned.1.call-update) | async-done | bytes 2363408 | tf_op jit(solution)/shard_map/while/body/eval_jaxpr/psum | solution.py:176
  782.0 41.5 %dynamic_update_slice.17 = f32[2,577,1024]{2,0,1:T(2,128)} dynamic-update-slice(f32[2,577,1024]{2,0,1:T(2,128)} %get-tuple-element.1144, f32[1,577,1024]{2,0,1:T(1,128)} %copy.194, s32[]{:T(128)S(6)} %copy.233, s32[]{:T(128)} %constant.680.clone.1..sunk, s32[]{:T(128)} %constant.680.clone.1..sunk) | dynamic-update-slice | bytes 4726788 | tf_op jit(solution)/shard_map/while/body/jit(dynamic_update_index_in_dim)/dynamic_update_slice | solution.py:253
  823.5 41.5 %dynamic_update_slice.18 = f32[2,577,1024]{2,0,1:T(2,128)} dynamic-update-slice(f32[2,577,1024]{2,0,1:T(2,128)} %get-tuple-element.1145, f32[1,577,1024]{2,0,1:T(1,128)} %copy.195, s32[]{:T(128)S(6)} %copy.233, s32[]{:T(128)} %constant.680.clone.1..sunk, s32[]{:T(128)} %constant.680.clone.1..sunk) | dynamic-update-slice | bytes 4726788 | tf_op jit(solution)/shard_map/while/body/jit(dynamic_update_index_in_dim)/dynamic_update_slice | solution.py:253
  867.5 9.2 all-gather.37
  895.7 10.0 all-gather.38
  936.3 43.3 %all-reduce.14.cloned.1.call-done = bf16[577,1024]{1,0:T(8,128)(2,1)} async-done(((bf16[577,1024]{1,0:T(8,128)(2,1)}), bf16[577,1024]{1,0:T(8,128)(2,1)}) %all-reduce.14.cloned.1.call-update) | async-done | bytes 1181712 | tf_op jit(solution)/shard_map/while/body/eval_jaxpr/psum | solution.py:71
  982.2 27.5 %all-gather.55.cloned.1.call-done = bf16[1,1024,1024]{2,1,0:T(8,128)(2,1)} async-done(((bf16[1,128,1024]{2,1,0:T(8,128)(2,1)}), bf16[1,1024,1024]{2,1,0:T(8,128)(2,1)}) %all-gather.55.cloned.1.call-update) | async-done | bytes 2097168 | tf_op jit(solution)/shard_map/while/body/eval_jaxpr/all_gather | solution.py:200
  1009.7 10.8 multiply_convert_fusion.8
  1020.5 19.2 all-gather.59.cloned.1.call-done
  1070.7 9.2 all-gather.46
  1081.2 19.7 all-reduce.16.cloned.1.call-done
  1105.4 23.0 %all-gather.63.cloned.1.call-done = bf16[1,3,1024,256]{3,2,1,0:T(8,128)(2,1)} async-done(((bf16[1,3,128,256]{3,2,1,0:T(8,128)(2,1)}), bf16[1,3,1024,256]{3,2,1,0:T(8,128)(2,1)}) %all-gather.63.cloned.1.call-update) | async-done | bytes 1572880 | tf_op jit(solution)/shard_map/while/body/eval_jaxpr/all_gather | solution.py:198
  1151.7 9.0 all-gather.42
  1162.7 44.1 %all-reduce.18.cloned.1.call-done = bf16[577,1024]{1,0:T(8,128)(2,1)} async-done(((bf16[577,1024]{1,0:T(8,128)(2,1)}), bf16[577,1024]{1,0:T(8,128)(2,1)}) %all-reduce.18.cloned.1.call-update) | async-done | bytes 1181712 | tf_op jit(solution)/shard_map/while/body/eval_jaxpr/psum | solution.py:71
  1210.3 26.7 %all-gather.61.cloned.1.call-done = bf16[1,1024,1024]{2,1,0:T(8,128)(2,1)} async-done(((bf16[1,128,1024]{2,1,0:T(8,128)(2,1)}), bf16[1,1024,1024]{2,1,0:T(8,128)(2,1)}) %all-gather.61.cloned.1.call-update) | async-done | bytes 2097168 | tf_op jit(solution)/shard_map/while/body/eval_jaxpr/all_gather | solution.py:200
  1237.0 10.5 multiply_convert_fusion.9
  1247.5 19.6 all-gather.65.cloned.1.call-done
  1294.6 38.4 %all-reduce.20.cloned.1.call-done = bf16[577,1024]{1,0:T(8,128)(2,1)} async-done(((bf16[577,1024]{1,0:T(8,128)(2,1)}), bf16[577,1024]{1,0:T(8,128)(2,1)}) %all-reduce.20.cloned.1.call-update) | async-done | bytes 1181712 | tf_op jit(solution)/shard_map/while/body/eval_jaxpr/psum | solution.py:124
  1372.1 42.3 %all-reduce.22.cloned.1.call-done = bf16[577,1024]{1,0:T(8,128)(2,1)} async-done(((bf16[577,1024]{1,0:T(8,128)(2,1)}), bf16[577,1024]{1,0:T(8,128)(2,1)}) %all-reduce.22.cloned.1.call-update) | async-done | bytes 1181712 | tf_op jit(solution)/shard_map/while/body/eval_jaxpr/psum | solution.py:176
  1434.0 49.0 %all-reduce.24.cloned.1.call-done = bf16[577,1024]{1,0:T(8,128)(2,1)} async-done(((bf16[577,1024]{1,0:T(8,128)(2,1)}), bf16[577,1024]{1,0:T(8,128)(2,1)}) %all-reduce.24.cloned.1.call-update) | async-done | bytes 1181712 | tf_op jit(solution)/shard_map/while/body/eval_jaxpr/psum | solution.py:124
  1525.1 77.6 %all-reduce.26.cloned.1.call-done = (bf16[577,1024]{1,0:T(8,128)(2,1)}, bf16[577,1024]{1,0:T(8,128)(2,1)}) async-done(((bf16[577,1024]{1,0:T(8,128)(2,1)}, bf16[577,1024]{1,0:T(8,128)(2,1)}), (bf16[577,1024]{1,0:T(8,128)(2,1)}, bf16[577,1024]{1,0:T(8,128)(2,1)})) %all-reduce.26.cloned.1.call-update) | async-done | bytes 2363408 | tf_op jit(solution)/shard_map/while/body/eval_jaxpr/psum | solution.py:176
  1615.8 41.5 %dynamic_update_slice.17 = f32[2,577,1024]{2,0,1:T(2,128)} dynamic-update-slice(f32[2,577,1024]{2,0,1:T(2,128)} %get-tuple-element.1144, f32[1,577,1024]{2,0,1:T(1,128)} %copy.194, s32[]{:T(128)S(6)} %copy.233, s32[]{:T(128)} %constant.680.clone.1..sunk, s32[]{:T(128)} %constant.680.clone.1..sunk) | dynamic-update-slice | bytes 4726788 | tf_op jit(solution)/shard_map/while/body/jit(dynamic_update_index_in_dim)/dynamic_update_slice | solution.py:253
  1657.3 41.5 %dynamic_update_slice.18 = f32[2,577,1024]{2,0,1:T(2,128)} dynamic-update-slice(f32[2,577,1024]{2,0,1:T(2,128)} %get-tuple-element.1145, f32[1,577,1024]{2,0,1:T(1,128)} %copy.195, s32[]{:T(128)S(6)} %copy.233, s32[]{:T(128)} %constant.680.clone.1..sunk, s32[]{:T(128)} %constant.680.clone.1..sunk) | dynamic-update-slice | bytes 4726788 | tf_op jit(solution)/shard_map/while/body/jit(dynamic_update_index_in_dim)/dynamic_update_slice | solution.py:253
  1724.3 11.4 copy.146
  1749.1 21.5 %all-reduce.3 = (bf16[2,2,32,8]{2,1,0,3:T(2,128)(2,1)S(1)}, bf16[2,128,8]{1,0,2:T(2,128)(2,1)S(1)}) all-reduce(bf16[2,2,32,8]{2,1,0,3:T(2,128)(2,1)S(1)} %copy.130, bf16[2,128,8]{1,0,2:T(2,128)(2,1)S(1)} %copy.131), channel_id=22, replica_groups=mesh['fsdp'=8,'head'=4] {'fsdp'}, use_global_device_ids=true, to_apply=%region_54.0.clone | all-reduce | flops 3072 | bytes 12288
  1779.9 38.3 %reduce-scatter.19.cloned.1.call-done = bf16[128,512]{1,0:T(8,128)(2,1)} async-done(((bf16[1024,512]{1,0:T(8,128)(2,1)}), bf16[128,512]{1,0:T(8,128)(2,1)}) %reduce-scatter.19.cloned.1.call-update) | async-done | bytes 131088
  1820.1 47.9 %reduce-scatter.15.cloned.1.call-done = bf16[2,3,128,256]{3,2,1,0:T(8,128)(2,1)} async-done(((bf16[2,3,1024,256]{3,2,1,0:T(8,128)(2,1)}), bf16[2,3,128,256]{3,2,1,0:T(8,128)(2,1)}) %reduce-scatter.15.cloned.1.call-update) | async-done | bytes 393232 | tf_op jit(solution)/shard_map/reduce_scatter | solution.py:258
  1869.9 53.0 %reduce-scatter.21.cloned.1.call-done = bf16[128,2048]{1,0:T(8,128)(2,1)} async-done(((bf16[1024,2048]{1,0:T(8,128)(2,1)}), bf16[128,2048]{1,0:T(8,128)(2,1)}) %reduce-scatter.21.cloned.1.call-update) | async-done | bytes 524304
  1925.9 51.6 %reduce-scatter.17.cloned.1.call-done = bf16[2,128,1024]{2,1,0:T(8,128)(2,1)} async-done(((bf16[2,1024,1024]{2,1,0:T(8,128)(2,1)}), bf16[2,128,1024]{2,1,0:T(8,128)(2,1)}) %reduce-scatter.17.cloned.1.call-update) | async-done | bytes 524304 | tf_op jit(solution)/shard_map/reduce_scatter | solution.py:264
  (779 shorter events, 582.7 us)
Async XLA Ops:
  28.9 146.9 %copy-start.2 = (bf16[2,577,1024]{2,1,0:T(8,128)(2,1)}, bf16[2,577,1024]{2,1,0:T(8,128)(2,1)S(1)}, u32[]{:S(2)}) copy-start(bf16[2,577,1024]{2,1,0:T(8,128)(2,1)S(1)} %get-tuple-element.1169) | copy-start | bytes 7090180 | tf_op jit(solution)/shard_map/while
  28.9 43.8 %all-gather.57.cloned.1.call-start = ((), (), s32[]{:S(2)}) async-start(), calls=%async_computation.13 | async-start | bytes 1769472 | tf_op jit(solution)/shard_map/while/body/eval_jaxpr/all_gather | solution.py:198
  29.8 115.7 %all-reduce.14.cloned.1.call-start = ((), (), s32[]{:S(2)}) async-start(), calls=%async_computation.14 | async-start | bytes 2392064 | tf_op jit(solution)/shard_map/while/body/eval_jaxpr/psum | solution.py:71
  88.7 87.1 %all-gather.55.cloned.1.call-start = ((), (), s32[]{:S(2)}) async-start(), calls=%async_computation.12 | async-start | bytes 2359296 | tf_op jit(solution)/shard_map/while/body/eval_jaxpr/all_gather | solution.py:200
  89.6 116.1 %all-gather.59.cloned.1.call-start = ((), (), s32[]{:S(2)}) async-start(), calls=%async_computation.15 | async-start | bytes 2359296 | tf_op jit(solution)/shard_map/while/body/eval_jaxpr/all_gather | solution.py:201
  91.5 175.3 %all-reduce.16.cloned.1.call-start = ((), (), s32[]{:S(2)}) async-start(), calls=%async_computation.16 | async-start | bytes 2392064 | tf_op jit(solution)/shard_map/while/body/eval_jaxpr/psum | solution.py:78
  99.9 75.9 %copy-start.67 = (f32[1024]{0:T(1024)}, f32[1024]{0:T(1024)S(1)}, u32[]{:S(2)}) copy-start(f32[1024]{0:T(1024)S(1)} %reshape.1126) | copy-start | bytes 12292 | tf_op jit(solution)/shard_map/while
  205.7 61.2 %copy-start.60 = (f32[1,1,1024]{2,1,0:T(1,128)S(1)}, f32[1,1,1024]{2,1,0:T(1,128)}, u32[]{:S(2)}) copy-start(f32[1,1,1024]{2,1,0:T(1,128)} %get-tuple-element.1024) | copy-start | bytes 12292 | tf_op jit(solution)/shard_map/while
  210.2 84.1 %all-gather.63.cloned.1.call-start = ((), (), s32[]{:S(2)}) async-start(), calls=%async_computation.18 | async-start | bytes 1769472 | tf_op jit(solution)/shard_map/while/body/eval_jaxpr/all_gather | solution.py:198
  210.8 161.9 %all-reduce.18.cloned.1.call-start = ((), (), s32[]{:S(2)}) async-start(), calls=%async_computation.19 | async-start | bytes 2392064 | tf_op jit(solution)/shard_map/while/body/eval_jaxpr/psum | solution.py:71
  316.1 86.8 %all-gather.61.cloned.1.call-start = ((), (), s32[]{:S(2)}) async-start(), calls=%async_computation.17 | async-start | bytes 2359296 | tf_op jit(solution)/shard_map/while/body/eval_jaxpr/all_gather | solution.py:200
  316.8 116.2 %all-gather.65.cloned.1.call-start = ((), (), s32[]{:S(2)}) async-start(), calls=%async_computation.20 | async-start | bytes 2359296 | tf_op jit(solution)/shard_map/while/body/eval_jaxpr/all_gather | solution.py:215
  317.6 181.4 %all-reduce.20.cloned.1.call-start = ((), (), s32[]{:S(2)}) async-start(), calls=%async_computation.21 | async-start | bytes 2392064 | tf_op jit(solution)/shard_map/while/body/eval_jaxpr/psum | solution.py:124
  442.3 138.3 %all-reduce.22.cloned.1.call-start = ((), (), s32[]{:S(2)}) async-start(), calls=%async_computation.22 | async-start | bytes 2392064 | tf_op jit(solution)/shard_map/while/body/eval_jaxpr/psum | solution.py:176
  524.1 125.1 %all-reduce.24.cloned.1.call-start = ((), (), s32[]{:S(2)}) async-start(), calls=%async_computation.23 | async-start | bytes 2392064 | tf_op jit(solution)/shard_map/while/body/eval_jaxpr/psum | solution.py:124
  592.7 176.2 %all-reduce.26.cloned.1.call-start = ((), (), s32[]{:S(2)}) async-start(), calls=%async_computation.24 | async-start | bytes 4784128 | tf_op jit(solution)/shard_map/while/body/eval_jaxpr/psum | solution.py:176
  593.0 56.3 %copy-start.3 = (bf16[2,577,1024]{2,1,0:T(8,128)(2,1)S(1)}, bf16[2,577,1024]{2,1,0:T(8,128)(2,1)}, u32[]{:S(2)}) copy-start(bf16[2,577,1024]{2,1,0:T(8,128)(2,1)} %copy-done.2) | copy-start | bytes 7090180 | tf_op jit(solution)/shard_map/while
  593.0 56.3 %copy-start.55 = (f32[1,1,1024]{2,1,0:T(1,128)S(1)}, f32[1,1,1024]{2,1,0:T(1,128)}, u32[]{:S(2)}) copy-start(f32[1,1,1024]{2,1,0:T(1,128)} %get-tuple-element.1029) | copy-start | bytes 12292 | tf_op jit(solution)/shard_map/while
  686.9 82.0 %copy-start.46 = (f32[577]{0:T(1024)S(1)}, f32[577]{0:T(1024)}, u32[]{:S(2)}) copy-start(f32[577]{0:T(1024)} %copy-done.45) | copy-start | bytes 6928 | tf_op jit(solution)/shard_map/while
  686.9 82.0 %copy-start.49 = (f32[577]{0:T(1024)S(1)}, f32[577]{0:T(1024)}, u32[]{:S(2)}) copy-start(f32[577]{0:T(1024)} %copy-done.48) | copy-start | bytes 6928 | tf_op jit(solution)/shard_map/while
  686.9 82.0 %copy-start.51 = (f32[1,1,1024]{2,1,0:T(1,128)S(1)}, f32[1,1,1024]{2,1,0:T(1,128)}, u32[]{:S(2)}) copy-start(f32[1,1,1024]{2,1,0:T(1,128)} %copy-done.50) | copy-start | bytes 12292 | tf_op jit(solution)/shard_map/while
  866.0 143.7 %copy-start.2 = (bf16[2,577,1024]{2,1,0:T(8,128)(2,1)}, bf16[2,577,1024]{2,1,0:T(8,128)(2,1)S(1)}, u32[]{:S(2)}) copy-start(bf16[2,577,1024]{2,1,0:T(8,128)(2,1)S(1)} %get-tuple-element.1169) | copy-start | bytes 7090180 | tf_op jit(solution)/shard_map/while
  866.0 42.9 %all-gather.57.cloned.1.call-start = ((), (), s32[]{:S(2)}) async-start(), calls=%async_computation.13 | async-start | bytes 1769472 | tf_op jit(solution)/shard_map/while/body/eval_jaxpr/all_gather | solution.py:198
  867.0 112.7 %all-reduce.14.cloned.1.call-start = ((), (), s32[]{:S(2)}) async-start(), calls=%async_computation.14 | async-start | bytes 2392064 | tf_op jit(solution)/shard_map/while/body/eval_jaxpr/psum | solution.py:71
  924.9 84.8 %all-gather.55.cloned.1.call-start = ((), (), s32[]{:S(2)}) async-start(), calls=%async_computation.12 | async-start | bytes 2359296 | tf_op jit(solution)/shard_map/while/body/eval_jaxpr/all_gather | solution.py:200
  925.8 113.8 %all-gather.59.cloned.1.call-start = ((), (), s32[]{:S(2)}) async-start(), calls=%async_computation.15 | async-start | bytes 2359296 | tf_op jit(solution)/shard_map/while/body/eval_jaxpr/all_gather | solution.py:201
  927.8 173.0 %all-reduce.16.cloned.1.call-start = ((), (), s32[]{:S(2)}) async-start(), calls=%async_computation.16 | async-start | bytes 2392064 | tf_op jit(solution)/shard_map/while/body/eval_jaxpr/psum | solution.py:78
  936.3 73.4 %copy-start.67 = (f32[1024]{0:T(1024)}, f32[1024]{0:T(1024)S(1)}, u32[]{:S(2)}) copy-start(f32[1024]{0:T(1024)S(1)} %reshape.1126) | copy-start | bytes 12292 | tf_op jit(solution)/shard_map/while
  1039.6 61.2 %copy-start.60 = (f32[1,1,1024]{2,1,0:T(1,128)S(1)}, f32[1,1,1024]{2,1,0:T(1,128)}, u32[]{:S(2)}) copy-start(f32[1,1,1024]{2,1,0:T(1,128)} %get-tuple-element.1024) | copy-start | bytes 12292 | tf_op jit(solution)/shard_map/while
  1044.1 84.3 %all-gather.63.cloned.1.call-start = ((), (), s32[]{:S(2)}) async-start(), calls=%async_computation.18 | async-start | bytes 1769472 | tf_op jit(solution)/shard_map/while/body/eval_jaxpr/all_gather | solution.py:198
  1044.9 161.9 %all-reduce.18.cloned.1.call-start = ((), (), s32[]{:S(2)}) async-start(), calls=%async_computation.19 | async-start | bytes 2392064 | tf_op jit(solution)/shard_map/while/body/eval_jaxpr/psum | solution.py:71
  1150.2 86.9 %all-gather.61.cloned.1.call-start = ((), (), s32[]{:S(2)}) async-start(), calls=%async_computation.17 | async-start | bytes 2359296 | tf_op jit(solution)/shard_map/while/body/eval_jaxpr/all_gather | solution.py:200
  1150.9 116.2 %all-gather.65.cloned.1.call-start = ((), (), s32[]{:S(2)}) async-start(), calls=%async_computation.20 | async-start | bytes 2359296 | tf_op jit(solution)/shard_map/while/body/eval_jaxpr/all_gather | solution.py:215
  1151.6 181.4 %all-reduce.20.cloned.1.call-start = ((), (), s32[]{:S(2)}) async-start(), calls=%async_computation.21 | async-start | bytes 2392064 | tf_op jit(solution)/shard_map/while/body/eval_jaxpr/psum | solution.py:124
  1276.4 138.0 %all-reduce.22.cloned.1.call-start = ((), (), s32[]{:S(2)}) async-start(), calls=%async_computation.22 | async-start | bytes 2392064 | tf_op jit(solution)/shard_map/while/body/eval_jaxpr/psum | solution.py:176
  1357.9 125.1 %all-reduce.24.cloned.1.call-start = ((), (), s32[]{:S(2)}) async-start(), calls=%async_computation.23 | async-start | bytes 2392064 | tf_op jit(solution)/shard_map/while/body/eval_jaxpr/psum | solution.py:124
  1426.5 176.2 %all-reduce.26.cloned.1.call-start = ((), (), s32[]{:S(2)}) async-start(), calls=%async_computation.24 | async-start | bytes 4784128 | tf_op jit(solution)/shard_map/while/body/eval_jaxpr/psum | solution.py:176
  1426.7 56.3 %copy-start.3 = (bf16[2,577,1024]{2,1,0:T(8,128)(2,1)S(1)}, bf16[2,577,1024]{2,1,0:T(8,128)(2,1)}, u32[]{:S(2)}) copy-start(bf16[2,577,1024]{2,1,0:T(8,128)(2,1)} %copy-done.2) | copy-start | bytes 7090180 | tf_op jit(solution)/shard_map/while
  1426.8 56.3 %copy-start.55 = (f32[1,1,1024]{2,1,0:T(1,128)S(1)}, f32[1,1,1024]{2,1,0:T(1,128)}, u32[]{:S(2)}) copy-start(f32[1,1,1024]{2,1,0:T(1,128)} %get-tuple-element.1029) | copy-start | bytes 12292 | tf_op jit(solution)/shard_map/while
  1520.8 82.0 %copy-start.46 = (f32[577]{0:T(1024)S(1)}, f32[577]{0:T(1024)}, u32[]{:S(2)}) copy-start(f32[577]{0:T(1024)} %copy-done.45) | copy-start | bytes 6928 | tf_op jit(solution)/shard_map/while
  1520.8 82.0 %copy-start.49 = (f32[577]{0:T(1024)S(1)}, f32[577]{0:T(1024)}, u32[]{:S(2)}) copy-start(f32[577]{0:T(1024)} %copy-done.48) | copy-start | bytes 6928 | tf_op jit(solution)/shard_map/while
  1520.8 82.0 %copy-start.51 = (f32[1,1,1024]{2,1,0:T(1,128)S(1)}, f32[1,1,1024]{2,1,0:T(1,128)}, u32[]{:S(2)}) copy-start(f32[1,1,1024]{2,1,0:T(1,128)} %copy-done.50) | copy-start | bytes 12292 | tf_op jit(solution)/shard_map/while
  1704.8 68.3 %reduce-scatter.23.cloned.1.call-start = ((), (), s32[]{:S(2)}) async-start(), calls=%async_computation.10 | async-start | bytes 294912
  1707.0 71.4 %reduce-scatter.25.cloned.1.call-start = ((), (), s32[]{:S(2)}) async-start(), calls=%async_computation.11 | async-start | bytes 294912
  1709.3 109.0 %reduce-scatter.19.cloned.1.call-start = ((), (), s32[]{:S(2)}) async-start(), calls=%async_computation.8 | async-start | bytes 1179648
  1713.2 154.8 %reduce-scatter.15.cloned.1.call-start = ((), (), s32[]{:S(2)}) async-start(), calls=%async_computation.6 | async-start | bytes 3538944 | tf_op jit(solution)/shard_map/reduce_scatter | solution.py:258
  1718.1 204.8 %reduce-scatter.21.cloned.1.call-start = ((), (), s32[]{:S(2)}) async-start(), calls=%async_computation.9 | async-start | bytes 4718592
  1741.3 236.2 %reduce-scatter.17.cloned.1.call-start = ((), (), s32[]{:S(2)}) async-start(), calls=%async_computation.7 | async-start | bytes 4718592 | tf_op jit(solution)/shard_map/reduce_scatter | solution.py:264
  (168 other events, 1368.9 us)
Sparse Core Ops, SparseCore 0:
  32.3 28.2 all-gather.56
  88.8 56.6 all-reduce.13
  148.0 27.6 all-gather.54
  177.5 28.1 all-gather.58
  210.3 56.5 all-reduce.15
  268.8 25.4 all-gather.62
  316.2 56.4 all-reduce.17
  375.2 27.6 all-gather.60
  404.8 28.1 all-gather.64
  442.4 56.5 all-reduce.19
  524.2 56.3 all-reduce.21
  592.9 56.2 all-reduce.23
  672.5 96.3 all-reduce.25
  869.2 25.2 all-gather.56
  925.0 54.5 all-reduce.13
  981.9 27.6 all-gather.54
  1011.4 28.1 all-gather.58
  1044.3 56.5 all-reduce.15
  1102.9 25.4 all-gather.62
  1150.3 56.4 all-reduce.17
  1209.3 27.6 all-gather.60
  1238.9 28.1 all-gather.64
  1276.5 56.5 all-reduce.19
  1358.0 56.2 all-reduce.21
  1426.7 56.2 all-reduce.23
  1506.3 96.3 all-reduce.25
Sparse Core Ops, SparseCore 1:
  1708.8 32.1 reduce-scatter.22
  1744.8 33.6 reduce-scatter.24
  1782.0 36.2 reduce-scatter.18
  1821.7 46.2 reduce-scatter.14
  1871.7 51.1 reduce-scatter.20
  1926.3 51.2 reduce-scatter.16
where the time goes:
time: 2010 us; the launch traced here: 1990 us
  waiting for transfers between devices  1060 us (53%)
  local copies, waits for them, and re-layouts  305 us (15%)
  matrix products  276 us (14%)
  blocking collectives  198 us (10%)
  other arithmetic  121 us (6%)
    dot_general x96, matrix products, product(): return jnp.einsum(form, left, right, preferred_element_type=jnp.float32)  276 us
    psum x4, waiting for transfers between devices, layer_backward(): lax.psum(partial_sum.astype(jnp.bfloat16), 'head').astype(jnp.float32)  240 us
    psum x6, waiting for transfers between devices, layer_forward(): lax.psum(partial_rows.astype(jnp.bfloat16), 'head').astype(jnp.float32)  216 us
    dynamic_update_slice x8, local copies, waits for them, and re-layouts, body(): lax.scan(image_step, initial, (images, cotangent))  181 us
    psum x4, waiting for transfers between devices, layer_backward(): lax.psum(partial_rows.astype(jnp.bfloat16), 'head').astype(jnp.float32)  175 us
    all_gather x4, waiting for transfers between devices, fetch_forward(): lax.all_gather(w_in[layer_index], 'fsdp', axis=0, tiled=True)  109 us
    unnamed x10, waiting for transfers between devices  95.3 us
    reduce_scatter x1, waiting for transfers between devices, body(): lax.psum_scatter(totals[2].astype(jnp.bfloat16), 'fsdp', scatter_dimensio...  51.6 us
  transfers between devices with their start and end apart: 32, of which 29 were waited for; matrix products, arithmetic and copies ran while one was open for 13% of the time, Pallas kernels for 0%

commit v1 on v0

v1 whole, which is shorter than its diff:
```python
import functools

import jax
import jax.numpy as jnp
from jax import lax
from jax.sharding import PartitionSpec as P

HD = 64
LAYERS = 2
TP = 4
AXES = ("fsdp", "head")
epsilon = 1e-06


def product(left, right, form):
    return jnp.einsum(form, left, right, preferred_element_type=jnp.float32)


def low(v):
    return v.astype(jnp.bfloat16)


def wide(v):
    return v.astype(jnp.float32)


class Places:
    def __init__(self, fsdp, head):
        self.fsdp, self.head = fsdp, head
        self.blocks = fsdp // TP
        index, plane = lax.axis_index("fsdp"), lax.axis_index("head")
        self.block, self.role, self.plane = index // TP, index % TP, plane

    def pairs(self, move, sends=None):
        found = []
        for block in range(self.blocks):
            for role in range(TP):
                for plane in range(self.head):
                    if sends is not None and not sends(block, role, plane):
                        continue
                    to_block, to_role, to_plane = move(block, role, plane)
                    found.append(
                        (
                            (block * TP + role) * self.head + plane,
                            (to_block * TP + to_role) * self.head + to_plane,
                        )
                    )
        return found

    def role_xor(self, v, bits, sends=None):
        return lax.ppermute(v, AXES, self.pairs(lambda b, r, p: (b, r ^ bits, p), sends))

    def plane_xor(self, v, bits, sends=None):
        return lax.ppermute(v, AXES, self.pairs(lambda b, r, p: (b, r, p ^ bits), sends))

    def block_shift(self, v, step):
        return lax.ppermute(v, AXES, self.pairs(lambda b, r, p: ((b + step) % self.blocks, r, p)))


def pick(parts, index):
    return lax.dynamic_index_in_dim(jnp.stack(parts), index, 0, keepdims=False)


def by_xor(parts, index):
    a, b, c, d = parts
    odd = (index & 1) == 1
    a, b = jnp.where(odd, b, a), jnp.where(odd, a, b)
    c, d = jnp.where(odd, d, c), jnp.where(odd, c, d)
    top = (index & 2) == 2
    return [jnp.where(top, c, a), jnp.where(top, d, b), jnp.where(top, a, c), jnp.where(top, b, d)]


def gather_group(pl, pack):
    exchanged = [lax.dynamic_index_in_dim(pack, pl.role, 0, False)]
    for bits in (1, 2, 3):
        exchanged.append(pl.role_xor(lax.dynamic_index_in_dim(pack, pl.role ^ bits, 0, False), bits))
    piece = jnp.concatenate(by_xor(exchanged, pl.role), axis=-1)
    planes = [piece] + [pl.plane_xor(piece, bits) for bits in (1, 2, 3)]
    planes = jnp.stack(planes, axis=1)
    if pl.blocks == 2:
        other = pl.block_shift(planes, 1)
        first = pl.block == 0
        both = [jnp.where(first, planes, other), jnp.where(first, other, planes)]
    else:
        shifted = jnp.stack([planes] + [pl.block_shift(planes, s) for s in range(1, pl.blocks)])
        both = [
            lax.dynamic_index_in_dim(shifted, (pl.block - b) % pl.blocks, 0, False)
            for b in range(pl.blocks)
        ]
    whole = jnp.concatenate(both, axis=-1)
    return whole.reshape(whole.shape[0], whole.shape[1] * whole.shape[2], whole.shape[3])


def scatter_group(pl, grads):
    mats, rows, width = grads.shape
    grads = grads.reshape(mats, pl.head, rows // pl.head, pl.blocks, width // pl.blocks)
    total = lax.dynamic_index_in_dim(grads, pl.block, 3, False)
    for step in range(1, pl.blocks):
        sent = lax.dynamic_index_in_dim(grads, (pl.block + step) % pl.blocks, 3, False)
        total = total + wide(pl.block_shift(low(sent), step))
    mine = total[:, 0]
    for bits in (1, 2, 3):
        mine = mine + wide(pl.plane_xor(low(total[:, bits]), bits))
    mine = low(mine).reshape(mats, rows // pl.head, TP, -1)
    exchanged = [lax.dynamic_index_in_dim(mine, pl.role, 2, False)]
    for bits in (1, 2, 3):
        exchanged.append(pl.role_xor(lax.dynamic_index_in_dim(mine, pl.role ^ bits, 2, False), bits))
    return wide(jnp.stack(by_xor(exchanged, pl.role)))


def sum_roles(pl, rows):
    half = rows.shape[1] // 2
    core = pl.role & 1
    rows = low(rows)
    kept = jnp.where(core == 0, rows[:, :half], rows[:, half:])
    sent = jnp.where(core == 0, rows[:, half:], rows[:, :half])
    chip = low(wide(kept) + wide(pl.role_xor(sent, 1)))
    total = low(wide(chip) + wide(pl.role_xor(chip, 2)))
    other = pl.role_xor(total, 1)
    return wide(
        jnp.concatenate(
            [jnp.where(core == 0, total, other), jnp.where(core == 0, other, total)], axis=1
        )
    )


def share_images(pl, held):
    own = lax.dynamic_index_in_dim(held, pl.plane // 2, 0, False)
    owner = lambda b, r, p: (r & 1) == (p & 1)
    other = pl.role_xor(own, 2, owner)
    top = pl.role >= 2
    pair = jnp.stack([jnp.where(top, other, own), jnp.where(top, own, other)])
    passed = pl.role_xor(pair, 1, owner)
    return jnp.where((pl.role & 1) == (pl.plane & 1), pair, passed)


def return_images(pl, pair):
    mine = low(jnp.where(pl.role >= 2, pair[1], pair[0]))
    owner = lambda b, r, p: (r & 1) == (p & 1)
    one, two, three = [pl.plane_xor(mine, bits, owner) for bits in (1, 2, 3)]
    odd = (pl.role & 1) != (pl.plane & 1)
    near = jnp.where(odd, one, mine)
    far = jnp.where(odd, three, two)
    first = pl.plane < 2
    return wide(jnp.stack([jnp.where(first, near, far), jnp.where(first, far, near)]))


def norm_rows(stream, gain, shift):
    average = jnp.mean(stream, axis=-1, keepdims=True)
    centred = stream - average
    inverse = lax.rsqrt(jnp.mean(centred * centred, axis=-1, keepdims=True) + epsilon)
    unit = centred * inverse
    return low(unit * gain + shift), unit, inverse


def norm_back(upstream, unit, inverse, gain):
    scaled = upstream * gain
    return inverse * (
        scaled
        - jnp.mean(scaled, axis=-1, keepdims=True)
        - unit * jnp.mean(scaled * unit, axis=-1, keepdims=True)
    )


def split_heads(rows):
    return rows.reshape(rows.shape[0], rows.shape[1] // HD, HD)


def layer_forward(pl, stream, weights):
    (w_qkv, w_out), (w_in, w_down), qv_bias, in_bias, gains, shifts = weights
    normed, unit_first, inverse_first = norm_rows(stream, gains[0], shifts[0])
    queries = low(product(normed, w_qkv[0], "sd,ad->sa") + qv_bias[0])
    key_rows = low(product(normed, w_qkv[1], "sd,ad->sa"))
    value_rows = low(product(normed, w_qkv[2], "sd,ad->sa") + qv_bias[1])
    scores = product(split_heads(queries), split_heads(key_rows), "qhd,khd->hqk") * HD ** (-0.5)
    largest = jnp.max(scores, axis=-1, keepdims=True)
    logsum = largest + jnp.log(jnp.sum(jnp.exp(scores - largest), axis=-1, keepdims=True))
    soft_low = low(jnp.exp(scores - logsum))
    attended = product(soft_low, split_heads(value_rows), "hqk,khd->qhd")
    attended = low(attended.reshape(queries.shape))
    branch = sum_roles(pl, product(attended, w_out, "sa,ad->sd"))
    stream = stream + branch + shifts[2]
    normed_second, unit_second, inverse_second = norm_rows(stream, gains[1], shifts[1])
    hidden = product(normed_second, w_in, "sd,fd->sf") + in_bias
    active = low(jax.nn.gelu(hidden, approximate=False))
    branch = sum_roles(pl, product(active, w_down, "sf,fd->sd"))
    stream = stream + branch + shifts[3]
    stored = (
        unit_first, inverse_first, normed, queries, key_rows, value_rows, logsum, attended,
        unit_second, inverse_second, normed_second, hidden, active,
    )
    return stream, stored


def layer_backward(pl, upstream, weights, stored):
    (w_qkv, w_out), (w_in, w_down), qv_bias, in_bias, gains, shifts = weights
    (
        unit_first, inverse_first, normed, queries, key_rows, value_rows, logsum, attended,
        unit_second, inverse_second, normed_second, hidden, active,
    ) = stored
    shift_down = jnp.sum(upstream, axis=0)
    upstream_low = low(upstream)
    grad_down = product(active, upstream_low, "sf,sd->fd")
    grad_active = product(upstream_low, w_down, "sd,fd->sf")
    unused, gelu_back = jax.vjp(functools.partial(jax.nn.gelu, approximate=False), hidden)
    grad_hidden = low(gelu_back(grad_active)[0])
    grad_in_bias = jnp.sum(wide(grad_hidden), axis=0)
    grad_in = product(grad_hidden, normed_second, "sf,sd->fd")
    grad_normed_second = sum_roles(pl, product(grad_hidden, w_in, "sf,fd->sd"))
    gain_second = jnp.sum(grad_normed_second * unit_second, axis=0)
    shift_second = jnp.sum(grad_normed_second, axis=0)
    grad_mid = upstream + norm_back(grad_normed_second, unit_second, inverse_second, gains[1])
    shift_out = jnp.sum(grad_mid, axis=0)
    mid_low = low(grad_mid)
    grad_out = product(attended, mid_low, "sa,sd->ad")
    grad_attended = low(product(mid_low, w_out, "sd,ad->sa"))
    query_heads, key_heads, value_heads = map(split_heads, (queries, key_rows, value_rows))
    factor = HD ** (-0.5)
    soft = jnp.exp(product(query_heads, key_heads, "qhd,khd->hqk") * factor - logsum)
    attended_heads = split_heads(grad_attended)
    flat = queries.shape
    grad_values = low(product(low(soft), attended_heads, "hqk,qhd->khd").reshape(flat))
    grad_soft = product(attended_heads, value_heads, "qhd,khd->hqk")
    grad_scores = low(soft * (grad_soft - jnp.sum(grad_soft * soft, axis=-1, keepdims=True)))
    grad_queries = low((product(grad_scores, key_heads, "hqk,khd->qhd") * factor).reshape(flat))
    grad_keys = low((product(grad_scores, query_heads, "hqk,qhd->khd") * factor).reshape(flat))
    grad_qv = jnp.stack([jnp.sum(wide(grad_queries), axis=0), jnp.sum(wide(grad_values), axis=0)])
    grad_qkv = [product(g, normed, "sa,sd->ad") for g in (grad_queries, grad_keys, grad_values)]
    partial_sum = (
        product(grad_queries, w_qkv[0], "sa,ad->sd")
        + product(grad_keys, w_qkv[1], "sa,ad->sd")
        + product(grad_values, w_qkv[2], "sa,ad->sd")
    )
    grad_normed_first = sum_roles(pl, partial_sum)
    gain_first = jnp.sum(grad_normed_first * unit_first, axis=0)
    shift_first = jnp.sum(grad_normed_first, axis=0)
    upstream = grad_mid + norm_back(grad_normed_first, unit_first, inverse_first, gains[0])
    attn_grads = jnp.stack(grad_qkv + [grad_out])
    mlp_grads = jnp.stack([grad_in, grad_down])
    by_feature = jnp.stack(
        [gain_first, gain_second, shift_first, shift_second, shift_out, shift_down]
    )
    return upstream, (attn_grads, mlp_grads, grad_qv, grad_in_bias, by_feature)


def body(images, cotangent, w_qkv, w_out, w_in, w_down, qv_bias, in_bias, gains, shifts):
    fsdp, head = lax.axis_size("fsdp"), lax.axis_size("head")
    pl = Places(fsdp, head)
    cols = w_qkv.shape[2]
    width, units = w_qkv.shape[3] // TP, w_in.shape[2] // TP

    first = share_images(pl, images)
    small = jnp.concatenate(
        [qv_bias.reshape(-1), in_bias.reshape(-1), gains.reshape(-1), shifts.reshape(-1)]
    )
    small = wide(lax.all_gather(small, AXES, axis=0, tiled=False)).reshape(fsdp, head, -1)
    sizes = [qv_bias.size, in_bias.size, gains.size, shifts.size]
    marks = [0]
    for s in sizes:
        marks.append(marks[-1] + s)
    qv_all, in_all, gain_all, shift_all = [small[:, :, a:b] for a, b in zip(marks, marks[1:])]
    gain_all = gain_all[:, 0].reshape(fsdp, LAYERS, 2, cols).transpose(1, 2, 0, 3).reshape(LAYERS, 2, -1)
    shift_all = shift_all[:, 0].reshape(fsdp, LAYERS, 4, cols).transpose(1, 2, 0, 3).reshape(LAYERS, 4, -1)
    xor_planes = pl.plane ^ jnp.arange(head)
    qv_all = qv_all.reshape(fsdp, head, LAYERS, 2, -1).transpose(2, 3, 1, 4, 0).reshape(LAYERS, 2, head, TP, width)
    qv_mine = lax.dynamic_index_in_dim(qv_all, pl.role, 3, False)[:, :, xor_planes].reshape(LAYERS, 2, -1)
    in_all = in_all.reshape(fsdp, head, LAYERS, -1).transpose(2, 1, 3, 0).reshape(LAYERS, head, TP, units)
    in_mine = lax.dynamic_index_in_dim(in_all, pl.role, 2, False)[:, xor_planes].reshape(LAYERS, -1)

    weights = []
    for l in range(LAYERS):
        attn = jnp.concatenate([w_qkv[l].transpose(0, 2, 1), w_out[l][None]]).reshape(4, TP, width, cols)
        mlp = jnp.stack([w_in[l].T, w_down[l]]).reshape(2, TP, units, cols)
        attn = gather_group(pl, attn.transpose(1, 0, 2, 3))
        mlp = gather_group(pl, mlp.transpose(1, 0, 2, 3))
        weights.append(((attn[:3], attn[3]), (mlp[0], mlp[1]), qv_mine[l], in_mine[l], gain_all[l], shift_all[l]))

    streams = [wide(first[0]), wide(first[1])]
    stored = [[], []]
    for l in range(LAYERS):
        for i in range(2):
            streams[i], kept = layer_forward(pl, streams[i], weights[l])
            stored[i].append(kept)
    block_out = return_images(pl, streams)
    second = share_images(pl, cotangent)
    upstreams = [wide(second[0]), wide(second[1])]
    parts = {}
    for l in reversed(range(LAYERS)):
        sums = None
        for i in range(2):
            upstreams[i], grads = layer_backward(pl, upstreams[i], weights[l], stored[i][l])
            sums = grads if sums is None else tuple(a + b for a, b in zip(sums, grads))
        mlp = scatter_group(pl, sums[1])
        attn = scatter_group(pl, sums[0])
        parts[l] = (attn, mlp, *sums[2:])
    input_grad = return_images(pl, upstreams)

    attn = jnp.stack([parts[l][0] for l in range(LAYERS)])
    mlp = jnp.stack([parts[l][1] for l in range(LAYERS)])
    attn = attn.transpose(0, 2, 1, 3, 4).reshape(LAYERS, 4, TP * width, cols)
    mlp = mlp.transpose(0, 2, 1, 3, 4).reshape(LAYERS, 2, TP * units, cols)
    grad_qkv = attn[:, :3].transpose(0, 1, 3, 2)
    grad_out = attn[:, 3]
    grad_in = mlp[:, 0].transpose(0, 2, 1)
    grad_down = mlp[:, 1]

    by_feature = jnp.stack([parts[l][4] for l in range(LAYERS)])
    qv = jnp.stack([parts[l][2] for l in range(LAYERS)]).reshape(LAYERS, 2, head, width)[:, :, xor_planes]
    inner = jnp.stack([parts[l][3] for l in range(LAYERS)]).reshape(LAYERS, head, units)[:, xor_planes]
    qv_full = lax.dynamic_update_index_in_dim(
        jnp.zeros((LAYERS, 2, head, TP, width), jnp.float32), qv, pl.role, 3
    )
    inner_full = lax.dynamic_update_index_in_dim(
        jnp.zeros((LAYERS, head, TP, units), jnp.float32), inner, pl.role, 2
    )
    vector = jnp.concatenate([by_feature.reshape(-1) / TP, qv_full.reshape(-1), inner_full.reshape(-1)])
    vector = lax.psum(vector, AXES)
    f, h = lax.axis_index("fsdp"), lax.axis_index("head")
    a, b = by_feature.size, by_feature.size + qv_full.size
    by_feature = vector[:a].reshape(LAYERS, 6, fsdp, cols)
    by_feature = lax.dynamic_index_in_dim(by_feature, f, 2, False)
    qv = vector[a:b].reshape(LAYERS, 2, head, -1, fsdp)
    qv = lax.dynamic_index_in_dim(lax.dynamic_index_in_dim(qv, h, 2, False), f, 3, True)
    inner = vector[b:].reshape(LAYERS, head, -1, fsdp)
    inner = lax.dynamic_index_in_dim(lax.dynamic_index_in_dim(inner, h, 1, False), f, 2, True)
    return (
        block_out, input_grad, grad_qkv, grad_out, grad_in, grad_down,
        qv, inner, by_feature[:, :2], by_feature[:, 2:],
    )


def solution(mesh):
    placed = (
        P("fsdp", None, None),
        P("fsdp", None, None),
        P(None, None, "fsdp", "head"),
        P(None, "head", "fsdp"),
        P(None, "fsdp", "head"),
        P(None, "head", "fsdp"),
        P(None, None, "head", "fsdp"),
        P(None, "head", "fsdp"),
        P(None, None, "fsdp"),
        P(None, None, "fsdp"),
    )
    return jax.shard_map(
        body, mesh=mesh, in_specs=placed, out_specs=placed, check_vma=False
    )
```

time: 2010 us -> 1470 us (0.73)
  waiting for transfers between devices: 1060 us -> 435 us
  starting transfers between devices: 1.37 us -> 186 us
  other arithmetic: 121 us -> 273 us
  blocking collectives: 198 us -> 70.1 us
  matrix products: 276 us -> 210 us
  local copies, waits for them, and re-layouts: 305 us -> 261 us
    psum x14 -> x1, waiting for transfers between devices: 631 us -> 149 us  [body(): vector = lax.psum(vector, AXES)]
    ppermute x0 -> x114, waiting for transfers between devices: none -> 286 us  [the longest x76 123 us: role_xor(): lax.ppermute(v, AXES, self.pairs(lambda b, r, p: (b, r ^ bits, p), sends))]
    all_gather x12 -> x0, waiting for transfers between devices: 232 us -> none  [the longest x4 109 us: fetch_forward(): lax.all_gather(w_in[layer_index], 'fsdp', axis=0, tiled=True)]
    ppermute x0 -> x114, starting transfers between devices: none -> 186 us  [the longest x76 106 us: role_xor(): lax.ppermute(v, AXES, self.pairs(lambda b, r, p: (b, r ^ bits, p), sends))]
    dynamic_update_slice x8 -> x2, local copies, waits for them, and re-layouts: 181 us -> 0.33 us  [the longest x1 0.27 us: body(): lax.dynamic_update_index_in_dim(jnp.zeros((LAYERS, 2, head, TP, width), j...]
    all_gather x20 -> x1, blocking collectives: 176 us -> 70.1 us  [body(): lax.all_gather(small, AXES, axis=0, tiled=False)]
    reduce_scatter x2 -> x0, waiting for transfers between devices: 99.5 us -> none  [the longest x1 51.6 us: body(): lax.psum_scatter(totals[2].astype(jnp.bfloat16), 'fsdp', scatter_dimensio...]
    unnamed x10 -> x1, waiting for transfers between devices: 95.3 us -> 0.02 us
  transfers between devices with their start and end apart: 32 -> 115, of which waited for: 29 -> 43; matrix products, arithmetic and copies ran while one was open for 13% -> 37% of each run, Pallas kernels for 0% -> 0%
where the time goes in v1:
time: 1470 us; the launch traced here: 1450 us
  waiting for transfers between devices  435 us (30%)
  other arithmetic  273 us (19%)
  local copies, waits for them, and re-layouts  261 us (18%)
  matrix products  210 us (14%)
  starting transfers between devices  186 us (13%)
  blocking collectives  70.1 us (5%)
  between operations  19.6 us (1%)
    dot_general x96, matrix products, product(): return jnp.einsum(form, left, right, preferred_element_type=jnp.float32)  210 us
    psum x1, waiting for transfers between devices, body(): vector = lax.psum(vector, AXES)  149 us
    ppermute x76, waiting for transfers between devices, role_xor(): lax.ppermute(v, AXES, self.pairs(lambda b, r, p: (b, r ^ bits, p), sends))  123 us
    ppermute x30, waiting for transfers between devices, plane_xor(): lax.ppermute(v, AXES, self.pairs(lambda b, r, p: (b, r, p ^ bits), sends))  122 us
    ppermute x76, starting transfers between devices, role_xor(): lax.ppermute(v, AXES, self.pairs(lambda b, r, p: (b, r ^ bits, p), sends))  106 us
    convert_element_type x51, other arithmetic, low(): return v.astype(jnp.bfloat16)  94.9 us
    unnamed x827, local copies, waits for them, and re-layouts  75.4 us
    ppermute x30, starting transfers between devices, plane_xor(): lax.ppermute(v, AXES, self.pairs(lambda b, r, p: (b, r, p ^ bits), sends))  72.3 us
  transfers between devices with their start and end apart: 115, of which 43 were waited for; matrix products, arithmetic and copies ran while one was open for 37% of the time, Pallas kernels for 0%

profile of v1, /device:TPU:1, one launch (start us, length us, event | category | flops | bytes accessed | tf_op | source)
XLA Modules:
  0.0 1454.4 jit_solution(3458035453624072614)
XLA Ops:
  35.2 10.2 collective-permute-start.5
  47.8 6.3 collective-permute-done.5
  57.0 6.1 collective-permute-done.7
  64.5 70.1 %all-gather.1 = bf16[32,1,1920]{2,1,0:T(2,128)(2,1)S(1)} all-gather(bf16[1,1,1920]{2,1,0:T(2,128)(2,1)S(1)} %reshape.4347), channel_id=2, replica_groups=mesh['fsdp'=8,'head'=4] {'fsdp','head'}, dimensions={0}, use_global_device_ids=true | all-gather | bytes 126720 | tf_op jit(solution)/shard_map/all_gather | solution.py:256
  171.5 5.4 collective-permute-start.9
  191.9 8.4 collective-permute-done.10
  212.5 11.4 collective-permute-done.16
  270.0 9.8 collective-permute-start.25
  292.1 7.3 fusion.74
  303.6 8.0 collective-permute-start.35
  317.8 16.8 %collective-permute-done.35 = bf16[2,256,512]{2,1,0:T(8,128)(2,1)} collective-permute-done((bf16[2,256,512]{2,1,0:T(8,128)(2,1)}, bf16[2,256,512]{2,1,0:T(8,128)(2,1)}, u32[]{:S(2)}, u32[]{:S(2)}) %collective-permute-start.35) | collective-permute-done | bytes 524320 | tf_op jit(solution)/shard_map/ppermute | solution.py:54
  335.9 12.7 collective-permute-done.37
  399.0 11.8 collective-permute-done.30
  424.7 9.1 convert_reduce_fusion.12
  438.4 14.4 collective-permute-done.60
  494.0 9.8 collective-permute-done.63
  566.0 9.1 collective-permute-done.66
  602.5 7.5 fusion.76
  618.1 11.4 collective-permute-done.46
  634.8 5.9 fusion.445
  681.2 9.6 collective-permute-done.69
  694.0 9.6 collective-permute-done.49
  736.6 7.3 convert_reduce_fusion.13
  749.8 12.3 fusion.106
  780.3 5.6 convolution_bitcast_fusion.1
  794.2 8.1 collective-permute-done.52
  804.2 11.0 collective-permute-done.72
  859.7 14.4 collective-permute-start.74
  902.4 11.4 collective-permute-done.93
  926.6 8.6 collective-permute-done.96
  936.1 6.9 collective-permute-start.97
  945.4 5.8 copy.588
  966.1 12.7 fusion.124
  982.4 6.5 fusion.126
  992.4 5.7 convolution_bitcast_fusion.5
  998.2 5.5 fusion.447
  1003.7 5.8 fusion.456
  1025.7 11.6 collective-permute-done.108
  1037.3 13.5 collective-permute-done.110
  1144.1 12.3 collective-permute-done.86
  1159.1 10.8 collective-permute-start.87
  1180.4 8.0 collective-permute-done.89
  1205.5 17.7 %collective-permute-done.100 = bf16[2,4,256,512]{3,2,1,0:T(8,128)(2,1)} collective-permute-done((bf16[2,4,256,512]{3,2,1,0:T(8,128)(2,1)}, bf16[2,4,256,512]{3,2,1,0:T(8,128)(2,1)}, u32[]{:S(2)}, u32[]{:S(2)}) %collective-permute-start.100) | collective-permute-done | bytes 2097184 | tf_op jit(solution)/shard_map/ppermute | solution.py:57
  1239.7 11.3 collective-permute-done.101
  1253.0 10.0 collective-permute-done.103
  1266.2 8.8 collective-permute-start.104
  1281.9 148.9 %all-reduce.2.cloned.1.call-done = f32[24576]{0:T(1024)} async-done(((f32[24576]{0:T(1024)}), f32[24576]{0:T(1024)}) %all-reduce.2.cloned.1.call-update) | async-done | bytes 98320 | tf_op jit(solution)/shard_map/psum | solution.py:317
  1441.5 5.8 copy.589
  (1458 shorter events, 777.8 us)
Async XLA Ops:
  7.2 1423.7 %all-reduce.2.cloned.1.call-start = ((), (), s32[]{:S(2)}) async-start(), calls=%async_computation | async-start | bytes 196608 | tf_op jit(solution)/shard_map/psum | solution.py:317
  29.9 113.1 %collective-permute-start.1 = (bf16[2,577,1024]{2,0,1:T(2,128)(2,1)}, bf16[2,577,1024]{2,0,1:T(2,128)(2,1)}, u32[]{:S(2)}, u32[]{:S(2)}) collective-permute-start(bf16[2,577,1024]{2,0,1:T(2,128)(2,1)} %copy.475), channel_id=1, source_target_pairs={{0,4},{2,6},{5,1},{7,3},{8,12},{10,14},{13,9},{15,11},{16,20},{18,... | collective-permute-start | bytes 7090184 | tf_op jit(solution)/shard_map/ppermute | solution.py:51
  63.2 77.5 %collective-permute-start.8 = (bf16[4,4,64,512]{3,2,0,1:T(8,128)(2,1)S(1)}, bf16[4,4,64,512]{3,2,0,1:T(8,128)(2,1)S(1)}, u32[]{:S(2)}, u32[]{:S(2)}) collective-permute-start(bf16[4,4,64,512]{3,2,0,1:T(8,128)(2,1)S(1)} %pad_maximum_fusion.18), channel_id=1, source_target_pairs={{0,16},{1,17},{2,18},{3,19},{4,20},{5,21},{6,22},{7,23},{8,24},{9,... | collective-permute-start | bytes 3145736 | tf_op jit(solution)/shard_map/ppermute | solution.py:57
  188.4 35.5 %collective-permute-start.16 = (bf16[2,256,512]{2,1,0:T(8,128)(2,1)}, bf16[2,256,512]{2,1,0:T(8,128)(2,1)}, u32[]{:S(2)}, u32[]{:S(2)}) collective-permute-start(bf16[2,256,512]{2,1,0:T(8,128)(2,1)} %get-tuple-element.292), channel_id=1, source_target_pairs={{0,2},{1,3},{2,0},{3,1},{4,6},{5,7},{6,4},{7,5},{8,10},{9,11},{10,... | collective-permute-start | bytes 1572872 | tf_op jit(solution)/shard_map/ppermute | solution.py:54
  188.4 37.1 %collective-permute-start.17 = (bf16[2,256,512]{2,1,0:T(8,128)(2,1)}, bf16[2,256,512]{2,1,0:T(8,128)(2,1)}, u32[]{:S(2)}, u32[]{:S(2)}) collective-permute-start(bf16[2,256,512]{2,1,0:T(8,128)(2,1)} %get-tuple-element.292), channel_id=1, source_target_pairs={{0,3},{1,2},{2,1},{3,0},{4,7},{5,6},{6,5},{7,4},{8,11},{9,10},{10,... | collective-permute-start | bytes 1572872 | tf_op jit(solution)/shard_map/ppermute | solution.py:54
  201.3 27.3 %collective-permute-start.11 = (bf16[577,512]{1,0:T(8,128)(2,1)}, bf16[577,512]{1,0:T(8,128)(2,1)}, u32[]{:S(2)}, u32[]{:S(2)}) collective-permute-start(bf16[577,512]{1,0:T(8,128)(2,1)} %add_convert_fusion.50), channel_id=1, source_target_pairs={{0,4},{1,5},{2,6},{3,7},{4,0},{5,1},{6,2},{7,3},{8,12},{9,13},{10,... | collective-permute-start | bytes 1772552 | tf_op jit(solution)/shard_map/ppermute | solution.py:51
  205.8 62.4 %collective-permute-start.32 = (bf16[2,256,128]{2,1,0:T(8,128)(2,1)}, bf16[2,256,128]{2,1,0:T(8,128)(2,1)}, u32[]{:S(2)}, u32[]{:S(2)}) collective-permute-start(bf16[2,256,128]{2,1,0:T(8,128)(2,1)} %get-tuple-element.285), channel_id=1, source_target_pairs={{0,12},{1,13},{2,14},{3,15},{4,8},{5,9},{6,10},{7,11},{8,4},{9,5},... | collective-permute-start | bytes 393224 | tf_op jit(solution)/shard_map/ppermute | solution.py:51
  210.8 53.9 %collective-permute-start.22 = (bf16[4,64,128]{2,1,0:T(8,128)(2,1)}, bf16[4,64,128]{2,1,0:T(8,128)(2,1)}, u32[]{:S(2)}, u32[]{:S(2)}) collective-permute-start(bf16[4,64,128]{2,1,0:T(8,128)(2,1)} %get-tuple-element.329), channel_id=1, source_target_pairs={{0,12},{1,13},{2,14},{3,15},{4,8},{5,9},{6,10},{7,11},{8,4},{9,5},... | collective-permute-start | bytes 196616 | tf_op jit(solution)/shard_map/ppermute | solution.py:51
  223.8 42.6 %collective-permute-start.23 = (bf16[4,64,128]{2,1,0:T(8,128)(2,1)}, bf16[4,64,128]{2,1,0:T(8,128)(2,1)}, u32[]{:S(2)}, u32[]{:S(2)}) collective-permute-start(bf16[4,64,128]{2,1,0:T(8,128)(2,1)} %get-tuple-element.328), channel_id=1, source_target_pairs={{0,8},{1,9},{2,10},{3,11},{4,12},{5,13},{6,14},{7,15},{8,0},{9,1},... | collective-permute-start | bytes 196616 | tf_op jit(solution)/shard_map/ppermute | solution.py:51
  228.4 55.8 %collective-permute-start.18 = (bf16[2,4,256,512]{3,2,0,1:T(8,128)(2,1)}, bf16[2,4,256,512]{3,2,0,1:T(8,128)(2,1)}, u32[]{:S(2)}, u32[]{:S(2)}) collective-permute-start(bf16[2,4,256,512]{3,2,0,1:T(8,128)(2,1)} %pad_maximum_fusion.4), channel_id=1, source_target_pairs={{0,16},{1,17},{2,18},{3,19},{4,20},{5,21},{6,22},{7,23},{8,24},{9,... | collective-permute-start | bytes 6291464 | tf_op jit(solution)/shard_map/ppermute | solution.py:57
  268.2 84.6 %collective-permute-start.57 = (bf16[577,1024]{1,0:T(8,128)(2,1)}, bf16[577,1024]{1,0:T(8,128)(2,1)}, u32[]{:S(2)}, u32[]{:S(2)}) collective-permute-start(bf16[577,1024]{1,0:T(8,128)(2,1)} %bitcast.1499), channel_id=1, source_target_pairs={{0,8},{2,10},{5,13},{7,15},{8,0},{10,2},{13,5},{15,7},{16,24},{18,... | collective-permute-start | bytes 3545096 | tf_op jit(solution)/shard_map/ppermute | solution.py:51
  270.0 33.6 %collective-permute-start.25 = (bf16[4,64,512]{2,1,0:T(8,128)(2,1)S(1)}, bf16[4,64,512]{2,1,0:T(8,128)(2,1)S(1)}, u32[]{:S(2)}, u32[]{:S(2)}) collective-permute-start(bf16[4,64,512]{2,1,0:T(8,128)(2,1)S(1)} %get-tuple-element.326), channel_id=1, source_target_pairs={{0,1},{1,0},{2,3},{3,2},{4,5},{5,4},{6,7},{7,6},{8,9},{9,8},{10,11... | collective-permute-start | bytes 786440 | tf_op jit(solution)/shard_map/ppermute | solution.py:54
  279.9 31.8 %collective-permute-start.26 = (bf16[4,64,512]{2,1,0:T(8,128)(2,1)S(1)}, bf16[4,64,512]{2,1,0:T(8,128)(2,1)S(1)}, u32[]{:S(2)}, u32[]{:S(2)}) collective-permute-start(bf16[4,64,512]{2,1,0:T(8,128)(2,1)S(1)} %get-tuple-element.326), channel_id=1, source_target_pairs={{0,2},{1,3},{2,0},{3,1},{4,6},{5,7},{6,4},{7,5},{8,10},{9,11},{10,... | collective-permute-start | bytes 786440 | tf_op jit(solution)/shard_map/ppermute | solution.py:54
  282.8 30.4 %collective-permute-start.27 = (bf16[4,64,512]{2,1,0:T(8,128)(2,1)S(1)}, bf16[4,64,512]{2,1,0:T(8,128)(2,1)S(1)}, u32[]{:S(2)}, u32[]{:S(2)}) collective-permute-start(bf16[4,64,512]{2,1,0:T(8,128)(2,1)S(1)} %get-tuple-element.326), channel_id=1, source_target_pairs={{0,3},{1,2},{2,1},{3,0},{4,7},{5,6},{6,5},{7,4},{8,11},{9,10},{10,... | collective-permute-start | bytes 786440 | tf_op jit(solution)/shard_map/ppermute | solution.py:54
  303.6 31.0 %collective-permute-start.35 = (bf16[2,256,512]{2,1,0:T(8,128)(2,1)}, bf16[2,256,512]{2,1,0:T(8,128)(2,1)}, u32[]{:S(2)}, u32[]{:S(2)}) collective-permute-start(bf16[2,256,512]{2,1,0:T(8,128)(2,1)} %get-tuple-element.280), channel_id=1, source_target_pairs={{0,1},{1,0},{2,3},{3,2},{4,5},{5,4},{6,7},{7,6},{8,9},{9,8},{10,11... | collective-permute-start | bytes 1572872 | tf_op jit(solution)/shard_map/ppermute | solution.py:54
  313.2 35.5 %collective-permute-start.37 = (bf16[2,256,512]{2,1,0:T(8,128)(2,1)}, bf16[2,256,512]{2,1,0:T(8,128)(2,1)}, u32[]{:S(2)}, u32[]{:S(2)}) collective-permute-start(bf16[2,256,512]{2,1,0:T(8,128)(2,1)} %get-tuple-element.280), channel_id=1, source_target_pairs={{0,3},{1,2},{2,1},{3,0},{4,7},{5,6},{6,5},{7,4},{8,11},{9,10},{10,... | collective-permute-start | bytes 1572872 | tf_op jit(solution)/shard_map/ppermute | solution.py:54
  315.5 49.7 %collective-permute-start.28 = (bf16[4,4,64,512]{3,2,0,1:T(8,128)(2,1)}, bf16[4,4,64,512]{3,2,0,1:T(8,128)(2,1)}, u32[]{:S(2)}, u32[]{:S(2)}) collective-permute-start(bf16[4,4,64,512]{3,2,0,1:T(8,128)(2,1)} %pad_maximum_fusion.19), channel_id=1, source_target_pairs={{0,16},{1,17},{2,18},{3,19},{4,20},{5,21},{6,22},{7,23},{8,24},{9,... | collective-permute-start | bytes 3145736 | tf_op jit(solution)/shard_map/ppermute | solution.py:57
  351.6 45.2 %collective-permute-start.38 = (bf16[2,4,256,512]{3,2,0,1:T(8,128)(2,1)}, bf16[2,4,256,512]{3,2,0,1:T(8,128)(2,1)}, u32[]{:S(2)}, u32[]{:S(2)}) collective-permute-start(bf16[2,4,256,512]{3,2,0,1:T(8,128)(2,1)} %pad_maximum_fusion.5), channel_id=1, source_target_pairs={{0,16},{1,17},{2,18},{3,19},{4,20},{5,21},{6,22},{7,23},{8,24},{9,... | collective-permute-start | bytes 6291464 | tf_op jit(solution)/shard_map/ppermute | solution.py:57
  363.9 48.8 %collective-permute-start.58 = (bf16[2,577,1024]{2,0,1:T(2,128)(2,1)}, bf16[2,577,1024]{2,0,1:T(2,128)(2,1)}, u32[]{:S(2)}, u32[]{:S(2)}) collective-permute-start(bf16[2,577,1024]{2,0,1:T(2,128)(2,1)} %copy.506), channel_id=1, source_target_pairs={{0,4},{2,6},{5,1},{7,3},{8,12},{10,14},{13,9},{15,11},{16,20},{18,... | collective-permute-start | bytes 7090184 | tf_op jit(solution)/shard_map/ppermute | solution.py:51
  493.5 29.5 %collective-permute-start.39 = (bf16[577,512]{1,0:T(8,128)(2,1)}, bf16[577,512]{1,0:T(8,128)(2,1)}, u32[]{:S(2)}, u32[]{:S(2)}) collective-permute-start(bf16[577,512]{1,0:T(8,128)(2,1)} %broadcast_select_fusion.50), channel_id=1, source_target_pairs={{0,4},{1,5},{2,6},{3,7},{4,0},{5,1},{6,2},{7,3},{8,12},{9,13},{10,... | collective-permute-start | bytes 1772552 | tf_op jit(solution)/shard_map/ppermute | solution.py:51
  525.4 26.4 %collective-permute-start.40 = (bf16[577,512]{1,0:T(8,128)(2,1)}, bf16[577,512]{1,0:T(8,128)(2,1)}, u32[]{:S(2)}, u32[]{:S(2)}) collective-permute-start(bf16[577,512]{1,0:T(8,128)(2,1)} %add_convert_fusion.45), channel_id=1, source_target_pairs={{0,8},{1,9},{2,10},{3,11},{4,12},{5,13},{6,14},{7,15},{8,0},{9,1},... | collective-permute-start | bytes 1772552 | tf_op jit(solution)/shard_map/ppermute | solution.py:51
  554.1 114.0 %collective-permute-start.41 = (bf16[577,512]{1,0:T(8,128)(2,1)}, bf16[577,512]{1,0:T(8,128)(2,1)}, u32[]{:S(2)}, u32[]{:S(2)}) collective-permute-start(bf16[577,512]{1,0:T(8,128)(2,1)} %add_convert_fusion.44), channel_id=1, source_target_pairs={{0,4},{1,5},{2,6},{3,7},{4,0},{5,1},{6,2},{7,3},{8,12},{9,13},{10,... | collective-permute-start | bytes 1772552 | tf_op jit(solution)/shard_map/ppermute | solution.py:51
  632.5 41.8 %collective-permute-start.68 = (bf16[577,512]{1,0:T(8,128)(2,1)}, bf16[577,512]{1,0:T(8,128)(2,1)}, u32[]{:S(2)}, u32[]{:S(2)}) collective-permute-start(bf16[577,512]{1,0:T(8,128)(2,1)} %broadcast_select_fusion.26), channel_id=1, source_target_pairs={{0,4},{1,5},{2,6},{3,7},{4,0},{5,1},{6,2},{7,3},{8,12},{9,13},{10,... | collective-permute-start | bytes 1772552 | tf_op jit(solution)/shard_map/ppermute | solution.py:51
  677.3 26.3 %collective-permute-start.49 = (bf16[577,512]{1,0:T(8,128)(2,1)S(1)}, bf16[577,512]{1,0:T(8,128)(2,1)S(1)}, u32[]{:S(2)}, u32[]{:S(2)}) collective-permute-start(bf16[577,512]{1,0:T(8,128)(2,1)S(1)} %add_convert_fusion.39), channel_id=1, source_target_pairs={{0,8},{1,9},{2,10},{3,11},{4,12},{5,13},{6,14},{7,15},{8,0},{9,1},... | collective-permute-start | bytes 1772552 | tf_op jit(solution)/shard_map/ppermute | solution.py:51
  691.8 34.9 %collective-permute-start.70 = (bf16[577,512]{1,0:T(8,128)(2,1)}, bf16[577,512]{1,0:T(8,128)(2,1)}, u32[]{:S(2)}, u32[]{:S(2)}) collective-permute-start(bf16[577,512]{1,0:T(8,128)(2,1)} %add_convert_fusion.28), channel_id=1, source_target_pairs={{0,4},{1,5},{2,6},{3,7},{4,0},{5,1},{6,2},{7,3},{8,12},{9,13},{10,... | collective-permute-start | bytes 1772552 | tf_op jit(solution)/shard_map/ppermute | solution.py:51
  746.4 39.5 %collective-permute-start.51 = (bf16[577,512]{1,0:T(8,128)(2,1)}, bf16[577,512]{1,0:T(8,128)(2,1)}, u32[]{:S(2)}, u32[]{:S(2)}) collective-permute-start(bf16[577,512]{1,0:T(8,128)(2,1)} %broadcast_select_fusion.38), channel_id=1, source_target_pairs={{0,4},{1,5},{2,6},{3,7},{4,0},{5,1},{6,2},{7,3},{8,12},{9,13},{10,... | collective-permute-start | bytes 1772552 | tf_op jit(solution)/shard_map/ppermute | solution.py:51
  749.3 39.1 %collective-permute-start.71 = (bf16[577,512]{1,0:T(8,128)(2,1)}, bf16[577,512]{1,0:T(8,128)(2,1)}, u32[]{:S(2)}, u32[]{:S(2)}) collective-permute-start(bf16[577,512]{1,0:T(8,128)(2,1)} %broadcast_select_fusion.23), channel_id=1, source_target_pairs={{0,4},{1,5},{2,6},{3,7},{4,0},{5,1},{6,2},{7,3},{8,12},{9,13},{10,... | collective-permute-start | bytes 1772552 | tf_op jit(solution)/shard_map/ppermute | solution.py:51
  789.7 25.5 %collective-permute-start.72 = (bf16[577,512]{1,0:T(8,128)(2,1)S(1)}, bf16[577,512]{1,0:T(8,128)(2,1)S(1)}, u32[]{:S(2)}, u32[]{:S(2)}) collective-permute-start(bf16[577,512]{1,0:T(8,128)(2,1)S(1)} %add_convert_fusion.27), channel_id=1, source_target_pairs={{0,8},{1,9},{2,10},{3,11},{4,12},{5,13},{6,14},{7,15},{8,0},{9,1},... | collective-permute-start | bytes 1772552 | tf_op jit(solution)/shard_map/ppermute | solution.py:51
  847.1 70.9 %collective-permute-start.54 = (bf16[577,1024]{1,0:T(8,128)(2,1)}, bf16[577,1024]{1,0:T(8,128)(2,1)}, u32[]{:S(2)}, u32[]{:S(2)}) collective-permute-start(bf16[577,1024]{1,0:T(8,128)(2,1)} %get-tuple-element.196), channel_id=1, source_target_pairs={{0,1},{2,3},{5,4},{7,6},{8,9},{10,11},{13,12},{15,14},{16,17},{18,... | collective-permute-start | bytes 3545096 | tf_op jit(solution)/shard_map/ppermute | solution.py:54
  848.5 70.0 %collective-permute-start.55 = (bf16[577,1024]{1,0:T(8,128)(2,1)}, bf16[577,1024]{1,0:T(8,128)(2,1)}, u32[]{:S(2)}, u32[]{:S(2)}) collective-permute-start(bf16[577,1024]{1,0:T(8,128)(2,1)} %get-tuple-element.196), channel_id=1, source_target_pairs={{0,3},{2,1},{5,6},{7,4},{8,11},{10,9},{13,14},{15,12},{16,19},{18,... | collective-permute-start | bytes 3545096 | tf_op jit(solution)/shard_map/ppermute | solution.py:54
  849.8 70.5 %collective-permute-start.56 = (bf16[577,1024]{1,0:T(8,128)(2,1)}, bf16[577,1024]{1,0:T(8,128)(2,1)}, u32[]{:S(2)}, u32[]{:S(2)}) collective-permute-start(bf16[577,1024]{1,0:T(8,128)(2,1)} %get-tuple-element.196), channel_id=1, source_target_pairs={{0,2},{2,0},{5,7},{7,5},{8,10},{10,8},{13,15},{15,13},{16,18},{18,... | collective-permute-start | bytes 3545096 | tf_op jit(solution)/shard_map/ppermute | solution.py:54
  859.7 39.0 %collective-permute-start.74 = (bf16[577,512]{1,0:T(8,128)(2,1)}, bf16[577,512]{1,0:T(8,128)(2,1)}, u32[]{:S(2)}, u32[]{:S(2)}) collective-permute-start(bf16[577,512]{1,0:T(8,128)(2,1)} %broadcast_select_fusion.20), channel_id=1, source_target_pairs={{0,4},{1,5},{2,6},{3,7},{4,0},{5,1},{6,2},{7,3},{8,12},{9,13},{10,... | collective-permute-start | bytes 1772552 | tf_op jit(solution)/shard_map/ppermute | solution.py:51
  888.7 25.1 %collective-permute-start.93 = (bf16[4,4,64,512]{3,2,1,0:T(8,128)(2,1)}, bf16[4,4,64,512]{3,2,1,0:T(8,128)(2,1)}, u32[]{:S(2)}, u32[]{:S(2)}) collective-permute-start(bf16[4,4,64,512]{3,2,1,0:T(8,128)(2,1)} %fusion.339), channel_id=1, source_target_pairs={{0,16},{1,17},{2,18},{3,19},{4,20},{5,21},{6,22},{7,23},{8,24},{9,... | collective-permute-start | bytes 3145736 | tf_op jit(solution)/shard_map/ppermute | solution.py:57
  913.8 89.9 %collective-permute-start.107 = (bf16[2,4,256,512]{3,2,1,0:T(8,128)(2,1)}, bf16[2,4,256,512]{3,2,1,0:T(8,128)(2,1)}, u32[]{:S(2)}, u32[]{:S(2)}) collective-permute-start(bf16[2,4,256,512]{3,2,1,0:T(8,128)(2,1)} %fusion.205), channel_id=1, source_target_pairs={{0,16},{1,17},{2,18},{3,19},{4,20},{5,21},{6,22},{7,23},{8,24},{9,... | collective-permute-start | bytes 6291464 | tf_op jit(solution)/shard_map/ppermute | solution.py:57
  920.4 32.2 %collective-permute-start.76 = (bf16[577,512]{1,0:T(8,128)(2,1)}, bf16[577,512]{1,0:T(8,128)(2,1)}, u32[]{:S(2)}, u32[]{:S(2)}) collective-permute-start(bf16[577,512]{1,0:T(8,128)(2,1)} %add_convert_fusion.24), channel_id=1, source_target_pairs={{0,4},{1,5},{2,6},{3,7},{4,0},{5,1},{6,2},{7,3},{8,12},{9,13},{10,... | collective-permute-start | bytes 1772552 | tf_op jit(solution)/shard_map/ppermute | solution.py:51
  965.6 50.6 %collective-permute-start.77 = (bf16[577,512]{1,0:T(8,128)(2,1)}, bf16[577,512]{1,0:T(8,128)(2,1)}, u32[]{:S(2)}, u32[]{:S(2)}) collective-permute-start(bf16[577,512]{1,0:T(8,128)(2,1)} %broadcast_select_fusion.17), channel_id=1, source_target_pairs={{0,4},{1,5},{2,6},{3,7},{4,0},{5,1},{6,2},{7,3},{8,12},{9,13},{10,... | collective-permute-start | bytes 1772552 | tf_op jit(solution)/shard_map/ppermute | solution.py:51
  1010.6 26.6 %collective-permute-start.108 = (bf16[2,256,512]{2,1,0:T(8,128)(2,1)}, bf16[2,256,512]{2,1,0:T(8,128)(2,1)S(1)}, u32[]{:S(2)}, u32[]{:S(2)}) collective-permute-start(bf16[2,256,512]{2,1,0:T(8,128)(2,1)} %get-tuple-element.206), channel_id=1, source_target_pairs={{0,1},{1,0},{2,3},{3,2},{4,5},{5,4},{6,7},{7,6},{8,9},{9,8},{10,11... | collective-permute-start | bytes 1572872 | tf_op jit(solution)/shard_map/ppermute | solution.py:54
  1014.6 36.1 %collective-permute-start.110 = (bf16[2,256,512]{2,1,0:T(8,128)(2,1)}, bf16[2,256,512]{2,1,0:T(8,128)(2,1)}, u32[]{:S(2)}, u32[]{:S(2)}) collective-permute-start(bf16[2,256,512]{2,1,0:T(8,128)(2,1)} %get-tuple-element.207), channel_id=1, source_target_pairs={{0,3},{1,2},{2,1},{3,0},{4,7},{5,6},{6,5},{7,4},{8,11},{9,10},{10,... | collective-permute-start | bytes 1572872 | tf_op jit(solution)/shard_map/ppermute | solution.py:54
  1018.3 43.5 %collective-permute-start.78 = (bf16[577,512]{1,0:T(8,128)(2,1)}, bf16[577,512]{1,0:T(8,128)(2,1)}, u32[]{:S(2)}, u32[]{:S(2)}) collective-permute-start(bf16[577,512]{1,0:T(8,128)(2,1)} %add_convert_fusion.23), channel_id=1, source_target_pairs={{0,8},{1,9},{2,10},{3,11},{4,12},{5,13},{6,14},{7,15},{8,0},{9,1},... | collective-permute-start | bytes 1772552 | tf_op jit(solution)/shard_map/ppermute | solution.py:51
  1109.5 32.3 %collective-permute-start.80 = (bf16[577,512]{1,0:T(8,128)(2,1)}, bf16[577,512]{1,0:T(8,128)(2,1)}, u32[]{:S(2)}, u32[]{:S(2)}) collective-permute-start(bf16[577,512]{1,0:T(8,128)(2,1)} %broadcast_select_fusion.14), channel_id=1, source_target_pairs={{0,4},{1,5},{2,6},{3,7},{4,0},{5,1},{6,2},{7,3},{8,12},{9,13},{10,... | collective-permute-start | bytes 1772552 | tf_op jit(solution)/shard_map/ppermute | solution.py:51
  1143.2 53.3 %collective-permute-start.81 = (bf16[577,512]{1,0:T(8,128)(2,1)S(1)}, bf16[577,512]{1,0:T(8,128)(2,1)}, u32[]{:S(2)}, u32[]{:S(2)}) collective-permute-start(bf16[577,512]{1,0:T(8,128)(2,1)S(1)} %add_convert_fusion.21), channel_id=1, source_target_pairs={{0,8},{1,9},{2,10},{3,11},{4,12},{5,13},{6,14},{7,15},{8,0},{9,1},... | collective-permute-start | bytes 1772552 | tf_op jit(solution)/shard_map/ppermute | solution.py:51
  1177.4 45.8 %collective-permute-start.100 = (bf16[2,4,256,512]{3,2,1,0:T(8,128)(2,1)}, bf16[2,4,256,512]{3,2,1,0:T(8,128)(2,1)}, u32[]{:S(2)}, u32[]{:S(2)}) collective-permute-start(bf16[2,4,256,512]{3,2,1,0:T(8,128)(2,1)} %fusion.204), channel_id=1, source_target_pairs={{0,16},{1,17},{2,18},{3,19},{4,20},{5,21},{6,22},{7,23},{8,24},{9,... | collective-permute-start | bytes 6291464 | tf_op jit(solution)/shard_map/ppermute | solution.py:57
  1231.0 32.0 %collective-permute-start.103 = (bf16[2,256,512]{2,1,0:T(8,128)(2,1)}, bf16[2,256,512]{2,1,0:T(8,128)(2,1)}, u32[]{:S(2)}, u32[]{:S(2)}) collective-permute-start(bf16[2,256,512]{2,1,0:T(8,128)(2,1)} %get-tuple-element.204), channel_id=1, source_target_pairs={{0,3},{1,2},{2,1},{3,0},{4,7},{5,6},{6,5},{7,4},{8,11},{9,10},{10,... | collective-permute-start | bytes 1572872 | tf_op jit(solution)/shard_map/ppermute | solution.py:54
  1236.8 202.4 %collective-permute-start.83 = (bf16[577,1024]{1,0:T(8,128)(2,1)}, bf16[577,1024]{1,0:T(8,128)(2,1)}, u32[]{:S(2)}, u32[]{:S(2)}) collective-permute-start(bf16[577,1024]{1,0:T(8,128)(2,1)} %fusion.42), channel_id=1, source_target_pairs={{0,1},{2,3},{5,4},{7,6},{8,9},{10,11},{13,12},{15,14},{16,17},{18,... | collective-permute-start | bytes 3545096 | tf_op jit(solution)/shard_map/ppermute | solution.py:54
  1238.1 201.1 %collective-permute-start.84 = (bf16[577,1024]{1,0:T(8,128)(2,1)}, bf16[577,1024]{1,0:T(8,128)(2,1)}, u32[]{:S(2)}, u32[]{:S(2)}) collective-permute-start(bf16[577,1024]{1,0:T(8,128)(2,1)} %fusion.42), channel_id=1, source_target_pairs={{0,3},{2,1},{5,6},{7,4},{8,11},{10,9},{13,14},{15,12},{16,19},{18,... | collective-permute-start | bytes 3545096 | tf_op jit(solution)/shard_map/ppermute | solution.py:54
  1251.0 188.2 %collective-permute-start.85 = (bf16[577,1024]{1,0:T(8,128)(2,1)}, bf16[577,1024]{1,0:T(8,128)(2,1)}, u32[]{:S(2)}, u32[]{:S(2)}) collective-permute-start(bf16[577,1024]{1,0:T(8,128)(2,1)} %fusion.42), channel_id=1, source_target_pairs={{0,2},{2,0},{5,7},{7,5},{8,10},{10,8},{13,15},{15,13},{16,18},{18,... | collective-permute-start | bytes 3545096 | tf_op jit(solution)/shard_map/ppermute | solution.py:54
  1276.4 159.9 %collective-permute-start.105 = (bf16[2,256,128]{2,1,0:T(8,128)(2,1)}, bf16[2,256,128]{2,1,0:T(8,128)(2,1)S(1)}, u32[]{:S(2)}, u32[]{:S(2)}) collective-permute-start(bf16[2,256,128]{2,1,0:T(8,128)(2,1)} %bitcast.1505), channel_id=1, source_target_pairs={{0,8},{1,9},{2,10},{3,11},{4,12},{5,13},{6,14},{7,15},{8,0},{9,1},... | collective-permute-start | bytes 393224 | tf_op jit(solution)/shard_map/ppermute | solution.py:51
  1279.1 157.2 %collective-permute-start.106 = (bf16[2,256,128]{2,1,0:T(8,128)(2,1)S(1)}, bf16[2,256,128]{2,1,0:T(8,128)(2,1)S(1)}, u32[]{:S(2)}, u32[]{:S(2)}) collective-permute-start(bf16[2,256,128]{2,1,0:T(8,128)(2,1)S(1)} %bitcast.1769), channel_id=1, source_target_pairs={{0,4},{1,5},{2,6},{3,7},{4,0},{5,1},{6,2},{7,3},{8,12},{9,13},{10,... | collective-permute-start | bytes 393224 | tf_op jit(solution)/shard_map/ppermute | solution.py:51
  (470 other events, 4340.3 us)
Sparse Core Ops, SparseCore 0:
  1275.8 154.9 all-reduce.1

commit v2 on v1

--- a/solution.py
+++ b/solution.py
@@ -1,15 +1,645 @@
 import functools
+import math
 
 import jax
 import jax.numpy as jnp
 from jax import lax
+from jax.experimental import pallas as pl
+from jax.experimental.pallas import tpu as pltpu
 from jax.sharding import PartitionSpec as P
 
+D = 1024
 HD = 64
 LAYERS = 2
 TP = 4
+HALF = D // 2
 AXES = ("fsdp", "head")
+MESH = pl.DeviceIdType.MESH
 epsilon = 1e-06
+f32, bf16 = jnp.float32, jnp.bfloat16
+
+
+def dot(left, right, left_dim, right_dim):
+    return lax.dot_general(
+        left, right, (((left_dim,), (right_dim,)), ((), ())), preferred_element_type=f32
+    )
+
+
+def flip1(n):
+    return n + 1 - 2 * (n % 2)
+
+
+def flip2(n):
+    return n + 2 - 4 * ((n // 2) % 2)
+
+
+def flip(n, bits):
+    if bits & 1:
+        n = flip1(n)
+    if bits & 2:
+        n = flip2(n)
+    return n
+
+
+class Spot:
+    def __init__(self, fsdp, head):
+        self.blocks = fsdp // TP
+        self.planes = head
+        index = lax.axis_index("fsdp")
+        self.index = index
+        self.block, self.role, self.plane = index // TP, index % TP, lax.axis_index("head")
+        self.core, self.side = self.role % 2, self.role // 2
+
+    def at(self, block=None, role=None, plane=None):
+        block = self.block if block is None else block
+        role = self.role if role is None else role
+        plane = self.plane if plane is None else plane
+        return (block * TP + role, plane)
+
+    def partners(self):
+        found = [self.at(role=flip(self.role, o)) for o in (1, 2, 3)]
+        found += [self.at(plane=flip(self.plane, o)) for o in (1, 2, 3)]
+        found += [self.at(block=(self.block + s) % self.blocks) for s in range(1, self.blocks)]
+        return found
+
+
+def greet(partners):
+    barrier = pltpu.get_barrier_semaphore()
+    for partner in partners:
+        pl.semaphore_signal(barrier, inc=1, device_id=partner, device_id_type=MESH)
+    pl.semaphore_wait(barrier, len(partners))
+
+
+def send(source, target, sems, where, device):
+    return pltpu.make_async_remote_copy(
+        src_ref=source,
+        dst_ref=target,
+        send_sem=sems[0].at[where],
+        recv_sem=sems[1].at[where],
+        device_id=device,
+        device_id_type=MESH,
+    )
+
+
+def lanes(start, size):
+    return pl.ds(pl.multiple_of(start, 128), size)
+
+
+class Gather:
+    def __init__(self, spot, packed, whole, role_sems, plane_sems, block_sems, base, local_sem, direct):
+        self.spot, self.packed, self.whole, self.direct = spot, packed, whole, direct
+        self.role_sems, self.plane_sems, self.block_sems = role_sems, plane_sems, block_sems
+        self.base, self.local_sem = base, local_sem
+        self.cols = D // spot.blocks // TP
+        self.span = D // spot.blocks
+
+    def piece(self, g, plane, block):
+        return self.whole.at[g, plane, :, lanes(block * self.span, self.span)]
+
+    def own(self, g):
+        spot = self.spot
+        if self.direct:
+            return pltpu.make_async_copy(
+                self.packed.at[g, spot.role],
+                self.whole.at[g, spot.plane, :, lanes(spot.index * self.cols, self.cols)],
+                self.local_sem.at[self.base + g],
+            )
+        return pltpu.make_async_copy(
+            self.packed.at[g], self.piece(g, spot.plane, spot.block), self.local_sem.at[self.base + g]
+        )
+
+    def to_role(self, g, o):
+        spot = self.spot
+        other = flip(spot.role, o)
+        return send(
+            self.packed.at[g, other],
+            self.whole.at[g, spot.plane, :, lanes(spot.index * self.cols, self.cols)],
+            self.role_sems,
+            (self.base + g, o),
+            spot.at(role=other),
+        )
+
+    def from_role(self, g, o):
+        spot = self.spot
+        other = flip(spot.role, o)
+        place = self.whole.at[
+            g, spot.plane, :, lanes((spot.block * TP + other) * self.cols, self.cols)
+        ]
+        return send(place, place, self.role_sems, (self.base + g, o), spot.at(role=other))
+
+    def to_plane(self, g, o):
+        spot = self.spot
+        place = self.piece(g, spot.plane, spot.block)
+        return send(
+            place, place, self.plane_sems, (self.base + g, o), spot.at(plane=flip(spot.plane, o))
+        )
+
+    def from_plane(self, g, o):
+        spot = self.spot
+        other = flip(spot.plane, o)
+        place = self.piece(g, other, spot.block)
+        return send(place, place, self.plane_sems, (self.base + g, o), spot.at(plane=other))
+
+    def to_block(self, g, s, o):
+        spot = self.spot
+        place = self.piece(g, flip(spot.plane, o), spot.block)
+        block = (spot.block + s) % spot.blocks
+        return send(
+            place, place, self.block_sems, (self.base + g, s, o), spot.at(block=block)
+        )
+
+    def from_block(self, g, s, o):
+        spot = self.spot
+        block = (spot.block + spot.blocks - s) % spot.blocks
+        place = self.piece(g, flip(spot.plane, o), block)
+        return send(
+            place, place, self.block_sems, (self.base + g, s, o), spot.at(block=block)
+        )
+
+    def begin(self, g):
+        self.own(g).start()
+        if self.direct:
+            for o in (1, 2, 3):
+                self.to_role(g, o).start()
+
+    def spread(self, g):
+        self.own(g).wait()
+        if self.direct:
+            for o in (1, 2, 3):
+                self.from_role(g, o).wait_recv()
+        for o in (1, 2, 3):
+            self.to_plane(g, o).start()
+        for s in range(1, self.spot.blocks):
+            self.to_block(g, s, 0).start()
+
+    def relay(self, g, o):
+        self.from_plane(g, o).wait_recv()
+        for s in range(1, self.spot.blocks):
+            self.to_block(g, s, o).start()
+
+    def complete(self, g):
+        for s in range(1, self.spot.blocks):
+            for o in range(4):
+                self.from_block(g, s, o).wait_recv()
+
+    def drain(self, g):
+        for o in (1, 2, 3):
+            if self.direct:
+                self.to_role(g, o).wait_send()
+            self.to_plane(g, o).wait_send()
+        for s in range(1, self.spot.blocks):
+            for o in range(4):
+                self.to_block(g, s, o).wait_send()
+
+
+class Exchange:
+    def __init__(self, spot, sent, core_in, chip, side_in, full, core_sems, side_sems, back_sems):
+        self.spot = spot
+        self.sent, self.core_in, self.chip, self.side_in, self.full = sent, core_in, chip, side_in, full
+        self.core_sems, self.side_sems, self.back_sems = core_sems, side_sems, back_sems
+        self.mine = lanes(spot.core * HALF, HALF)
+        self.theirs = lanes((1 - spot.core) * HALF, HALF)
+
+    def core_copy(self, i):
+        return send(
+            self.sent.at[i], self.core_in.at[i], self.core_sems, (i,),
+            self.spot.at(role=flip1(self.spot.role)),
+        )
+
+    def side_copy(self, i, slot):
+        return send(
+            self.chip.at[i], self.side_in.at[i, slot], self.side_sems, (i, slot),
+            self.spot.at(role=flip2(self.spot.role)),
+        )
+
+    def back_copy(self, i):
+        place = self.full.at[i, :, self.mine]
+        return send(place, place, self.back_sems, (i,), self.spot.at(role=flip1(self.spot.role)))
+
+    def back_in(self, i):
+        place = self.full.at[i, :, self.theirs]
+        return send(place, place, self.back_sems, (i,), self.spot.at(role=flip1(self.spot.role)))
+
+    def reduce(self, i, product, kept):
+        rows = kept.shape[0]
+        self.sent[i] = product(self.theirs).astype(bf16)
+        self.core_copy(i).start()
+        kept[...] = product(self.mine)
+        copy = self.core_copy(i)
+        copy.wait_recv()
+
+        def add(c, carry):
+            r = pl.ds(pl.multiple_of(c * 16, 16), 16)
+            self.chip[i, r] = (kept[r] + self.core_in[i, r].astype(f32)).astype(bf16)
+            return carry
+
+        lax.fori_loop(0, rows // 16, add, 0, unroll=2)
+        copy.wait_send()
+
+    def finish(self, i, slot):
+        copy = self.side_copy(i, slot)
+        copy.wait_recv()
+        rows = self.chip.shape[1]
+
+        def add(c, carry):
+            r = pl.ds(pl.multiple_of(c * 16, 16), 16)
+            total = self.chip[i, r].astype(f32) + self.side_in[i, slot, r].astype(f32)
+            self.full[i, r, self.mine] = total.astype(bf16)
+            return carry
+
+        lax.fori_loop(0, rows // 16, add, 0, unroll=2)
+        self.back_copy(i).start()
+        copy.wait_send()
+        self.back_in(i).wait_recv()
+        self.back_copy(i).wait_send()
+
+
+def each_rows(rows, size, step, unroll=1):
+    def one(c, carry):
+        step(pl.ds(pl.multiple_of(c * size, size), size))
+        return carry
+
+    lax.fori_loop(0, rows // size, one, 0, unroll=unroll)
+
+
+def forward_kernel(cfg, *refs):
+    fsdp, head, tokens, rows, direct = cfg
+    (
+        own_image, own_cot, packed, extras,
+        weights_out, vec_out, normed_out, unit_out, inverse_out, qkv_out, att_out, lse_out, hidden_out,
+        stream_out, chip_out, cot_out,
+        whole, extra, vec, pair, cots, stream, normed, unit, inverse, qkv, scores, soft, att_sum, att,
+        row_scale, lse, lse_rows, hidden, low_hidden, active, kept,
+        sent, core_in, chip, side_in, full,
+        role_s, role_r, plane_s, plane_r, block_s, block_r, local_sem,
+        core_s, core_r, side_s, side_r, back_s, back_r,
+        share_s, share_r, store_sem,
+    ) = refs
+    spot = Spot(fsdp, head)
+    groups = 3 * LAYERS
+    greet(spot.partners())
+    sems = ((role_s, role_r), (plane_s, plane_r), (block_s, block_r))
+    small = Gather(spot, extras, extra, *sems, groups, local_sem, direct)
+    large = Gather(spot, packed, whole, *sems, 0, local_sem, direct)
+    exchange = Exchange(
+        spot, sent, core_in, chip, side_in, full, (core_s, core_r), (side_s, side_r), (back_s, back_r)
+    )
+    owner = spot.core == spot.plane % 2
+    x, other_x = spot.side, 1 - spot.side
+
+    small.begin(0)
+    large.begin(0)
+
+    def share(source, held, n):
+        across = send(
+            source, held.at[x], (share_s, share_r), (n, 0), spot.at(role=flip2(spot.role))
+        )
+        across_in = send(
+            held.at[other_x], held.at[other_x], (share_s, share_r), (n, 0), spot.at(role=flip2(spot.role))
+        )
+        down = [
+            send(src, held.at[at], (share_s, share_r), (n, 1 + k), spot.at(role=flip1(spot.role)))
+            for k, (src, at) in enumerate(((source, x), (held.at[other_x], other_x)))
+        ]
+        mine = pltpu.make_async_copy(source, held.at[x], store_sem.at[30 + n])
+        return across, across_in, down, mine
+
+    def share_begin(source, held, n):
+        across, across_in, down, mine = share(source, held, n)
+
+        @pl.when(owner)
+        def _():
+            across.start()
+            mine.start()
+            down[0].start()
+
+    def share_end(source, held, n):
+        across, across_in, down, mine = share(source, held, n)
+
+        @pl.when(owner)
+        def _():
+            across_in.wait_recv()
+            down[1].start()
+            across.wait_send()
+            mine.wait()
+            down[0].wait_send()
+            down[1].wait_send()
+
+        @pl.when(jnp.logical_not(owner))
+        def _():
+            down[0].wait_recv()
+            down[1].wait_recv()
+
+    share_begin(own_image, pair, 0)
+    for g in range(1, groups):
+        large.begin(g)
+    small.spread(0)
+    large.spread(0)
+    large.spread(1)
+    for o in (1, 2, 3):
+        small.relay(0, o)
+    for o in (1, 2, 3):
+        large.relay(0, o)
+    large.spread(2)
+    share_end(own_image, pair, 0)
+    small.complete(0)
+
+    cols = D // fsdp
+    quarter = 64
+    for l in range(LAYERS):
+        vec[l, 0:6] = extra[0, 0, 16 * l : 16 * l + 16].astype(f32)[0:6]
+
+        def selector(width, offset):
+            c = lax.broadcasted_iota(jnp.int32, (D, width), 0)
+            j = lax.broadcasted_iota(jnp.int32, (D, width), 1)
+            return jnp.where((c // cols == j % fsdp) & (c % cols == offset + j // fsdp), 1.0, 0.0).astype(bf16)
+
+        per = quarter // fsdp
+        for plane in range(4):
+            block = extra[0, plane, 16 * l : 16 * l + 16]
+            vec[l, 6:7, plane * 256 : plane * 256 + 256] = dot(block, selector(256, 2 * per), 1, 0)[6:7]
+            if plane % 2 == 0:
+                following = extra[0, plane + 1, 16 * l : 16 * l + 16]
+                for k in range(2):
+                    pick = selector(quarter, k * per)
+                    two = jnp.concatenate([dot(block, pick, 1, 0), dot(following, pick, 1, 0)], axis=1)
+                    at = k * 256 + plane * quarter
+                    vec[l, 7:8, at : at + 128] = two[6:7]
+    store_vec = pltpu.make_async_copy(vec, vec_out, store_sem.at[28])
+    store_vec.start()
+    large.complete(0)
+
+    lane_head = lax.broadcasted_iota(jnp.int32, (1, 256), 1) // HD
+    key_bias = jnp.where(lax.broadcasted_iota(jnp.int32, (1, rows), 1) < tokens, 0.0, -1e30)
+
+    def stores(l, n, i):
+        return [
+            pltpu.make_async_copy(normed.at[i], normed_out.at[l, n, i], store_sem.at[0 + i]),
+            pltpu.make_async_copy(unit.at[i], unit_out.at[l, n, i], store_sem.at[2 + i]),
+            pltpu.make_async_copy(inverse.at[i], inverse_out.at[l, n, i], store_sem.at[4 + i]),
+        ]
+
+    def norm(l, n, i, read):
+        def step(r):
+            v = read(r)
+            stream[i, r] = v
+            average = jnp.mean(v, axis=-1, keepdims=True)
+            centred = v - average
+            scale = lax.rsqrt(jnp.mean(centred * centred, axis=-1, keepdims=True) + epsilon)
+            u = centred * scale
+            unit[i, r] = u.astype(bf16)
+            inverse[i, r] = jnp.broadcast_to(scale, (16, 128))
+            normed[i, r] = (u * vec[l, n : n + 1] + vec[l, 2 + n : 3 + n]).astype(bf16)
+
+        each_rows(rows, 16, step, unroll=2)
+        for copy in stores(l, n, i):
+            copy.start()
+
+    def attn_stage(l, i):
+        g = 3 * l
+
+        @pl.when(l > 0)
+        def _():
+            exchange.finish(i, 1)
+            for copy in stores(l - 1, 1, i):
+                copy.wait()
+            before = jnp.maximum(l - 1, 0)
+            norm(l, 0, i, lambda r: stream[i, r] + full[i, r].astype(f32) + vec[before, 5:6])
+
+        @pl.when(l == 0)
+        def _():
+            norm(l, 0, i, lambda r: pair[i, r].astype(f32))
+
+        store_qkv = pltpu.make_async_copy(qkv, qkv_out.at[l, i], store_sem.at[6])
+        store_att = pltpu.make_async_copy(att.at[i], att_out.at[l, i], store_sem.at[8 + i])
+        store_lse = pltpu.make_async_copy(lse_rows.at[i], lse_out.at[l, i], store_sem.at[10 + i])
+
+        @pl.when(l + i > 0)
+        def _():
+            store_qkv.wait()
+
+        @pl.when(l > 0)
+        def _():
+            store_att.wait()
+            store_lse.wait()
+
+        for k in range(3):
+            w = whole[g, :, k * HD : k * HD + HD].reshape(256, D)
+            part = dot(normed[i], w, 1, 1)
+            if k == 0:
+                part = part + vec[l, 7:8, 0:256]
+            if k == 2:
+                part = part + vec[l, 7:8, 256:512]
+            qkv[:, k * 256 : k * 256 + 256] = part.astype(bf16)
+        store_qkv.start()
+
+        att_sum[...] = jnp.zeros_like(att_sum)
+        lse[...] = jnp.zeros_like(lse)
+
+        def one_head(h, carry):
+            mask = jnp.where(lane_head == h, 1.0, 0.0)
+            q = qkv[:, 0:256] * (mask * HD ** (-0.5)).astype(bf16)
+            scores[...] = dot(q, qkv[:, 256:512], 1, 1)
+            here = lax.broadcasted_iota(jnp.int32, (1, 128), 1) == h
+
+            def step(r):
+                s = scores[r] + key_bias
+                largest = jnp.max(s, axis=-1, keepdims=True)
+                e = jnp.exp(s - largest)
+                total = jnp.sum(e, axis=-1, keepdims=True)
+                soft[r] = e.astype(bf16)
+                row_scale[r] = jnp.broadcast_to(1.0 / total, (16, 128))
+                lse[r] = jnp.where(here, largest + jnp.log(total), lse[r])
+
+            each_rows(rows, 16, step, unroll=2)
+            o = dot(soft[...], qkv[:, 512:768], 1, 0)
+            scale = row_scale[...]
+            att_sum[...] += o * jnp.concatenate([scale, scale], axis=1) * mask
+            return carry
+
+        lax.fori_loop(0, 4, one_head, 0)
+        att[i] = att_sum[...].astype(bf16)
+        lse_rows[i] = jnp.transpose(lse[...])[0:8]
+        store_att.start()
+        store_lse.start()
+        exchange.reduce(
+            i, lambda at: dot(att[i], whole[g, :, 192:256, at].reshape(256, HALF), 1, 0), kept
+        )
+        exchange.side_copy(i, 0).start()
+
+    def mlp_stage(l, i):
+        g = 3 * l
+        exchange.finish(i, 0)
+        for copy in stores(l, 0, i):
+            copy.wait()
+        norm(l, 1, i, lambda r: stream[i, r] + full[i, r].astype(f32) + vec[l, 4:5])
+        store_hidden = pltpu.make_async_copy(low_hidden.at[i], hidden_out.at[l, i], store_sem.at[12 + i])
+
+        @pl.when(l > 0)
+        def _():
+            store_hidden.wait()
+
+        hidden[...] = dot(normed[i], whole[g + 1].reshape(D, D), 1, 1)
+
+        def step(r):
+            v = hidden[r] + vec[l, 6:7]
+            low_hidden[i, r] = v.astype(bf16)
+            active[r] = (v * (0.5 + 0.5 * lax.erf(v * (0.5**0.5)))).astype(bf16)
+
+        each_rows(rows, 16, step, unroll=2)
+        store_hidden.start()
+
+        @pl.when(i == 0)
+        def _():
+            large.complete(g + 2)
+
+        exchange.reduce(i, lambda at: dot(active[...], whole[g + 2, :, :, at].reshape(D, HALF), 1, 0), kept)
+
+        @pl.when(l < LAYERS - 1)
+        def _():
+            exchange.side_copy(i, 1).start()
+
+        @pl.when(l == LAYERS - 1)
+        def _():
+            pltpu.make_async_copy(chip.at[i], chip_out.at[i], store_sem.at[14 + i]).start()
+            pltpu.make_async_copy(stream.at[i], stream_out.at[i], store_sem.at[16 + i]).start()
+
+    def store_weights(g):
+        return pltpu.make_async_copy(whole.at[g], weights_out.at[g], store_sem.at[18 + g])
+
+    def one_layer(l, carry):
+        g = 3 * l
+
+        @pl.when(l > 0)
+        def _():
+            large.complete(g)
+
+        attn_stage(l, 0)
+
+        @pl.when(l == 0)
+        def _():
+            share_begin(own_cot, cots, 1)
+            large.spread(3)
+
+        for o in (1, 2, 3):
+            large.relay(g + 1, o)
+        attn_stage(l, 1)
+
+        for o in (1, 2, 3):
+            large.relay(g + 2, o)
+
+        @pl.when(l == 0)
+        def _():
+            large.spread(4)
+
+        large.complete(g + 1)
+        mlp_stage(l, 0)
+
+        @pl.when(l == 0)
+        def _():
+            for o in (1, 2, 3):
+                large.relay(3, o)
+            large.spread(5)
+
+        mlp_stage(l, 1)
+        for k in range(3):
+            store_weights(g + k).start()
+        return carry
+
+    lax.fori_loop(0, LAYERS, one_layer, 0)
+    share_end(own_cot, cots, 1)
+    store_cots = pltpu.make_async_copy(cots, cot_out, store_sem.at[29])
+    store_cots.start()
+    last = LAYERS - 1
+    for i in range(2):
+        for copy in stores(last, 1, i):
+            copy.wait()
+        pltpu.make_async_copy(att.at[i], att_out.at[last, i], store_sem.at[8 + i]).wait()
+        pltpu.make_async_copy(lse_rows.at[i], lse_out.at[last, i], store_sem.at[10 + i]).wait()
+        pltpu.make_async_copy(low_hidden.at[i], hidden_out.at[last, i], store_sem.at[12 + i]).wait()
+        pltpu.make_async_copy(chip.at[i], chip_out.at[i], store_sem.at[14 + i]).wait()
+        pltpu.make_async_copy(stream.at[i], stream_out.at[i], store_sem.at[16 + i]).wait()
+    pltpu.make_async_copy(qkv, qkv_out.at[last, 1], store_sem.at[6]).wait()
+    store_vec.wait()
+    store_cots.wait()
+
+    def finish_group(g, carry):
+        store_weights(g).wait()
+        large.drain(g)
+        return carry
+
+    lax.fori_loop(0, groups, finish_group, 0)
+    small.drain(0)
+
+
+def forward_call(fsdp, head, tokens, rows, direct, own_image, own_cot, packed, extras):
+    groups = 3 * LAYERS
+    blocks = fsdp // TP
+    anyspace = pl.BlockSpec(memory_space=pl.ANY)
+    shape = jax.ShapeDtypeStruct
+    dma = pltpu.SemaphoreType.DMA
+    out_shape = (
+        shape((groups, 4, 256, D), bf16),
+        shape((LAYERS, 8, D), f32),
+        shape((LAYERS, 2, 2, rows, D), bf16),
+        shape((LAYERS, 2, 2, rows, D), bf16),
+        shape((LAYERS, 2, 2, rows, 128), f32),
+        shape((LAYERS, 2, rows, 768), bf16),
+        shape((LAYERS, 2, rows, 256), bf16),
+        shape((LAYERS, 2, 8, rows), f32),
+        shape((LAYERS, 2, rows, D), bf16),
+        shape((2, rows, D), f32),
+        shape((2, rows, HALF), bf16),
+        shape((2, rows, D), bf16),
+    )
+    scratch = [
+        pltpu.VMEM((groups, 4, 256, D), bf16),
+        pltpu.VMEM((1, 4, 32, D), bf16),
+        pltpu.VMEM((LAYERS, 8, D), f32),
+        pltpu.VMEM((2, rows, D), bf16),
+        pltpu.VMEM((2, rows, D), bf16),
+        pltpu.VMEM((2, rows, D), f32),
+        pltpu.VMEM((2, rows, D), bf16),
+        pltpu.VMEM((2, rows, D), bf16),
+        pltpu.VMEM((2, rows, 128), f32),
+        pltpu.VMEM((rows, 768), bf16),
+        pltpu.VMEM((rows, rows), f32),
+        pltpu.VMEM((rows, rows), bf16),
+        pltpu.VMEM((rows, 256), f32),
+        pltpu.VMEM((2, rows, 256), bf16),
+        pltpu.VMEM((rows, 128), f32),
+        pltpu.VMEM((rows, 128), f32),
+        pltpu.VMEM((2, 8, rows), f32),
+        pltpu.VMEM((rows, D), f32),
+        pltpu.VMEM((2, rows, D), bf16),
+        pltpu.VMEM((rows, D), bf16),
+        pltpu.VMEM((rows, HALF), f32),
+        pltpu.VMEM((2, rows, HALF), bf16),
+        pltpu.VMEM((2, rows, HALF), bf16),
+        pltpu.VMEM((2, rows, HALF), bf16),
+        pltpu.VMEM((2, 2, rows, HALF), bf16),
+        pltpu.VMEM((2, rows, D), bf16),
+        dma((groups + 1, 4)), dma((groups + 1, 4)),
+        dma((groups + 1, 4)), dma((groups + 1, 4)),
+        dma((groups + 1, blocks, 4)), dma((groups + 1, blocks, 4)),
+        dma((groups + 1,)),
+        dma((2,)), dma((2,)),
+        dma((2, 2)), dma((2, 2)),
+        dma((2,)), dma((2,)),
+        dma((2, 3)), dma((2, 3)),
+        dma((32,)),
+    ]
+    return pl.pallas_call(
+        functools.partial(forward_kernel, (fsdp, head, tokens, rows, direct)),
+        out_shape=out_shape,
+        in_specs=[anyspace] * 4,
+        out_specs=tuple(anyspace for _ in out_shape),
+        scratch_shapes=scratch,
+        compiler_params=pltpu.CompilerParams(
+            collective_id=0, has_side_effects=True, vmem_limit_bytes=60 << 20
+        ),
+        name="forward_layers",
+    )(own_image, own_cot, packed, extras)
 
 
 def product(left, right, form):
@@ -70,44 +700,6 @@
     return [jnp.where(top, c, a), jnp.where(top, d, b), jnp.where(top, a, c), jnp.where(top, b, d)]
 
 
-def gather_group(pl, pack):
-    exchanged = [lax.dynamic_index_in_dim(pack, pl.role, 0, False)]
-    for bits in (1, 2, 3):
-        exchanged.append(pl.role_xor(lax.dynamic_index_in_dim(pack, pl.role ^ bits, 0, False), bits))
-    piece = jnp.concatenate(by_xor(exchanged, pl.role), axis=-1)
-    planes = [piece] + [pl.plane_xor(piece, bits) for bits in (1, 2, 3)]
-    planes = jnp.stack(planes, axis=1)
-    if pl.blocks == 2:
-        other = pl.block_shift(planes, 1)
-        first = pl.block == 0
-        both = [jnp.where(first, planes, other), jnp.where(first, other, planes)]
-    else:
-        shifted = jnp.stack([planes] + [pl.block_shift(planes, s) for s in range(1, pl.blocks)])
-        both = [
-            lax.dynamic_index_in_dim(shifted, (pl.block - b) % pl.blocks, 0, False)
-            for b in range(pl.blocks)
-        ]
-    whole = jnp.concatenate(both, axis=-1)
-    return whole.reshape(whole.shape[0], whole.shape[1] * whole.shape[2], whole.shape[3])
-
-
-def scatter_group(pl, grads):
-    mats, rows, width = grads.shape
-    grads = grads.reshape(mats, pl.head, rows // pl.head, pl.blocks, width // pl.blocks)
-    total = lax.dynamic_index_in_dim(grads, pl.block, 3, False)
-    for step in range(1, pl.blocks):
-        sent = lax.dynamic_index_in_dim(grads, (pl.block + step) % pl.blocks, 3, False)
-        total = total + wide(pl.block_shift(low(sent), step))
-    mine = total[:, 0]
-    for bits in (1, 2, 3):
-        mine = mine + wide(pl.plane_xor(low(total[:, bits]), bits))
-    mine = low(mine).reshape(mats, rows // pl.head, TP, -1)
-    exchanged = [lax.dynamic_index_in_dim(mine, pl.role, 2, False)]
-    for bits in (1, 2, 3):
-        exchanged.append(pl.role_xor(lax.dynamic_index_in_dim(mine, pl.role ^ bits, 2, False), bits))
-    return wide(jnp.stack(by_xor(exchanged, pl.role)))
-
-
 def sum_roles(pl, rows):
     half = rows.shape[1] // 2
     core = pl.role & 1
@@ -124,15 +716,22 @@
     )
 
 
-def share_images(pl, held):
-    own = lax.dynamic_index_in_dim(held, pl.plane // 2, 0, False)
-    owner = lambda b, r, p: (r & 1) == (p & 1)
-    other = pl.role_xor(own, 2, owner)
-    top = pl.role >= 2
-    pair = jnp.stack([jnp.where(top, other, own), jnp.where(top, own, other)])
-    passed = pl.role_xor(pair, 1, owner)
-    return jnp.where((pl.role & 1) == (pl.plane & 1), pair, passed)
-
+def scatter_group(pl, grads):
+    mats, head, units, width = grads.shape
+    grads = grads.reshape(mats, head, units, pl.blocks, width // pl.blocks)
+    total = lax.dynamic_index_in_dim(grads, pl.block, 3, False)
+    for step in range(1, pl.blocks):
+        sent = lax.dynamic_index_in_dim(grads, (pl.block + step) % pl.blocks, 3, False)
+        total = total + wide(pl.block_shift(low(sent), step))
+    mine = lax.dynamic_index_in_dim(total, pl.plane, 1, False)
+    for bits in (1, 2, 3):
+        sent = lax.dynamic_index_in_dim(total, pl.plane ^ bits, 1, False)
+        mine = mine + wide(pl.plane_xor(low(sent), bits))
+    mine = low(mine).reshape(mats, units, TP, -1)
+    exchanged = [lax.dynamic_index_in_dim(mine, pl.role, 2, False)]
+    for bits in (1, 2, 3):
+        exchanged.append(pl.role_xor(lax.dynamic_index_in_dim(mine, pl.role ^ bits, 2, False), bits))
+    return wide(jnp.stack(by_xor(exchanged, pl.role)))
 
 def return_images(pl, pair):
     mine = low(jnp.where(pl.role >= 2, pair[1], pair[0]))
@@ -164,32 +763,6 @@
 
 def split_heads(rows):
     return rows.reshape(rows.shape[0], rows.shape[1] // HD, HD)
-
-
-def layer_forward(pl, stream, weights):
-    (w_qkv, w_out), (w_in, w_down), qv_bias, in_bias, gains, shifts = weights
-    normed, unit_first, inverse_first = norm_rows(stream, gains[0], shifts[0])
-    queries = low(product(normed, w_qkv[0], "sd,ad->sa") + qv_bias[0])
-    key_rows = low(product(normed, w_qkv[1], "sd,ad->sa"))
-    value_rows = low(product(normed, w_qkv[2], "sd,ad->sa") + qv_bias[1])
-    scores = product(split_heads(queries), split_heads(key_rows), "qhd,khd->hqk") * HD ** (-0.5)
-    largest = jnp.max(scores, axis=-1, keepdims=True)
-    logsum = largest + jnp.log(jnp.sum(jnp.exp(scores - largest), axis=-1, keepdims=True))
-    soft_low = low(jnp.exp(scores - logsum))
-    attended = product(soft_low, split_heads(value_rows), "hqk,khd->qhd")
-    attended = low(attended.reshape(queries.shape))
-    branch = sum_roles(pl, product(attended, w_out, "sa,ad->sd"))
-    stream = stream + branch + shifts[2]
-    normed_second, unit_second, inverse_second = norm_rows(stream, gains[1], shifts[1])
-    hidden = product(normed_second, w_in, "sd,fd->sf") + in_bias
-    active = low(jax.nn.gelu(hidden, approximate=False))
-    branch = sum_roles(pl, product(active, w_down, "sf,fd->sd"))
-    stream = stream + branch + shifts[3]
-    stored = (
-        unit_first, inverse_first, normed, queries, key_rows, value_rows, logsum, attended,
-        unit_second, inverse_second, normed_second, hidden, active,
-    )
-    return stream, stored
 
 
 def layer_backward(pl, upstream, weights, stored):
@@ -243,57 +816,81 @@
     return upstream, (attn_grads, mlp_grads, grad_qv, grad_in_bias, by_feature)
 
 
+def pack_inputs(pl, w_qkv, w_out, w_in, w_down, qv_bias, in_bias, gains, shifts):
+    fsdp = lax.axis_size("fsdp")
+    cols = w_qkv.shape[2]
+    groups = []
+    small = []
+    for l in range(LAYERS):
+        attn = jnp.concatenate([w_qkv[l].transpose(0, 2, 1), w_out[l][None]]).reshape(4, TP, HD, cols)
+        groups.append(attn.transpose(1, 0, 2, 3).reshape(TP, 256, cols))
+        groups.append(w_in[l].T.reshape(TP, 256, cols))
+        groups.append(w_down[l].reshape(TP, 256, cols))
+        features = jnp.concatenate([gains[l], shifts[l]])
+        features = jnp.broadcast_to(features[None], (TP, 6, cols))
+        qv = qv_bias[l].reshape(2, TP, -1).transpose(1, 0, 2).reshape(TP, -1)
+        units = jnp.concatenate([qv, in_bias[l].reshape(TP, -1)], axis=1)
+        units = jnp.pad(units, ((0, 0), (0, cols - units.shape[1])))[:, None]
+        small.append(jnp.pad(jnp.concatenate([features, units], axis=1), ((0, 0), (0, 9), (0, 0))))
+    packed, extras = jnp.stack(groups), jnp.concatenate(small, axis=1)[None]
+    if cols % 128 == 0:
+        return packed, extras, True
+    return gather_roles(pl, packed), gather_roles(pl, extras), False
+
+
+def gather_roles(pl, pack):
+    exchanged = [lax.dynamic_index_in_dim(pack, pl.role, 1, False)]
+    for bits in (1, 2, 3):
+        exchanged.append(pl.role_xor(lax.dynamic_index_in_dim(pack, pl.role ^ bits, 1, False), bits))
+    return jnp.concatenate(by_xor(exchanged, pl.role), axis=-1)
+
+
 def body(images, cotangent, w_qkv, w_out, w_in, w_down, qv_bias, in_bias, gains, shifts):
     fsdp, head = lax.axis_size("fsdp"), lax.axis_size("head")
-    pl = Places(fsdp, head)
+    places = Places(fsdp, head)
     cols = w_qkv.shape[2]
     width, units = w_qkv.shape[3] // TP, w_in.shape[2] // TP
-
-    first = share_images(pl, images)
-    small = jnp.concatenate(
-        [qv_bias.reshape(-1), in_bias.reshape(-1), gains.reshape(-1), shifts.reshape(-1)]
-    )
-    small = wide(lax.all_gather(small, AXES, axis=0, tiled=False)).reshape(fsdp, head, -1)
-    sizes = [qv_bias.size, in_bias.size, gains.size, shifts.size]
-    marks = [0]
-    for s in sizes:
-        marks.append(marks[-1] + s)
-    qv_all, in_all, gain_all, shift_all = [small[:, :, a:b] for a, b in zip(marks, marks[1:])]
-    gain_all = gain_all[:, 0].reshape(fsdp, LAYERS, 2, cols).transpose(1, 2, 0, 3).reshape(LAYERS, 2, -1)
-    shift_all = shift_all[:, 0].reshape(fsdp, LAYERS, 4, cols).transpose(1, 2, 0, 3).reshape(LAYERS, 4, -1)
-    xor_planes = pl.plane ^ jnp.arange(head)
-    qv_all = qv_all.reshape(fsdp, head, LAYERS, 2, -1).transpose(2, 3, 1, 4, 0).reshape(LAYERS, 2, head, TP, width)
-    qv_mine = lax.dynamic_index_in_dim(qv_all, pl.role, 3, False)[:, :, xor_planes].reshape(LAYERS, 2, -1)
-    in_all = in_all.reshape(fsdp, head, LAYERS, -1).transpose(2, 1, 3, 0).reshape(LAYERS, head, TP, units)
-    in_mine = lax.dynamic_index_in_dim(in_all, pl.role, 2, False)[:, xor_planes].reshape(LAYERS, -1)
-
-    weights = []
-    for l in range(LAYERS):
-        attn = jnp.concatenate([w_qkv[l].transpose(0, 2, 1), w_out[l][None]]).reshape(4, TP, width, cols)
-        mlp = jnp.stack([w_in[l].T, w_down[l]]).reshape(2, TP, units, cols)
-        attn = gather_group(pl, attn.transpose(1, 0, 2, 3))
-        mlp = gather_group(pl, mlp.transpose(1, 0, 2, 3))
-        weights.append(((attn[:3], attn[3]), (mlp[0], mlp[1]), qv_mine[l], in_mine[l], gain_all[l], shift_all[l]))
-
-    streams = [wide(first[0]), wide(first[1])]
-    stored = [[], []]
-    for l in range(LAYERS):
-        for i in range(2):
-            streams[i], kept = layer_forward(pl, streams[i], weights[l])
-            stored[i].append(kept)
-    block_out = return_images(pl, streams)
-    second = share_images(pl, cotangent)
-    upstreams = [wide(second[0]), wide(second[1])]
+    tokens = images.shape[1]
+    rows = -(-tokens // 32) * 32
+    packed, extras, direct = pack_inputs(places, w_qkv, w_out, w_in, w_down, qv_bias, in_bias, gains, shifts)
+    pad = ((0, rows - tokens), (0, 0))
+    own_image = jnp.pad(lax.dynamic_index_in_dim(images, places.plane // 2, 0, False), pad)
+    own_cot = jnp.pad(lax.dynamic_index_in_dim(cotangent, places.plane // 2, 0, False), pad)
+    (
+        whole, vec, normed, unit, inverse, qkv, att, lse, hidden, stream, chip, cots
+    ) = forward_call(fsdp, head, tokens, rows, direct, own_image, own_cot, packed, extras)
+    streams = []
+    core = places.role & 1
+    for i in range(2):
+        total = low(wide(chip[i]) + wide(places.role_xor(chip[i], 2)))
+        other = places.role_xor(total, 1)
+        both = jnp.concatenate([jnp.where(core == 0, total, other), jnp.where(core == 0, other, total)], axis=1)
+        streams.append((stream[i] + wide(both) + vec[1, 5])[:tokens])
+    block_out = return_images(places, streams)
+    upstreams = [wide(cots[i, :tokens]) for i in range(2)]
     parts = {}
     for l in reversed(range(LAYERS)):
         sums = None
+        attn_w = whole[3 * l].reshape(4, 4, HD, D).transpose(1, 0, 2, 3).reshape(4, 256, D)
+        weights = (
+            (attn_w[:3], attn_w[3]),
+            (whole[3 * l + 1].reshape(D, D), whole[3 * l + 2].reshape(D, D)),
+            None, None, vec[l, 0:2], None,
+        )
         for i in range(2):
-            upstreams[i], grads = layer_backward(pl, upstreams[i], weights[l], stored[i][l])
+            kept = (
+                wide(unit[l, 0, i, :tokens]), inverse[l, 0, i, :tokens, 0:1], normed[l, 0, i, :tokens],
+                qkv[l, i, :tokens, 0:256], qkv[l, i, :tokens, 256:512], qkv[l, i, :tokens, 512:768],
+                lse[l, i, 0:4, :tokens][:, :, None], att[l, i, :tokens],
+                wide(unit[l, 1, i, :tokens]), inverse[l, 1, i, :tokens, 0:1], normed[l, 1, i, :tokens],
+                wide(hidden[l, i, :tokens]), low(jax.nn.gelu(wide(hidden[l, i, :tokens]), approximate=False)),
+            )
+            upstreams[i], grads = layer_backward(places, upstreams[i], weights, kept)
             sums = grads if sums is None else tuple(a + b for a, b in zip(sums, grads))
-        mlp = scatter_group(pl, sums[1])
-        attn = scatter_group(pl, sums[0])
+        mlp = scatter_group(places, sums[1].reshape(2, 4, 256, D))
+        attn = scatter_group(places, sums[0].reshape(4, 4, HD, D))
         parts[l] = (attn, mlp, *sums[2:])
-    input_grad = return_images(pl, upstreams)
+    input_grad = return_images(places, upstreams)
 
     attn = jnp.stack([parts[l][0] for l in range(LAYERS)])
     mlp = jnp.stack([parts[l][1] for l in range(LAYERS)])
@@ -305,13 +902,13 @@
     grad_down = mlp[:, 1]
 
     by_feature = jnp.stack([parts[l][4] for l in range(LAYERS)])
-    qv = jnp.stack([parts[l][2] for l in range(LAYERS)]).reshape(LAYERS, 2, head, width)[:, :, xor_planes]
-    inner = jnp.stack([parts[l][3] for l in range(LAYERS)]).reshape(LAYERS, head, units)[:, xor_planes]
+    qv = jnp.stack([parts[l][2] for l in range(LAYERS)]).reshape(LAYERS, 2, head, width)
+    inner = jnp.stack([parts[l][3] for l in range(LAYERS)]).reshape(LAYERS, head, units)
     qv_full = lax.dynamic_update_index_in_dim(
-        jnp.zeros((LAYERS, 2, head, TP, width), jnp.float32), qv, pl.role, 3
+        jnp.zeros((LAYERS, 2, head, TP, width), jnp.float32), qv, places.role, 3
     )
     inner_full = lax.dynamic_update_index_in_dim(
-        jnp.zeros((LAYERS, head, TP, units), jnp.float32), inner, pl.role, 2
+        jnp.zeros((LAYERS, head, TP, units), jnp.float32), inner, places.role, 2
     )
     vector = jnp.concatenate([by_feature.reshape(-1) / TP, qv_full.reshape(-1), inner_full.reshape(-1)])
     vector = lax.psum(vector, AXES)

time: 1470 us -> 1170 us (0.80)
  Pallas kernels: 0 us -> 253 us
  waiting for transfers between devices: 435 us -> 277 us
  other arithmetic: 273 us -> 152 us
  starting transfers between devices: 186 us -> 90.8 us
  blocking collectives: 70.1 us -> 0 us
  matrix products: 210 us -> 143 us
  local copies, waits for them, and re-layouts: 261 us -> 227 us
    pallas_call x0 -> x1, Pallas kernels: none -> 253 us  [forward_call(): pl.pallas_call(functools.partial(forward_kernel, (fsdp, head, tokens, row...]
    ppermute x76 -> x40, waiting for transfers between devices: 123 us -> 47.1 us  [role_xor(): lax.ppermute(v, AXES, self.pairs(lambda b, r, p: (b, r ^ bits, p), sends))]
    all_gather x1 -> x0, blocking collectives: 70.1 us -> none  [body(): lax.all_gather(small, AXES, axis=0, tiled=False)]
    dot_general x96 -> x68, matrix products: 210 us -> 143 us  [product(): return jnp.einsum(form, left, right, preferred_element_type=jnp.float32)]
    ppermute x76 -> x40, starting transfers between devices: 106 us -> 44.2 us  [role_xor(): lax.ppermute(v, AXES, self.pairs(lambda b, r, p: (b, r ^ bits, p), sends))]
    convert_element_type x51 -> x27, other arithmetic: 94.9 us -> 35.2 us  [low(): return v.astype(jnp.bfloat16)]
    ppermute x8 -> x4, waiting for transfers between devices: 41.6 us -> 0.01 us  [block_shift(): lax.ppermute(v, AXES, self.pairs(lambda b, r, p: ((b + step) % self.block...]
    ppermute x30 -> x18, waiting for transfers between devices: 122 us -> 81.5 us  [plane_xor(): lax.ppermute(v, AXES, self.pairs(lambda b, r, p: (b, r, p ^ bits), sends))]
  transfers between devices with their start and end apart: 115 -> 63, of which waited for: 43 -> 18; matrix products, arithmetic and copies ran while one was open for 37% -> 36% of each run, Pallas kernels for 0% -> 0%
where the time goes in v2:
time: 1170 us; the launch traced here: 1160 us
  waiting for transfers between devices  277 us (24%)
  Pallas kernels  253 us (22%)
  local copies, waits for them, and re-layouts  227 us (19%)
  other arithmetic  152 us (13%)
  matrix products  143 us (12%)
  starting transfers between devices  90.8 us (8%)
  between operations  17.5 us (1%)
    pallas_call x1, Pallas kernels, forward_call(): pl.pallas_call(functools.partial(forward_kernel, (fsdp, head, tokens, row...  253 us
    psum x1, waiting for transfers between devices, body(): vector = lax.psum(vector, AXES)  149 us
    dot_general x68, matrix products, product(): return jnp.einsum(form, left, right, preferred_element_type=jnp.float32)  143 us
    ppermute x18, waiting for transfers between devices, plane_xor(): lax.ppermute(v, AXES, self.pairs(lambda b, r, p: (b, r, p ^ bits), sends))  81.5 us
    dot_general x23, local copies, waits for them, and re-layouts, product(): return jnp.einsum(form, left, right, preferred_element_type=jnp.float32)  74 us
    ppermute x40, waiting for transfers between devices, role_xor(): lax.ppermute(v, AXES, self.pairs(lambda b, r, p: (b, r ^ bits, p), sends))  47.1 us
    ppermute x40, starting transfers between devices, role_xor(): lax.ppermute(v, AXES, self.pairs(lambda b, r, p: (b, r ^ bits, p), sends))  44.2 us
    ppermute x18, starting transfers between devices, plane_xor(): lax.ppermute(v, AXES, self.pairs(lambda b, r, p: (b, r, p ^ bits), sends))  43.6 us
  transfers between devices with their start and end apart: 63, of which 18 were waited for; matrix products, arithmetic and copies ran while one was open for 36% of the time, Pallas kernels for 0%

profile of v2, /device:TPU:1, one launch (start us, length us, event | category | flops | bytes accessed | tf_op | source)
XLA Modules:
  0.0 1159.7 jit_solution(16348087967423384132)
XLA Ops:
  7.2 7.2 constant_dynamic-slice_fusion.17
  22.4 252.8 %forward_layers.1 = (bf16[6,4,256,1024]{3,2,1,0:T(8,128)(2,1)}, f32[2,8,1024]{2,1,0:T(8,128)}, bf16[2,2,2,608,1024]{4,3,2,1,0:T(8,128)(2,1)}, bf16[2,2,2,608,102...) custom-call(bf16[608,1024]{1,0:T(8,128)(2,1)} %pad.21.refs_0_, ...), custom_call_target="tpu_custom_call" | custom-call | tf_op jit(solution)/shard_map/forward_layers/pallas_call | solution.py:632
  275.2 9.4 fusion.566
  284.6 8.6 convert_reduce_fusion.10
  297.4 7.0 convert_reduce_fusion.11
  307.9 21.9 %fusion.413 = (bf16[1024,577]{0,1:T(8,128)(2,1)}, bf16[1024,577]{0,1:T(8,128)(2,1)}, bf16[1024,577]{0,1:T(8,128)(2,1)}, bf16[1024,577]{0,1:T(8,128)(2,1)}) fusion(bf16[2,2,608,1024]{3,2,1,0:T(8,128)(2,1)S(1)} %copy-done.66), kind=kLoop, calls=%fused_computation.542 | loop fusion | flops 155983872 | bytes 9453568 | tf_op jit(solution)/shard_map/sf,sd->fd/dot_general | solution.py:646
  331.4 7.3 slice_bitcast_fusion.4
  364.9 4.4 dot_general.499
  403.7 5.6 slice_bitcast_fusion.1
  448.9 4.4 dot_general.426
  479.5 7.6 collective-permute-done.8
  489.3 10.6 collective-permute-done.20
  508.8 5.2 fusion.379
  514.0 5.1 convert_bitcast_fusion.17
  522.9 4.6 convert_reduce_fusion.14
  527.6 4.3 multiply_reduce_fusion.3
  543.6 4.3 multiply_reduce_fusion.1
  560.1 6.3 collective-permute-start.10
  605.1 9.6 collective-permute-done.56
  614.7 17.7 %collective-permute-done.57 = bf16[2,256,512]{2,1,0:T(8,128)(2,1)S(1)} collective-permute-done((bf16[2,256,512]{2,1,0:T(8,128)(2,1)S(1)}, bf16[2,256,512]{2,1,0:T(8,128)(2,1)S(1)}, u32[]{:S(2)}, u32[]{:S(2)}) %collective-permute-start.57) | collective-permute-done | bytes 524320 | tf_op jit(solution)/shard_map/ppermute | solution.py:684
  642.9 5.8 copy.332
  653.1 10.6 collective-permute-start.42
  669.4 4.6 collective-permute-done.42
  674.3 7.6 collective-permute-done.44
  684.4 4.2 collective-permute-start.45
  696.1 4.4 fusion.380
  700.6 6.4 convert_reduce_fusion.9
  707.0 5.4 fusion.554
  716.3 7.2 convert_reduce_fusion.13
  727.2 7.1 convert_reduce_fusion.12
  760.5 9.9 collective-permute-done.26
  772.6 10.5 collective-permute-done.14
  785.4 4.4 maximum_add_fusion
  800.0 5.0 fusion.381
  810.3 4.6 convert_reduce_fusion.18
  814.9 4.3 multiply_reduce_fusion.2
  828.7 4.3 multiply_reduce_fusion
  848.0 4.1 dot_general.437
  864.9 5.7 fusion.556
  875.3 4.5 collective-permute-start.49
  888.6 13.6 %collective-permute-done.49 = bf16[2,256,512]{2,1,0:T(8,128)(2,1)S(1)} collective-permute-done((bf16[2,256,512]{2,1,0:T(8,128)(2,1)S(1)}, bf16[2,256,512]{2,1,0:T(8,128)(2,1)S(1)}, u32[]{:S(2)}, u32[]{:S(2)}) %collective-permute-start.49) | collective-permute-done | bytes 524320 | tf_op jit(solution)/shard_map/ppermute | solution.py:684
  903.0 13.3 %collective-permute-done.50 = bf16[2,256,512]{2,1,0:T(8,128)(2,1)} collective-permute-done((bf16[2,256,512]{2,1,0:T(8,128)(2,1)S(1)}, bf16[2,256,512]{2,1,0:T(8,128)(2,1)}, u32[]{:S(2)}, u32[]{:S(2)}) %collective-permute-start.50) | collective-permute-done | bytes 524320 | tf_op jit(solution)/shard_map/ppermute | solution.py:684
  935.0 10.6 collective-permute-start.35
  950.2 6.0 collective-permute-done.35
  956.2 8.8 collective-permute-done.36
  974.5 4.1 fusion.385
  990.4 148.8 %all-reduce.8.cloned.1.call-done = f32[24576]{0:T(1024)} async-done(((f32[24576]{0:T(1024)}), f32[24576]{0:T(1024)}) %all-reduce.8.cloned.1.call-update) | async-done | bytes 98320 | tf_op jit(solution)/shard_map/psum | solution.py:914
  1146.9 5.8 copy.333
  (814 shorter events, 406.6 us)
Async XLA Ops:
  7.2 1132.0 %all-reduce.8.cloned.1.call-start = ((), (), s32[]{:S(2)}) async-start(), calls=%async_computation | async-start | bytes 196608 | tf_op jit(solution)/shard_map/psum | solution.py:914
  296.6 173.9 %collective-permute-start.7 = (bf16[577,512]{1,0:T(8,128)(2,1)}, bf16[577,512]{1,0:T(8,128)(2,1)}, u32[]{:S(2)}, u32[]{:S(2)}) collective-permute-start(bf16[577,512]{1,0:T(8,128)(2,1)} %broadcast_select_fusion.31), channel_id=1, source_target_pairs={{0,4},{1,5},{2,6},{3,7},{4,0},{5,1},{6,2},{7,3},{8,12},{9,13},{10,... | collective-permute-start | bytes 1772552 | tf_op jit(solution)/shard_map/ppermute | solution.py:681
  307.8 164.8 %collective-permute-start.19 = (bf16[577,512]{1,0:T(8,128)(2,1)}, bf16[577,512]{1,0:T(8,128)(2,1)}, u32[]{:S(2)}, u32[]{:S(2)}) collective-permute-start(bf16[577,512]{1,0:T(8,128)(2,1)} %broadcast_select_fusion.19), channel_id=1, source_target_pairs={{0,4},{1,5},{2,6},{3,7},{4,0},{5,1},{6,2},{7,3},{8,12},{9,13},{10,... | collective-permute-start | bytes 1772552 | tf_op jit(solution)/shard_map/ppermute | solution.py:681
  382.8 207.3 %collective-permute-start.55 = (bf16[2,4,256,512]{3,2,1,0:T(8,128)(2,1)}, bf16[2,4,256,512]{3,2,1,0:T(8,128)(2,1)}, u32[]{:S(2)}, u32[]{:S(2)}) collective-permute-start(bf16[2,4,256,512]{3,2,1,0:T(8,128)(2,1)} %fusion.391), channel_id=1, source_target_pairs={{0,16},{1,17},{2,18},{3,19},{4,20},{5,21},{6,22},{7,23},{8,24},{9,... | collective-permute-start | bytes 6291464 | tf_op jit(solution)/shard_map/ppermute | solution.py:687
  384.5 91.0 %collective-permute-start = (bf16[608,512]{1,0:T(8,128)(2,1)}, bf16[608,512]{1,0:T(8,128)(2,1)}, u32[]{:S(2)}, u32[]{:S(2)}) collective-permute-start(bf16[608,512]{1,0:T(8,128)(2,1)} %get-tuple-element.225), channel_id=1, source_target_pairs={{0,8},{1,9},{2,10},{3,11},{4,12},{5,13},{6,14},{7,15},{8,0},{9,1},... | collective-permute-start | bytes 1867784 | tf_op jit(solution)/shard_map/ppermute | solution.py:681
  384.7 90.8 %collective-permute-start.2 = (bf16[608,512]{1,0:T(8,128)(2,1)}, bf16[608,512]{1,0:T(8,128)(2,1)}, u32[]{:S(2)}, u32[]{:S(2)}) collective-permute-start(bf16[608,512]{1,0:T(8,128)(2,1)} %get-tuple-element.226), channel_id=1, source_target_pairs={{0,8},{1,9},{2,10},{3,11},{4,12},{5,13},{6,14},{7,15},{8,0},{9,1},... | collective-permute-start | bytes 1867784 | tf_op jit(solution)/shard_map/ppermute | solution.py:681
  472.3 14.8 %collective-permute-start.8 = (bf16[577,512]{1,0:T(8,128)(2,1)S(1)}, bf16[577,512]{1,0:T(8,128)(2,1)S(1)}, u32[]{:S(2)}, u32[]{:S(2)}) collective-permute-start(bf16[577,512]{1,0:T(8,128)(2,1)S(1)} %add_convert_fusion.21), channel_id=1, source_target_pairs={{0,8},{1,9},{2,10},{3,11},{4,12},{5,13},{6,14},{7,15},{8,0},{9,1},... | collective-permute-start | bytes 1772552 | tf_op jit(solution)/shard_map/ppermute | solution.py:681
  474.3 25.6 %collective-permute-start.20 = (bf16[577,512]{1,0:T(8,128)(2,1)S(1)}, bf16[577,512]{1,0:T(8,128)(2,1)S(1)}, u32[]{:S(2)}, u32[]{:S(2)}) collective-permute-start(bf16[577,512]{1,0:T(8,128)(2,1)S(1)} %add_convert_fusion.13), channel_id=1, source_target_pairs={{0,8},{1,9},{2,10},{3,11},{4,12},{5,13},{6,14},{7,15},{8,0},{9,1},... | collective-permute-start | bytes 1772552 | tf_op jit(solution)/shard_map/ppermute | solution.py:681
  477.2 24.1 %collective-permute-start.1 = (bf16[608,512]{1,0:T(8,128)(2,1)S(1)}, bf16[608,512]{1,0:T(8,128)(2,1)S(1)}, u32[]{:S(2)}, u32[]{:S(2)}) collective-permute-start(bf16[608,512]{1,0:T(8,128)(2,1)S(1)} %get-tuple-element.223), channel_id=1, source_target_pairs={{0,4},{1,5},{2,6},{3,7},{4,0},{5,1},{6,2},{7,3},{8,12},{9,13},{10,... | collective-permute-start | bytes 1867784 | tf_op jit(solution)/shard_map/ppermute | solution.py:681
  479.5 22.0 %collective-permute-start.3 = (bf16[608,512]{1,0:T(8,128)(2,1)S(1)}, bf16[608,512]{1,0:T(8,128)(2,1)S(1)}, u32[]{:S(2)}, u32[]{:S(2)}) collective-permute-start(bf16[608,512]{1,0:T(8,128)(2,1)S(1)} %get-tuple-element.224), channel_id=1, source_target_pairs={{0,4},{1,5},{2,6},{3,7},{4,0},{5,1},{6,2},{7,3},{8,12},{9,13},{10,... | collective-permute-start | bytes 1867784 | tf_op jit(solution)/shard_map/ppermute | solution.py:681
  487.2 19.7 %collective-permute-start.9 = (bf16[577,512]{1,0:T(8,128)(2,1)S(1)}, bf16[577,512]{1,0:T(8,128)(2,1)S(1)}, u32[]{:S(2)}, u32[]{:S(2)}) collective-permute-start(bf16[577,512]{1,0:T(8,128)(2,1)S(1)} %add_convert_fusion.20), channel_id=1, source_target_pairs={{0,4},{1,5},{2,6},{3,7},{4,0},{5,1},{6,2},{7,3},{8,12},{9,13},{10,... | collective-permute-start | bytes 1772552 | tf_op jit(solution)/shard_map/ppermute | solution.py:681
  504.3 93.4 %collective-permute-start.4 = (bf16[577,1024]{1,0:T(8,128)(2,1)}, bf16[577,1024]{1,0:T(8,128)(2,1)}, u32[]{:S(2)}, u32[]{:S(2)}) collective-permute-start(bf16[577,1024]{1,0:T(8,128)(2,1)} %fusion.388), channel_id=1, source_target_pairs={{0,1},{2,3},{5,4},{7,6},{8,9},{10,11},{13,12},{15,14},{16,17},{18,... | collective-permute-start | bytes 3545096 | tf_op jit(solution)/shard_map/ppermute | solution.py:684
  505.6 94.0 %collective-permute-start.5 = (bf16[577,1024]{1,0:T(8,128)(2,1)}, bf16[577,1024]{1,0:T(8,128)(2,1)}, u32[]{:S(2)}, u32[]{:S(2)}) collective-permute-start(bf16[577,1024]{1,0:T(8,128)(2,1)} %fusion.388), channel_id=1, source_target_pairs={{0,3},{2,1},{5,6},{7,4},{8,11},{10,9},{13,14},{15,12},{16,19},{18,... | collective-permute-start | bytes 3545096 | tf_op jit(solution)/shard_map/ppermute | solution.py:684
  506.9 93.6 %collective-permute-start.6 = (bf16[577,1024]{1,0:T(8,128)(2,1)}, bf16[577,1024]{1,0:T(8,128)(2,1)}, u32[]{:S(2)}, u32[]{:S(2)}) collective-permute-start(bf16[577,1024]{1,0:T(8,128)(2,1)} %fusion.388), channel_id=1, source_target_pairs={{0,2},{2,0},{5,7},{7,5},{8,10},{10,8},{13,15},{15,13},{16,18},{18,... | collective-permute-start | bytes 3545096 | tf_op jit(solution)/shard_map/ppermute | solution.py:684
  560.1 32.7 %collective-permute-start.10 = (bf16[577,512]{1,0:T(8,128)(2,1)}, bf16[577,512]{1,0:T(8,128)(2,1)}, u32[]{:S(2)}, u32[]{:S(2)}) collective-permute-start(bf16[577,512]{1,0:T(8,128)(2,1)} %broadcast_select_fusion.28), channel_id=1, source_target_pairs={{0,4},{1,5},{2,6},{3,7},{4,0},{5,1},{6,2},{7,3},{8,12},{9,13},{10,... | collective-permute-start | bytes 1772552 | tf_op jit(solution)/shard_map/ppermute | solution.py:681
  592.8 21.9 %collective-permute-start.56 = (bf16[2,256,512]{2,1,0:T(8,128)(2,1)S(1)}, bf16[2,256,512]{2,1,0:T(8,128)(2,1)S(1)}, u32[]{:S(2)}, u32[]{:S(2)}) collective-permute-start(bf16[2,256,512]{2,1,0:T(8,128)(2,1)S(1)} %get-tuple-element.181), channel_id=1, source_target_pairs={{0,1},{1,0},{2,3},{3,2},{4,5},{5,4},{6,7},{7,6},{8,9},{9,8},{10,11... | collective-permute-start | bytes 1572872 | tf_op jit(solution)/shard_map/ppermute | solution.py:684
  596.0 36.4 %collective-permute-start.57 = (bf16[2,256,512]{2,1,0:T(8,128)(2,1)S(1)}, bf16[2,256,512]{2,1,0:T(8,128)(2,1)S(1)}, u32[]{:S(2)}, u32[]{:S(2)}) collective-permute-start(bf16[2,256,512]{2,1,0:T(8,128)(2,1)S(1)} %get-tuple-element.183), channel_id=1, source_target_pairs={{0,2},{1,3},{2,0},{3,1},{4,6},{5,7},{6,4},{7,5},{8,10},{9,11},{10,... | collective-permute-start | bytes 1572872 | tf_op jit(solution)/shard_map/ppermute | solution.py:684
  597.7 34.7 %collective-permute-start.58 = (bf16[2,256,512]{2,1,0:T(8,128)(2,1)S(1)}, bf16[2,256,512]{2,1,0:T(8,128)(2,1)S(1)}, u32[]{:S(2)}, u32[]{:S(2)}) collective-permute-start(bf16[2,256,512]{2,1,0:T(8,128)(2,1)S(1)} %get-tuple-element.182), channel_id=1, source_target_pairs={{0,3},{1,2},{2,1},{3,0},{4,7},{5,6},{6,5},{7,4},{8,11},{9,10},{10,... | collective-permute-start | bytes 1572872 | tf_op jit(solution)/shard_map/ppermute | solution.py:684
  599.6 51.7 %collective-permute-start.41 = (bf16[4,4,64,512]{3,2,1,0:T(8,128)(2,1)}, bf16[4,4,64,512]{3,2,1,0:T(8,128)(2,1)}, u32[]{:S(2)}, u32[]{:S(2)}) collective-permute-start(bf16[4,4,64,512]{3,2,1,0:T(8,128)(2,1)} %fusion.481), channel_id=1, source_target_pairs={{0,16},{1,17},{2,18},{3,19},{4,20},{5,21},{6,22},{7,23},{8,24},{9,... | collective-permute-start | bytes 3145736 | tf_op jit(solution)/shard_map/ppermute | solution.py:687
  600.5 65.4 %collective-permute-start.11 = (bf16[577,512]{1,0:T(8,128)(2,1)}, bf16[577,512]{1,0:T(8,128)(2,1)}, u32[]{:S(2)}, u32[]{:S(2)}) collective-permute-start(bf16[577,512]{1,0:T(8,128)(2,1)} %add_convert_fusion.19), channel_id=1, source_target_pairs={{0,8},{1,9},{2,10},{3,11},{4,12},{5,13},{6,14},{7,15},{8,0},{9,1},... | collective-permute-start | bytes 1772552 | tf_op jit(solution)/shard_map/ppermute | solution.py:681
  638.3 10.4 collective-permute-start.59
  648.7 41.5 %collective-permute-start.23 = (bf16[577,512]{1,0:T(8,128)(2,1)}, bf16[577,512]{1,0:T(8,128)(2,1)}, u32[]{:S(2)}, u32[]{:S(2)}) collective-permute-start(bf16[577,512]{1,0:T(8,128)(2,1)} %add_convert_fusion.11), channel_id=1, source_target_pairs={{0,8},{1,9},{2,10},{3,11},{4,12},{5,13},{6,14},{7,15},{8,0},{9,1},... | collective-permute-start | bytes 1772552 | tf_op jit(solution)/shard_map/ppermute | solution.py:681
  653.1 20.9 %collective-permute-start.42 = (bf16[4,64,512]{2,1,0:T(8,128)(2,1)S(1)}, bf16[4,64,512]{2,1,0:T(8,128)(2,1)S(1)}, u32[]{:S(2)}, u32[]{:S(2)}) collective-permute-start(bf16[4,64,512]{2,1,0:T(8,128)(2,1)S(1)} %get-tuple-element.206), channel_id=1, source_target_pairs={{0,1},{1,0},{2,3},{3,2},{4,5},{5,4},{6,7},{7,6},{8,9},{9,8},{10,11... | collective-permute-start | bytes 786440 | tf_op jit(solution)/shard_map/ppermute | solution.py:684
  663.7 10.5 collective-permute-start.43
  663.9 18.0 %collective-permute-start.44 = (bf16[4,64,512]{2,1,0:T(8,128)(2,1)S(1)}, bf16[4,64,512]{2,1,0:T(8,128)(2,1)S(1)}, u32[]{:S(2)}, u32[]{:S(2)}) collective-permute-start(bf16[4,64,512]{2,1,0:T(8,128)(2,1)S(1)} %get-tuple-element.207), channel_id=1, source_target_pairs={{0,3},{1,2},{2,1},{3,0},{4,7},{5,6},{6,5},{7,4},{8,11},{9,10},{10,... | collective-permute-start | bytes 786440 | tf_op jit(solution)/shard_map/ppermute | solution.py:684
  668.1 26.6 %collective-permute-start.12 = (bf16[577,512]{1,0:T(8,128)(2,1)}, bf16[577,512]{1,0:T(8,128)(2,1)}, u32[]{:S(2)}, u32[]{:S(2)}) collective-permute-start(bf16[577,512]{1,0:T(8,128)(2,1)} %add_convert_fusion.18), channel_id=1, source_target_pairs={{0,4},{1,5},{2,6},{3,7},{4,0},{5,1},{6,2},{7,3},{8,12},{9,13},{10,... | collective-permute-start | bytes 1772552 | tf_op jit(solution)/shard_map/ppermute | solution.py:681
  726.9 28.5 %collective-permute-start.25 = (bf16[577,512]{1,0:T(8,128)(2,1)}, bf16[577,512]{1,0:T(8,128)(2,1)S(1)}, u32[]{:S(2)}, u32[]{:S(2)}) collective-permute-start(bf16[577,512]{1,0:T(8,128)(2,1)} %broadcast_select_fusion.13), channel_id=1, source_target_pairs={{0,4},{1,5},{2,6},{3,7},{4,0},{5,1},{6,2},{7,3},{8,12},{9,13},{10,... | collective-permute-start | bytes 1772552 | tf_op jit(solution)/shard_map/ppermute | solution.py:681
  737.8 18.5 %collective-permute-start.13 = (bf16[577,512]{1,0:T(8,128)(2,1)}, bf16[577,512]{1,0:T(8,128)(2,1)}, u32[]{:S(2)}, u32[]{:S(2)}) collective-permute-start(bf16[577,512]{1,0:T(8,128)(2,1)} %broadcast_select_fusion.25), channel_id=1, source_target_pairs={{0,4},{1,5},{2,6},{3,7},{4,0},{5,1},{6,2},{7,3},{8,12},{9,13},{10,... | collective-permute-start | bytes 1772552 | tf_op jit(solution)/shard_map/ppermute | solution.py:681
  755.6 14.8 %collective-permute-start.26 = (bf16[577,512]{1,0:T(8,128)(2,1)S(1)}, bf16[577,512]{1,0:T(8,128)(2,1)S(1)}, u32[]{:S(2)}, u32[]{:S(2)}) collective-permute-start(bf16[577,512]{1,0:T(8,128)(2,1)S(1)} %add_convert_fusion.9), channel_id=1, source_target_pairs={{0,8},{1,9},{2,10},{3,11},{4,12},{5,13},{6,14},{7,15},{8,0},{9,1},... | collective-permute-start | bytes 1772552 | tf_op jit(solution)/shard_map/ppermute | solution.py:681
  757.9 25.3 %collective-permute-start.14 = (bf16[577,512]{1,0:T(8,128)(2,1)S(1)}, bf16[577,512]{1,0:T(8,128)(2,1)S(1)}, u32[]{:S(2)}, u32[]{:S(2)}) collective-permute-start(bf16[577,512]{1,0:T(8,128)(2,1)S(1)} %add_convert_fusion.17), channel_id=1, source_target_pairs={{0,8},{1,9},{2,10},{3,11},{4,12},{5,13},{6,14},{7,15},{8,0},{9,1},... | collective-permute-start | bytes 1772552 | tf_op jit(solution)/shard_map/ppermute | solution.py:681
  770.5 26.6 %collective-permute-start.27 = (bf16[577,512]{1,0:T(8,128)(2,1)S(1)}, bf16[577,512]{1,0:T(8,128)(2,1)}, u32[]{:S(2)}, u32[]{:S(2)}) collective-permute-start(bf16[577,512]{1,0:T(8,128)(2,1)S(1)} %add_convert_fusion.8), channel_id=1, source_target_pairs={{0,4},{1,5},{2,6},{3,7},{4,0},{5,1},{6,2},{7,3},{8,12},{9,13},{10,... | collective-permute-start | bytes 1772552 | tf_op jit(solution)/shard_map/ppermute | solution.py:681
  784.1 14.2 %collective-permute-start.15 = (bf16[577,512]{1,0:T(8,128)(2,1)}, bf16[577,512]{1,0:T(8,128)(2,1)}, u32[]{:S(2)}, u32[]{:S(2)}) collective-permute-start(bf16[577,512]{1,0:T(8,128)(2,1)} %add_convert_fusion.16), channel_id=1, source_target_pairs={{0,4},{1,5},{2,6},{3,7},{4,0},{5,1},{6,2},{7,3},{8,12},{9,13},{10,... | collective-permute-start | bytes 1772552 | tf_op jit(solution)/shard_map/ppermute | solution.py:681
  796.4 74.2 %collective-permute-start.48 = (bf16[2,4,256,512]{3,2,1,0:T(8,128)(2,1)}, bf16[2,4,256,512]{3,2,1,0:T(8,128)(2,1)}, u32[]{:S(2)}, u32[]{:S(2)}) collective-permute-start(bf16[2,4,256,512]{3,2,1,0:T(8,128)(2,1)} %fusion.390), channel_id=1, source_target_pairs={{0,16},{1,17},{2,18},{3,19},{4,20},{5,21},{6,22},{7,23},{8,24},{9,... | collective-permute-start | bytes 6291464 | tf_op jit(solution)/shard_map/ppermute | solution.py:687
  845.1 40.2 %collective-permute-start.16 = (bf16[577,512]{1,0:T(8,128)(2,1)}, bf16[577,512]{1,0:T(8,128)(2,1)}, u32[]{:S(2)}, u32[]{:S(2)}) collective-permute-start(bf16[577,512]{1,0:T(8,128)(2,1)} %broadcast_select_fusion.22), channel_id=1, source_target_pairs={{0,4},{1,5},{2,6},{3,7},{4,0},{5,1},{6,2},{7,3},{8,12},{9,13},{10,... | collective-permute-start | bytes 1772552 | tf_op jit(solution)/shard_map/ppermute | solution.py:681
  847.8 75.4 %collective-permute-start.28 = (bf16[577,512]{1,0:T(8,128)(2,1)}, bf16[577,512]{1,0:T(8,128)(2,1)}, u32[]{:S(2)}, u32[]{:S(2)}) collective-permute-start(bf16[577,512]{1,0:T(8,128)(2,1)} %broadcast_select_fusion.10), channel_id=1, source_target_pairs={{0,4},{1,5},{2,6},{3,7},{4,0},{5,1},{6,2},{7,3},{8,12},{9,13},{10,... | collective-permute-start | bytes 1772552 | tf_op jit(solution)/shard_map/ppermute | solution.py:681
  875.3 26.9 %collective-permute-start.49 = (bf16[2,256,512]{2,1,0:T(8,128)(2,1)S(1)}, bf16[2,256,512]{2,1,0:T(8,128)(2,1)S(1)}, u32[]{:S(2)}, u32[]{:S(2)}) collective-permute-start(bf16[2,256,512]{2,1,0:T(8,128)(2,1)S(1)} %get-tuple-element.178), channel_id=1, source_target_pairs={{0,1},{1,0},{2,3},{3,2},{4,5},{5,4},{6,7},{7,6},{8,9},{9,8},{10,11... | collective-permute-start | bytes 1572872 | tf_op jit(solution)/shard_map/ppermute | solution.py:684
  879.7 36.5 %collective-permute-start.50 = (bf16[2,256,512]{2,1,0:T(8,128)(2,1)S(1)}, bf16[2,256,512]{2,1,0:T(8,128)(2,1)}, u32[]{:S(2)}, u32[]{:S(2)}) collective-permute-start(bf16[2,256,512]{2,1,0:T(8,128)(2,1)S(1)} %get-tuple-element.180), channel_id=1, source_target_pairs={{0,2},{1,3},{2,0},{3,1},{4,6},{5,7},{6,4},{7,5},{8,10},{9,11},{10,... | collective-permute-start | bytes 1572872 | tf_op jit(solution)/shard_map/ppermute | solution.py:684
  879.9 36.3 %collective-permute-start.51 = (bf16[2,256,512]{2,1,0:T(8,128)(2,1)S(1)}, bf16[2,256,512]{2,1,0:T(8,128)(2,1)}, u32[]{:S(2)}, u32[]{:S(2)}) collective-permute-start(bf16[2,256,512]{2,1,0:T(8,128)(2,1)S(1)} %get-tuple-element.179), channel_id=1, source_target_pairs={{0,3},{1,2},{2,1},{3,0},{4,7},{5,6},{6,5},{7,4},{8,11},{9,10},{10,... | collective-permute-start | bytes 1572872 | tf_op jit(solution)/shard_map/ppermute | solution.py:684
  885.2 47.3 %collective-permute-start.34 = (bf16[4,4,64,512]{3,2,1,0:T(8,128)(2,1)}, bf16[4,4,64,512]{3,2,1,0:T(8,128)(2,1)}, u32[]{:S(2)}, u32[]{:S(2)}) collective-permute-start(bf16[4,4,64,512]{3,2,1,0:T(8,128)(2,1)} %fusion.480), channel_id=1, source_target_pairs={{0,16},{1,17},{2,18},{3,19},{4,20},{5,21},{6,22},{7,23},{8,24},{9,... | collective-permute-start | bytes 3145736 | tf_op jit(solution)/shard_map/ppermute | solution.py:687
  902.2 45.6 %collective-permute-start.17 = (bf16[577,512]{1,0:T(8,128)(2,1)}, bf16[577,512]{1,0:T(8,128)(2,1)}, u32[]{:S(2)}, u32[]{:S(2)}) collective-permute-start(bf16[577,512]{1,0:T(8,128)(2,1)} %add_convert_fusion.15), channel_id=1, source_target_pairs={{0,8},{1,9},{2,10},{3,11},{4,12},{5,13},{6,14},{7,15},{8,0},{9,1},... | collective-permute-start | bytes 1772552 | tf_op jit(solution)/shard_map/ppermute | solution.py:681
  926.8 43.2 %collective-permute-start.29 = (bf16[577,512]{1,0:T(8,128)(2,1)S(1)}, bf16[577,512]{1,0:T(8,128)(2,1)S(1)}, u32[]{:S(2)}, u32[]{:S(2)}) collective-permute-start(bf16[577,512]{1,0:T(8,128)(2,1)S(1)} %add_convert_fusion.7), channel_id=1, source_target_pairs={{0,8},{1,9},{2,10},{3,11},{4,12},{5,13},{6,14},{7,15},{8,0},{9,1},... | collective-permute-start | bytes 1772552 | tf_op jit(solution)/shard_map/ppermute | solution.py:681
  935.0 21.2 %collective-permute-start.35 = (bf16[4,64,512]{2,1,0:T(8,128)(2,1)S(1)}, bf16[4,64,512]{2,1,0:T(8,128)(2,1)S(1)}, u32[]{:S(2)}, u32[]{:S(2)}) collective-permute-start(bf16[4,64,512]{2,1,0:T(8,128)(2,1)S(1)} %get-tuple-element.203), channel_id=1, source_target_pairs={{0,1},{1,0},{2,3},{3,2},{4,5},{5,4},{6,7},{7,6},{8,9},{9,8},{10,11... | collective-permute-start | bytes 786440 | tf_op jit(solution)/shard_map/ppermute | solution.py:684
  945.6 19.4 %collective-permute-start.36 = (bf16[4,64,512]{2,1,0:T(8,128)(2,1)S(1)}, bf16[4,64,512]{2,1,0:T(8,128)(2,1)S(1)}, u32[]{:S(2)}, u32[]{:S(2)}) collective-permute-start(bf16[4,64,512]{2,1,0:T(8,128)(2,1)S(1)} %get-tuple-element.205), channel_id=1, source_target_pairs={{0,2},{1,3},{2,0},{3,1},{4,6},{5,7},{6,4},{7,5},{8,10},{9,11},{10,... | collective-permute-start | bytes 786440 | tf_op jit(solution)/shard_map/ppermute | solution.py:684
  945.6 19.4 %collective-permute-start.37 = (bf16[4,64,512]{2,1,0:T(8,128)(2,1)S(1)}, bf16[4,64,512]{2,1,0:T(8,128)(2,1)S(1)}, u32[]{:S(2)}, u32[]{:S(2)}) collective-permute-start(bf16[4,64,512]{2,1,0:T(8,128)(2,1)S(1)} %get-tuple-element.204), channel_id=1, source_target_pairs={{0,3},{1,2},{2,1},{3,0},{4,7},{5,6},{6,5},{7,4},{8,11},{9,10},{10,... | collective-permute-start | bytes 786440 | tf_op jit(solution)/shard_map/ppermute | solution.py:684
  949.2 24.1 %collective-permute-start.18 = (bf16[577,512]{1,0:T(8,128)(2,1)S(1)}, bf16[577,512]{1,0:T(8,128)(2,1)}, u32[]{:S(2)}, u32[]{:S(2)}) collective-permute-start(bf16[577,512]{1,0:T(8,128)(2,1)S(1)} %add_convert_fusion.14), channel_id=1, source_target_pairs={{0,4},{1,5},{2,6},{3,7},{4,0},{5,1},{6,2},{7,3},{8,12},{9,13},{10,... | collective-permute-start | bytes 1772552 | tf_op jit(solution)/shard_map/ppermute | solution.py:681
  982.4 162.2 %collective-permute-start.31 = (bf16[577,1024]{1,0:T(8,128)(2,1)S(1)}, bf16[577,1024]{1,0:T(8,128)(2,1)}, u32[]{:S(2)}, u32[]{:S(2)}) collective-permute-start(bf16[577,1024]{1,0:T(8,128)(2,1)S(1)} %get-tuple-element.231), channel_id=1, source_target_pairs={{0,1},{2,3},{5,4},{7,6},{8,9},{10,11},{13,12},{15,14},{16,17},{18,... | collective-permute-start | bytes 3545096 | tf_op jit(solution)/shard_map/ppermute | solution.py:684
  983.7 161.0 %collective-permute-start.32 = (bf16[577,1024]{1,0:T(8,128)(2,1)S(1)}, bf16[577,1024]{1,0:T(8,128)(2,1)}, u32[]{:S(2)}, u32[]{:S(2)}) collective-permute-start(bf16[577,1024]{1,0:T(8,128)(2,1)S(1)} %get-tuple-element.231), channel_id=1, source_target_pairs={{0,3},{2,1},{5,6},{7,4},{8,11},{10,9},{13,14},{15,12},{16,19},{18,... | collective-permute-start | bytes 3545096 | tf_op jit(solution)/shard_map/ppermute | solution.py:684
  985.0 159.7 %collective-permute-start.33 = (bf16[577,1024]{1,0:T(8,128)(2,1)S(1)}, bf16[577,1024]{1,0:T(8,128)(2,1)}, u32[]{:S(2)}, u32[]{:S(2)}) collective-permute-start(bf16[577,1024]{1,0:T(8,128)(2,1)S(1)} %get-tuple-element.231), channel_id=1, source_target_pairs={{0,2},{2,0},{5,7},{7,5},{8,10},{10,8},{13,15},{15,13},{16,18},{18,... | collective-permute-start | bytes 3545096 | tf_op jit(solution)/shard_map/ppermute | solution.py:684
  (212 other events, 926.3 us)
Sparse Core Ops, SparseCore 0:
  988.6 150.4 all-reduce.7

commit v3 on v2

--- a/solution.py
+++ b/solution.py
@@ -642,16 +642,651 @@
     )(own_image, own_cot, packed, extras)
 
 
-def product(left, right, form):
-    return jnp.einsum(form, left, right, preferred_element_type=jnp.float32)
-
-
-def low(v):
-    return v.astype(jnp.bfloat16)
-
-
-def wide(v):
-    return v.astype(jnp.float32)
+class Scatter:
+    def __init__(self, spot, term, block_in, total, plane_in, mine, out, block_sems, plane_sems, role_sems, local_sem, block_free, plane_free, direct):
+        self.spot, self.direct = spot, direct
+        self.term, self.block_in, self.total = term, block_in, total
+        self.plane_in, self.mine, self.out = plane_in, mine, out
+        self.block_sems, self.plane_sems, self.role_sems, self.local_sem = block_sems, plane_sems, role_sems, local_sem
+        self.block_free, self.plane_free = block_free, plane_free
+        self.span = D // spot.blocks
+        self.cols = self.span // TP
+
+    def to_block(self, k, s):
+        block = (self.spot.block + s) % self.spot.blocks
+        return send(
+            self.term.at[k, :, :, lanes(block * self.span, self.span)],
+            self.block_in.at[k, s - 1],
+            self.block_sems, (k, s - 1), self.spot.at(block=block),
+        )
+
+    def to_plane(self, k, o):
+        other = flip(self.spot.plane, o)
+        return send(
+            self.total.at[k, other], self.plane_in.at[k, o - 1],
+            self.plane_sems, (k, o - 1), self.spot.at(plane=other),
+        )
+
+    def to_role(self, g, k, o):
+        other = flip(self.spot.role, o)
+        return send(
+            self.mine.at[k, :, lanes(other * self.cols, self.cols)], self.out.at[g, self.spot.role],
+            self.role_sems, (g, o), self.spot.at(role=other),
+        )
+
+    def from_role(self, g, k, o):
+        other = flip(self.spot.role, o)
+        place = self.out.at[g, other]
+        return send(place, place, self.role_sems, (g, o), self.spot.at(role=other))
+
+    def keep(self, g, k):
+        if self.direct:
+            return pltpu.make_async_copy(
+                self.mine.at[k, :, lanes(self.spot.role * self.cols, self.cols)],
+                self.out.at[g, self.spot.role], self.local_sem.at[g],
+            )
+        return pltpu.make_async_copy(self.mine.at[k], self.out.at[g], self.local_sem.at[g])
+
+    def send_terms(self, k, again):
+        for s in range(1, self.spot.blocks):
+            @pl.when(again)
+            def _():
+                pl.semaphore_wait(self.block_free.at[k, s - 1], 1)
+
+            self.to_block(k, s).start()
+
+    def before_terms(self, k, again):
+        @pl.when(again)
+        def _():
+            for s in range(1, self.spot.blocks):
+                self.to_block(k, s).wait_send()
+
+    def sum_blocks(self, k, again, more):
+        for s in range(1, self.spot.blocks):
+            self.to_block(k, s).wait_recv()
+
+        @pl.when(again)
+        def _():
+            for o in (1, 2, 3):
+                self.to_plane(k, o).wait_send()
+
+        units = self.term.shape[2]
+        own = lanes(self.spot.block * self.span, self.span)
+        for plane in range(4):
+            def step(r):
+                value = self.term[k, plane, r, own].astype(f32)
+                for s in range(1, self.spot.blocks):
+                    value = value + self.block_in[k, s - 1, plane, r].astype(f32)
+                self.total[k, plane, r] = value.astype(bf16)
+
+            each_rows(units, 16, step, unroll=2)
+
+        @pl.when(more)
+        def _():
+            for s in range(1, self.spot.blocks):
+                source = (self.spot.block + self.spot.blocks - s) % self.spot.blocks
+                pl.semaphore_signal(
+                    self.block_free.at[k, s - 1], inc=1, device_id=self.spot.at(block=source), device_id_type=MESH
+                )
+
+        for o in (1, 2, 3):
+            @pl.when(again)
+            def _():
+                pl.semaphore_wait(self.plane_free.at[k, o - 1], 1)
+
+            self.to_plane(k, o).start()
+
+    def sum_planes(self, g, k, again, more):
+        for o in (1, 2, 3):
+            self.to_plane(k, o).wait_recv()
+        units = self.term.shape[2]
+
+        @pl.when(again)
+        def _():
+            before = jnp.minimum(g + 3, self.out.shape[0] - 1)
+            self.keep(before, k).wait()
+            if self.direct:
+                for o in (1, 2, 3):
+                    self.to_role(before, k, o).wait_send()
+
+        def step(r):
+            value = self.total[k, self.spot.plane, r].astype(f32)
+            for o in (1, 2, 3):
+                value = value + self.plane_in[k, o - 1, r].astype(f32)
+            self.mine[k, r] = value.astype(bf16)
+
+        each_rows(units, 16, step, unroll=2)
+
+        @pl.when(more)
+        def _():
+            for o in (1, 2, 3):
+                pl.semaphore_signal(
+                    self.plane_free.at[k, o - 1], inc=1,
+                    device_id=self.spot.at(plane=flip(self.spot.plane, o)), device_id_type=MESH,
+                )
+
+        self.keep(g, k).start()
+        if self.direct:
+            for o in (1, 2, 3):
+                self.to_role(g, k, o).start()
+
+    def finish(self, g, k):
+        self.keep(g, k).wait()
+        for s in range(1, self.spot.blocks):
+            self.to_block(k, s).wait_send()
+        for o in (1, 2, 3):
+            self.to_plane(k, o).wait_send()
+            if self.direct:
+                self.to_role(g, k, o).wait_send()
+
+    def arrive(self, g, k):
+        if self.direct:
+            for o in (1, 2, 3):
+                self.from_role(g, k, o).wait_recv()
+
+
+def backward_kernel(cfg, *refs):
+    fsdp, head, tokens, rows, direct = cfg
+    (
+        weights_in, vec_in, normed_in, unit_in, inverse_in, qkv_in, att_in, lse_in, hidden_in,
+        stream_in, chip_in, cot_in,
+        out_pair, in_pair, grads, small_grads,
+        weight, vec, up, up_low, hid, gh, normed, unit, inverse, qkv, att, lse, big, soft, low_scores, gab, along,
+        kept, sent, core_in, chip, side_in, full, last_in, result, sums, unit_sums,
+        term, block_in, total, plane_in, mine,
+        small_term, small_block_in, small_total, small_plane_in, small_mine,
+        core_s, core_r, side_s, side_r, back_s, back_r,
+        block_s, block_r, plane_s, plane_r, role_s, role_r, local_sem, block_free, plane_free,
+        small_block_s, small_block_r, small_plane_s, small_plane_r, small_role_s, small_role_r, small_local,
+        small_block_free, small_plane_free,
+        last_s, last_r, out_s, out_r, load_sem, weight_sem,
+    ) = refs
+    spot = Spot(fsdp, head)
+    greet(spot.partners())
+    exchange = Exchange(
+        spot, sent, core_in, chip, side_in, full, (core_s, core_r), (side_s, side_r), (back_s, back_r)
+    )
+    scatter = Scatter(
+        spot, term, block_in, total, plane_in, mine, grads, (block_s, block_r), (plane_s, plane_r),
+        (role_s, role_r), local_sem, block_free, plane_free, direct,
+    )
+    small = Scatter(
+        spot, small_term, small_block_in, small_total, small_plane_in, small_mine, small_grads,
+        (small_block_s, small_block_r), (small_plane_s, small_plane_r), (small_role_s, small_role_r),
+        small_local, small_block_free, small_plane_free, direct,
+    )
+    owner = spot.core == spot.plane % 2
+    top = LAYERS - 1
+
+    def load(source, target, n):
+        return pltpu.make_async_copy(source, target, load_sem.at[n])
+
+    def load_weight(l, k):
+        return pltpu.make_async_copy(weights_in.at[3 * l + k], weight.at[k], weight_sem.at[k])
+
+    load_vec = load(vec_in, vec, 0)
+    load_cot = load(cot_in, up_low, 1)
+    last_chip = qkv.at[:, :, 0:HALF]
+    load_chip = load(chip_in, last_chip, 2)
+
+    def load_hidden(l):
+        return load(hidden_in.at[l], hid, 4)
+
+    def load_normed(l, n):
+        return load(normed_in.at[l, n], normed, 5)
+
+    def load_unit(l, n):
+        return [load(unit_in.at[l, n], unit, 6), load(inverse_in.at[l, n], inverse, 7)]
+
+    def load_attn(l):
+        return [load(qkv_in.at[l], qkv, 8), load(att_in.at[l], att, 9), load(lse_in.at[l], lse, 10)]
+
+    load_chip.start()
+    load_cot.start()
+    load_weight(top, 2).start()
+    load_hidden(top).start()
+    load_vec.start()
+    load_weight(top, 1).start()
+    load_weight(top, 0).start()
+    load_normed(top, 1).start()
+    for copy in load_unit(top, 1):
+        copy.start()
+
+    last_copy = send(
+        last_chip.at[1 - spot.side], last_in, (last_s, last_r), (0,), spot.at(role=flip2(spot.role))
+    )
+    half_copy = send(
+        result.at[:, exchange.mine], result.at[:, exchange.mine], (last_s, last_r), (1,),
+        spot.at(role=flip1(spot.role)),
+    )
+    half_in = send(
+        result.at[:, exchange.theirs], result.at[:, exchange.theirs], (last_s, last_r), (1,),
+        spot.at(role=flip1(spot.role)),
+    )
+    load_chip.wait()
+    last_copy.start()
+
+    sums[...] = jnp.zeros_like(sums)
+    unit_sums[...] = jnp.zeros_like(unit_sums)
+    load_cot.wait()
+
+    def eights(v):
+        return v[0:8] + v[8:16]
+
+    for i in range(2):
+        def widen(r):
+            v = up_low[i, r].astype(f32)
+            up[i, r] = v
+            sums[(top + 1) * 6 + 5] += eights(v)
+
+        each_rows(rows, 16, widen, unroll=2)
+    load_vec.wait()
+
+    def return_copies(n, pair_out):
+        slot = spot.plane // 2
+        source = result if n == 0 else up_low.at[spot.side]
+        mine_copy = pltpu.make_async_copy(source, pair_out.at[slot], load_sem.at[12 + n])
+        outs = [
+            send(
+                source, pair_out.at[slot], (out_s, out_r), (n, o), spot.at(plane=flip(spot.plane, o))
+            )
+            for o in (1, 2, 3)
+        ]
+        return mine_copy, outs
+
+    def return_begin(n, pair_out):
+        @pl.when(owner)
+        def _():
+            mine_copy, outs = return_copies(n, pair_out)
+            mine_copy.start()
+            for copy in outs:
+                copy.start()
+
+    def return_end(n, pair_out):
+        for o in (1, 2, 3):
+            other = flip(spot.plane, o)
+
+            @pl.when(spot.core == other % 2)
+            def _():
+                place = pair_out.at[other // 2]
+                send(place, place, (out_s, out_r), (n, o), spot.at(plane=other)).wait_recv()
+
+        @pl.when(owner)
+        def _():
+            mine_copy, outs = return_copies(n, pair_out)
+            mine_copy.wait()
+            for copy in outs:
+                copy.wait_send()
+
+    def norm_back(l, n, i):
+        def step(r):
+            g = full[i, r].astype(f32)
+            u = unit[i, r].astype(f32)
+            scaled = g * vec[l, n : n + 1]
+            first = jnp.mean(scaled, axis=-1, keepdims=True)
+            second = jnp.mean(scaled * u, axis=-1, keepdims=True)
+            scale = inverse[i, r, 0:1]
+            v = up[i, r] + scale * (scaled - first - u * second)
+            up[i, r] = v
+            up_low[i, r] = v.astype(bf16)
+            base = (l + 1) * 6
+            sums[base + n] += eights(g * u)
+            sums[base + 2 + n] += eights(g)
+            sums[base + 4 if n == 1 else base - 1] += eights(v)
+
+        each_rows(rows, 16, step, unroll=2)
+
+    def mlp_stage(l, i):
+        @pl.when(l < top)
+        def _():
+            exchange.finish(i, 1)
+            norm_back(jnp.minimum(l + 1, top), 0, i)
+
+        @pl.when(i == 0)
+        def _():
+            load_hidden(l).wait()
+            load_weight(l, 2).wait()
+
+        big[:, 0:D] = dot(up_low[i], weight[2].reshape(D, D), 1, 1)
+
+        def step(r):
+            v = hid[i, r].astype(f32)
+            below = 0.5 + 0.5 * lax.erf(v * (0.5**0.5))
+            slope = below + v * jnp.exp(-0.5 * v * v) * (1.0 / math.sqrt(2.0 * math.pi))
+            hid[i, r] = (v * below).astype(bf16)
+            low_grad = (big[r, 0:D] * slope).astype(bf16)
+            gh[i, r] = low_grad
+            unit_sums[l, 0] += eights(low_grad.astype(f32))
+
+        each_rows(rows, 16, step, unroll=2)
+
+        @pl.when(i == 0)
+        def _():
+            load_weight(l, 1).wait()
+
+        exchange.reduce(i, lambda at: dot(gh[i], weight[1, :, :, at].reshape(D, HALF), 1, 0), kept)
+        exchange.side_copy(i, 0).start()
+
+    lane_head = lax.broadcasted_iota(jnp.int32, (1, 256), 1) // HD
+    head_rows = jnp.where(
+        lax.broadcasted_iota(jnp.int32, (16, 256), 1) // HD == lax.broadcasted_iota(jnp.int32, (16, 256), 0), 1.0, 0.0
+    ).astype(bf16)
+
+    def attn_stage(l, i):
+        exchange.finish(i, 0)
+
+        @pl.when(i == 0)
+        def _():
+            for copy in load_unit(l, 1):
+                copy.wait()
+
+        norm_back(l, 1, i)
+
+        @pl.when(i == 0)
+        def _():
+            load_weight(l, 0).wait()
+            for copy in load_attn(l):
+                copy.wait()
+
+        gab[...] = dot(up_low[i], weight[0, :, 192:256].reshape(256, D), 1, 1).astype(bf16)
+        product = gab[...].astype(f32) * att[i].astype(f32)
+        high = product.astype(bf16)
+        rest = (product - high.astype(f32)).astype(bf16)
+        along[...] = dot(head_rows, high, 1, 1) + dot(head_rows, rest, 1, 1)
+
+        def one_head(h, carry):
+            mask = jnp.where(lane_head == h, 1.0, 0.0)
+            low_mask = mask.astype(bf16)
+            q = qkv[i, :, 0:256] * low_mask
+            big[:, 0:rows] = dot(qkv[i, :, 256:512], q * (HD ** (-0.5)), 1, 1)
+            big[:, 640 : 640 + rows] = dot(qkv[i, :, 512:768], gab[...] * low_mask, 1, 1)
+            lse_row = lse[i, pl.ds(h, 1)]
+            along_row = along[pl.ds(h, 1)]
+
+            def step(r):
+                keys = lax.broadcasted_iota(jnp.int32, (16, 1), 0) + r.start
+                p = jnp.exp(big[r, 0:rows] - lse_row)
+                p = jnp.where(keys < tokens, p, 0.0)
+                soft[r] = p.astype(bf16)
+                low_scores[r] = (p * (big[r, 640 : 640 + rows] - along_row)).astype(bf16)
+
+            each_rows(rows, 16, step, unroll=2)
+            scale = HD ** (-0.5)
+            grad_q = dot(low_scores[...], qkv[i, :, 256:512], 0, 0) * (mask * scale)
+            grad_k = dot(low_scores[...], q, 1, 0) * (mask * scale)
+            grad_v = dot(soft[...], gab[...], 1, 0) * mask
+            for m, part in enumerate((grad_q, grad_k, grad_v)):
+                part = part.astype(bf16)
+                at = slice(m * 256, m * 256 + 256)
+
+                @pl.when(h == 0)
+                def _():
+                    gh[i, :, at] = part
+
+                @pl.when(h > 0)
+                def _():
+                    gh[i, :, at] = gh[i, :, at] + part
+
+            return carry
+
+        lax.fori_loop(0, 4, one_head, 0)
+
+        def step(r):
+            unit_sums[l, 1, :, 0:768] += eights(gh[i, r, 0:768].astype(f32))
+
+        each_rows(rows, 16, step, unroll=2)
+
+        def partial(at):
+            terms = [
+                dot(gh[i, :, m * 256 : m * 256 + 256], weight[0, :, m * HD : m * HD + HD, at].reshape(256, HALF), 1, 0)
+                for m in range(3)
+            ]
+            return terms[0] + terms[1] + terms[2]
+
+        exchange.reduce(i, partial, kept)
+        exchange.side_copy(i, 1).start()
+
+    span = D // spot.blocks
+
+    def unit_term(k, left, right):
+        def one(plane, carry):
+            at = lanes(plane * 256, 256)
+            for b in range(spot.blocks):
+                to = slice(b * span, b * span + span)
+                part = dot(left[0, :, at], right[0, :, to], 0, 0) + dot(left[1, :, at], right[1, :, to], 0, 0)
+                term[k, plane, :, to] = part.astype(bf16)
+            return carry
+
+        lax.fori_loop(0, 4, one, 0)
+
+    def attn_term():
+        for m in range(4):
+            left = gh if m < 3 else att
+            right = normed if m < 3 else up_low
+            at = slice(m * 256, m * 256 + 256) if m < 3 else slice(0, 256)
+            for b in range(spot.blocks):
+                to = slice(b * span, b * span + span)
+                part = dot(left[0, :, at], right[0, :, to], 0, 0) + dot(left[1, :, at], right[1, :, to], 0, 0)
+                term[0, :, m * HD : m * HD + HD, to] = part.astype(bf16).reshape(4, HD, span)
+
+    def one_layer(step_index, carry):
+        l = top - step_index
+        again = l < top
+        more = l > 0
+        above = jnp.minimum(l + 1, top)
+        mlp_stage(l, 0)
+
+        @pl.when(again)
+        def _():
+            scatter.sum_blocks(1, above < top, above > 0)
+            scatter.sum_planes(3 * above + 2, 2, above < top, above > 0)
+
+        mlp_stage(l, 1)
+
+        @pl.when(l == top)
+        def _():
+            last_copy.wait_recv()
+            load_stream = load(stream_in.at[spot.side], big.at[:, 0:D], 11)
+            load_stream.start()
+
+            def add(r):
+                v = last_chip[spot.side, r].astype(f32) + last_in[r].astype(f32)
+                result[r, exchange.mine] = v.astype(bf16)
+
+            each_rows(rows, 16, add, unroll=2)
+            load_stream.wait()
+
+            @pl.when(jnp.logical_not(owner))
+            def _():
+                half_copy.start()
+                half_copy.wait_send()
+
+            @pl.when(owner)
+            def _():
+                half_in.wait_recv()
+
+                def whole_row(r):
+                    v = big[r, 0:D] + result[r].astype(f32) + vec[top, 5:6]
+                    result[r] = v.astype(bf16)
+
+                each_rows(rows, 16, whole_row, unroll=2)
+
+            last_copy.wait_send()
+            for copy in load_attn(top):
+                copy.start()
+            return_begin(0, out_pair)
+
+        @pl.when(again)
+        def _():
+            for copy in load_unit(l, 1):
+                copy.start()
+
+        scatter.before_terms(2, again)
+        unit_term(2, hid, up_low)
+        scatter.send_terms(2, again)
+        load_normed(l, 1).wait()
+        scatter.before_terms(1, again)
+        unit_term(1, gh, normed)
+        scatter.send_terms(1, again)
+
+        @pl.when(more)
+        def _():
+            below = jnp.maximum(l - 1, 0)
+            load_hidden(below).start()
+            load_weight(below, 1).start()
+            load_weight(below, 2).start()
+
+        load_normed(l, 0).start()
+
+        @pl.when(again)
+        def _():
+            scatter.sum_blocks(0, above < top, above > 0)
+            scatter.sum_planes(3 * above + 1, 1, above < top, above > 0)
+
+        attn_stage(l, 0)
+        attn_stage(l, 1)
+        for copy in load_unit(l, 0):
+            copy.start()
+        load_normed(l, 0).wait()
+        scatter.before_terms(0, again)
+        attn_term()
+        scatter.send_terms(0, again)
+
+        @pl.when(more)
+        def _():
+            below = jnp.maximum(l - 1, 0)
+            load_weight(below, 0).start()
+            load_normed(below, 1).start()
+            for copy in load_attn(below):
+                copy.start()
+
+        @pl.when(again)
+        def _():
+            scatter.sum_planes(3 * above, 0, above < top, above > 0)
+
+        scatter.sum_blocks(2, again, more)
+        for copy in load_unit(l, 0):
+            copy.wait()
+        return carry
+
+    lax.fori_loop(0, LAYERS, one_layer, 0)
+
+    for i in range(2):
+        exchange.finish(i, 1)
+        norm_back(0, 0, i)
+
+    return_begin(1, in_pair)
+
+    cols = D // fsdp
+    per = HD // fsdp
+    for l in range(LAYERS):
+        features = [jnp.sum(sums[(l + 1) * 6 + n], axis=0, keepdims=True) for n in range(6)]
+
+        def placed(values, width, offset):
+            c = lax.broadcasted_iota(jnp.int32, (D, width), 0)
+            j = lax.broadcasted_iota(jnp.int32, (D, width), 1)
+            pick = jnp.where((c // cols == j % fsdp) & (c % cols == offset + j // fsdp), 1.0, 0.0).astype(bf16)
+            return dot(jnp.broadcast_to(values, (16, width)).astype(bf16), pick, 1, 1)[0:1]
+
+        inner = jnp.sum(unit_sums[l, 0], axis=0, keepdims=True)
+        qkv_sums = jnp.sum(unit_sums[l, 1], axis=0, keepdims=True)
+        for plane in range(4):
+            row = placed(inner[:, plane * 256 : plane * 256 + 256], 256, 2 * per)
+            row = row + placed(qkv_sums[:, plane * HD : plane * HD + HD], HD, 0)
+            row = row + placed(qkv_sums[:, 512 + plane * HD : 512 + plane * HD + HD], HD, per)
+            block = jnp.concatenate(features + [row, jnp.zeros((9, D), f32)], axis=0)
+            small_term[0, plane, 16 * l : 16 * l + 16] = block.astype(bf16)
+    never = spot.plane < 0
+    small.send_terms(0, never)
+    scatter.sum_blocks(1, LAYERS > 1, False)
+    scatter.sum_planes(2, 2, LAYERS > 1, False)
+    scatter.sum_blocks(0, LAYERS > 1, False)
+    small.sum_blocks(0, never, never)
+    scatter.sum_planes(1, 1, LAYERS > 1, False)
+    scatter.sum_planes(0, 0, LAYERS > 1, False)
+    small.sum_planes(0, 0, never, never)
+    for k in range(3):
+        scatter.finish(k, k)
+    small.finish(0, 0)
+    for g in range(3 * LAYERS):
+        scatter.arrive(g, g % 3)
+    small.arrive(0, 0)
+    return_end(0, out_pair)
+    return_end(1, in_pair)
+
+
+def backward_call(fsdp, head, tokens, rows, direct, kept):
+    groups = 3 * LAYERS
+    blocks = fsdp // TP
+    span = D // blocks
+    cols = span // TP
+    anyspace = pl.BlockSpec(memory_space=pl.ANY)
+    shape = jax.ShapeDtypeStruct
+    dma, plain = pltpu.SemaphoreType.DMA, pltpu.SemaphoreType.REGULAR
+    out_shape = (
+        shape((2, rows, D), bf16),
+        shape((2, rows, D), bf16),
+        shape((groups, TP, 256, cols) if direct else (groups, 256, span), bf16),
+        shape((1, TP, 32, cols) if direct else (1, 32, span), bf16),
+    )
+    scratch = [
+        pltpu.VMEM((3, 4, 256, D), bf16),
+        pltpu.VMEM((LAYERS, 8, D), f32),
+        pltpu.VMEM((2, rows, D), f32),
+        pltpu.VMEM((2, rows, D), bf16),
+        pltpu.VMEM((2, rows, D), bf16),
+        pltpu.VMEM((2, rows, D), bf16),
+        pltpu.VMEM((2, rows, D), bf16),
+        pltpu.VMEM((2, rows, D), bf16),
+        pltpu.VMEM((2, rows, 128), f32),
+        pltpu.VMEM((2, rows, 768), bf16),
+        pltpu.VMEM((2, rows, 256), bf16),
+        pltpu.VMEM((2, 8, rows), f32),
+        pltpu.VMEM((rows, 640 + -(-rows // 128) * 128), f32),
+        pltpu.VMEM((rows, rows), bf16),
+        pltpu.VMEM((rows, rows), bf16),
+        pltpu.VMEM((rows, 256), bf16),
+        pltpu.VMEM((16, rows), f32),
+        pltpu.VMEM((rows, HALF), f32),
+        pltpu.VMEM((2, rows, HALF), bf16),
+        pltpu.VMEM((2, rows, HALF), bf16),
+        pltpu.VMEM((2, rows, HALF), bf16),
+        pltpu.VMEM((2, 2, rows, HALF), bf16),
+        pltpu.VMEM((2, rows, D), bf16),
+        pltpu.VMEM((rows, HALF), bf16),
+        pltpu.VMEM((rows, D), bf16),
+        pltpu.VMEM((6 * (LAYERS + 1), 8, D), f32),
+        pltpu.VMEM((LAYERS, 2, 8, D), f32),
+    ]
+    for slots, units in ((3, 256), (1, 32)):
+        scratch += [
+            pltpu.VMEM((slots, 4, units, D), bf16),
+            pltpu.VMEM((slots, blocks - 1, 4, units, span), bf16),
+            pltpu.VMEM((slots, 4, units, span), bf16),
+            pltpu.VMEM((slots, 3, units, span), bf16),
+            pltpu.VMEM((slots, units, span), bf16),
+        ]
+    scratch += [dma((2,)), dma((2,)), dma((2, 2)), dma((2, 2)), dma((2,)), dma((2,))]
+    for slots, count in ((3, groups), (1, 1)):
+        scratch += [
+            dma((slots, blocks - 1)), dma((slots, blocks - 1)),
+            dma((slots, 3)), dma((slots, 3)),
+            dma((count, 4)), dma((count, 4)),
+            dma((count,)),
+            plain((slots, blocks - 1)), plain((slots, 3)),
+        ]
+    scratch += [dma((2,)), dma((2,)), dma((2, 4)), dma((2, 4)), dma((16,)), dma((3,))]
+    return pl.pallas_call(
+        functools.partial(backward_kernel, (fsdp, head, tokens, rows, direct)),
+        out_shape=out_shape,
+        in_specs=[anyspace] * len(kept),
+        out_specs=tuple(anyspace for _ in out_shape),
+        scratch_shapes=scratch,
+        compiler_params=pltpu.CompilerParams(
+            collective_id=1, has_side_effects=True, vmem_limit_bytes=63 << 20
+        ),
+        name="backward_layers",
+    )(*kept)
 
 
 class Places:
@@ -680,16 +1315,6 @@
     def role_xor(self, v, bits, sends=None):
         return lax.ppermute(v, AXES, self.pairs(lambda b, r, p: (b, r ^ bits, p), sends))
 
-    def plane_xor(self, v, bits, sends=None):
-        return lax.ppermute(v, AXES, self.pairs(lambda b, r, p: (b, r, p ^ bits), sends))
-
-    def block_shift(self, v, step):
-        return lax.ppermute(v, AXES, self.pairs(lambda b, r, p: ((b + step) % self.blocks, r, p)))
-
-
-def pick(parts, index):
-    return lax.dynamic_index_in_dim(jnp.stack(parts), index, 0, keepdims=False)
-
 
 def by_xor(parts, index):
     a, b, c, d = parts
@@ -698,122 +1323,6 @@
     c, d = jnp.where(odd, d, c), jnp.where(odd, c, d)
     top = (index & 2) == 2
     return [jnp.where(top, c, a), jnp.where(top, d, b), jnp.where(top, a, c), jnp.where(top, b, d)]
-
-
-def sum_roles(pl, rows):
-    half = rows.shape[1] // 2
-    core = pl.role & 1
-    rows = low(rows)
-    kept = jnp.where(core == 0, rows[:, :half], rows[:, half:])
-    sent = jnp.where(core == 0, rows[:, half:], rows[:, :half])
-    chip = low(wide(kept) + wide(pl.role_xor(sent, 1)))
-    total = low(wide(chip) + wide(pl.role_xor(chip, 2)))
-    other = pl.role_xor(total, 1)
-    return wide(
-        jnp.concatenate(
-            [jnp.where(core == 0, total, other), jnp.where(core == 0, other, total)], axis=1
-        )
-    )
-
-
-def scatter_group(pl, grads):
-    mats, head, units, width = grads.shape
-    grads = grads.reshape(mats, head, units, pl.blocks, width // pl.blocks)
-    total = lax.dynamic_index_in_dim(grads, pl.block, 3, False)
-    for step in range(1, pl.blocks):
-        sent = lax.dynamic_index_in_dim(grads, (pl.block + step) % pl.blocks, 3, False)
-        total = total + wide(pl.block_shift(low(sent), step))
-    mine = lax.dynamic_index_in_dim(total, pl.plane, 1, False)
-    for bits in (1, 2, 3):
-        sent = lax.dynamic_index_in_dim(total, pl.plane ^ bits, 1, False)
-        mine = mine + wide(pl.plane_xor(low(sent), bits))
-    mine = low(mine).reshape(mats, units, TP, -1)
-    exchanged = [lax.dynamic_index_in_dim(mine, pl.role, 2, False)]
-    for bits in (1, 2, 3):
-        exchanged.append(pl.role_xor(lax.dynamic_index_in_dim(mine, pl.role ^ bits, 2, False), bits))
-    return wide(jnp.stack(by_xor(exchanged, pl.role)))
-
-def return_images(pl, pair):
-    mine = low(jnp.where(pl.role >= 2, pair[1], pair[0]))
-    owner = lambda b, r, p: (r & 1) == (p & 1)
-    one, two, three = [pl.plane_xor(mine, bits, owner) for bits in (1, 2, 3)]
-    odd = (pl.role & 1) != (pl.plane & 1)
-    near = jnp.where(odd, one, mine)
-    far = jnp.where(odd, three, two)
-    first = pl.plane < 2
-    return wide(jnp.stack([jnp.where(first, near, far), jnp.where(first, far, near)]))
-
-
-def norm_rows(stream, gain, shift):
-    average = jnp.mean(stream, axis=-1, keepdims=True)
-    centred = stream - average
-    inverse = lax.rsqrt(jnp.mean(centred * centred, axis=-1, keepdims=True) + epsilon)
-    unit = centred * inverse
-    return low(unit * gain + shift), unit, inverse
-
-
-def norm_back(upstream, unit, inverse, gain):
-    scaled = upstream * gain
-    return inverse * (
-        scaled
-        - jnp.mean(scaled, axis=-1, keepdims=True)
-        - unit * jnp.mean(scaled * unit, axis=-1, keepdims=True)
-    )
-
-
-def split_heads(rows):
-    return rows.reshape(rows.shape[0], rows.shape[1] // HD, HD)
-
-
-def layer_backward(pl, upstream, weights, stored):
-    (w_qkv, w_out), (w_in, w_down), qv_bias, in_bias, gains, shifts = weights
-    (
-        unit_first, inverse_first, normed, queries, key_rows, value_rows, logsum, attended,
-        unit_second, inverse_second, normed_second, hidden, active,
-    ) = stored
-    shift_down = jnp.sum(upstream, axis=0)
-    upstream_low = low(upstream)
-    grad_down = product(active, upstream_low, "sf,sd->fd")
-    grad_active = product(upstream_low, w_down, "sd,fd->sf")
-    unused, gelu_back = jax.vjp(functools.partial(jax.nn.gelu, approximate=False), hidden)
-    grad_hidden = low(gelu_back(grad_active)[0])
-    grad_in_bias = jnp.sum(wide(grad_hidden), axis=0)
-    grad_in = product(grad_hidden, normed_second, "sf,sd->fd")
-    grad_normed_second = sum_roles(pl, product(grad_hidden, w_in, "sf,fd->sd"))
-    gain_second = jnp.sum(grad_normed_second * unit_second, axis=0)
-    shift_second = jnp.sum(grad_normed_second, axis=0)
-    grad_mid = upstream + norm_back(grad_normed_second, unit_second, inverse_second, gains[1])
-    shift_out = jnp.sum(grad_mid, axis=0)
-    mid_low = low(grad_mid)
-    grad_out = product(attended, mid_low, "sa,sd->ad")
-    grad_attended = low(product(mid_low, w_out, "sd,ad->sa"))
-    query_heads, key_heads, value_heads = map(split_heads, (queries, key_rows, value_rows))
-    factor = HD ** (-0.5)
-    soft = jnp.exp(product(query_heads, key_heads, "qhd,khd->hqk") * factor - logsum)
-    attended_heads = split_heads(grad_attended)
-    flat = queries.shape
-    grad_values = low(product(low(soft), attended_heads, "hqk,qhd->khd").reshape(flat))
-    grad_soft = product(attended_heads, value_heads, "qhd,khd->hqk")
-    grad_scores = low(soft * (grad_soft - jnp.sum(grad_soft * soft, axis=-1, keepdims=True)))
-    grad_queries = low((product(grad_scores, key_heads, "hqk,khd->qhd") * factor).reshape(flat))
-    grad_keys = low((product(grad_scores, query_heads, "hqk,qhd->khd") * factor).reshape(flat))
-    grad_qv = jnp.stack([jnp.sum(wide(grad_queries), axis=0), jnp.sum(wide(grad_values), axis=0)])
-    grad_qkv = [product(g, normed, "sa,sd->ad") for g in (grad_queries, grad_keys, grad_values)]
-    partial_sum = (
-        product(grad_queries, w_qkv[0], "sa,ad->sd")
-        + product(grad_keys, w_qkv[1], "sa,ad->sd")
-        + product(grad_values, w_qkv[2], "sa,ad->sd")
-    )
-    grad_normed_first = sum_roles(pl, partial_sum)
-    gain_first = jnp.sum(grad_normed_first * unit_first, axis=0)
-    shift_first = jnp.sum(grad_normed_first, axis=0)
-    upstream = grad_mid + norm_back(grad_normed_first, unit_first, inverse_first, gains[0])
-    attn_grads = jnp.stack(grad_qkv + [grad_out])
-    mlp_grads = jnp.stack([grad_in, grad_down])
-    by_feature = jnp.stack(
-        [gain_first, gain_second, shift_first, shift_second, shift_out, shift_down]
-    )
-    return upstream, (attn_grads, mlp_grads, grad_qv, grad_in_bias, by_feature)
 
 
 def pack_inputs(pl, w_qkv, w_out, w_in, w_down, qv_bias, in_bias, gains, shifts):
@@ -845,84 +1354,50 @@
     return jnp.concatenate(by_xor(exchanged, pl.role), axis=-1)
 
 
+def scatter_roles(pl, mine):
+    groups, units, width = mine.shape
+    mine = mine.reshape(groups, units, TP, width // TP)
+    exchanged = [lax.dynamic_index_in_dim(mine, pl.role, 2, False)]
+    for bits in (1, 2, 3):
+        exchanged.append(pl.role_xor(lax.dynamic_index_in_dim(mine, pl.role ^ bits, 2, False), bits))
+    return jnp.stack(by_xor(exchanged, pl.role), axis=1)
+
+
 def body(images, cotangent, w_qkv, w_out, w_in, w_down, qv_bias, in_bias, gains, shifts):
     fsdp, head = lax.axis_size("fsdp"), lax.axis_size("head")
     places = Places(fsdp, head)
     cols = w_qkv.shape[2]
-    width, units = w_qkv.shape[3] // TP, w_in.shape[2] // TP
+    per = HD // fsdp
     tokens = images.shape[1]
     rows = -(-tokens // 32) * 32
-    packed, extras, direct = pack_inputs(places, w_qkv, w_out, w_in, w_down, qv_bias, in_bias, gains, shifts)
+    packed, extras, direct = pack_inputs(
+        places, w_qkv, w_out, w_in, w_down, qv_bias, in_bias, gains, shifts
+    )
     pad = ((0, rows - tokens), (0, 0))
     own_image = jnp.pad(lax.dynamic_index_in_dim(images, places.plane // 2, 0, False), pad)
     own_cot = jnp.pad(lax.dynamic_index_in_dim(cotangent, places.plane // 2, 0, False), pad)
-    (
-        whole, vec, normed, unit, inverse, qkv, att, lse, hidden, stream, chip, cots
-    ) = forward_call(fsdp, head, tokens, rows, direct, own_image, own_cot, packed, extras)
-    streams = []
-    core = places.role & 1
-    for i in range(2):
-        total = low(wide(chip[i]) + wide(places.role_xor(chip[i], 2)))
-        other = places.role_xor(total, 1)
-        both = jnp.concatenate([jnp.where(core == 0, total, other), jnp.where(core == 0, other, total)], axis=1)
-        streams.append((stream[i] + wide(both) + vec[1, 5])[:tokens])
-    block_out = return_images(places, streams)
-    upstreams = [wide(cots[i, :tokens]) for i in range(2)]
-    parts = {}
-    for l in reversed(range(LAYERS)):
-        sums = None
-        attn_w = whole[3 * l].reshape(4, 4, HD, D).transpose(1, 0, 2, 3).reshape(4, 256, D)
-        weights = (
-            (attn_w[:3], attn_w[3]),
-            (whole[3 * l + 1].reshape(D, D), whole[3 * l + 2].reshape(D, D)),
-            None, None, vec[l, 0:2], None,
-        )
-        for i in range(2):
-            kept = (
-                wide(unit[l, 0, i, :tokens]), inverse[l, 0, i, :tokens, 0:1], normed[l, 0, i, :tokens],
-                qkv[l, i, :tokens, 0:256], qkv[l, i, :tokens, 256:512], qkv[l, i, :tokens, 512:768],
-                lse[l, i, 0:4, :tokens][:, :, None], att[l, i, :tokens],
-                wide(unit[l, 1, i, :tokens]), inverse[l, 1, i, :tokens, 0:1], normed[l, 1, i, :tokens],
-                wide(hidden[l, i, :tokens]), low(jax.nn.gelu(wide(hidden[l, i, :tokens]), approximate=False)),
-            )
-            upstreams[i], grads = layer_backward(places, upstreams[i], weights, kept)
-            sums = grads if sums is None else tuple(a + b for a, b in zip(sums, grads))
-        mlp = scatter_group(places, sums[1].reshape(2, 4, 256, D))
-        attn = scatter_group(places, sums[0].reshape(4, 4, HD, D))
-        parts[l] = (attn, mlp, *sums[2:])
-    input_grad = return_images(places, upstreams)
-
-    attn = jnp.stack([parts[l][0] for l in range(LAYERS)])
-    mlp = jnp.stack([parts[l][1] for l in range(LAYERS)])
-    attn = attn.transpose(0, 2, 1, 3, 4).reshape(LAYERS, 4, TP * width, cols)
-    mlp = mlp.transpose(0, 2, 1, 3, 4).reshape(LAYERS, 2, TP * units, cols)
-    grad_qkv = attn[:, :3].transpose(0, 1, 3, 2)
-    grad_out = attn[:, 3]
-    grad_in = mlp[:, 0].transpose(0, 2, 1)
-    grad_down = mlp[:, 1]
-
-    by_feature = jnp.stack([parts[l][4] for l in range(LAYERS)])
-    qv = jnp.stack([parts[l][2] for l in range(LAYERS)]).reshape(LAYERS, 2, head, width)
-    inner = jnp.stack([parts[l][3] for l in range(LAYERS)]).reshape(LAYERS, head, units)
-    qv_full = lax.dynamic_update_index_in_dim(
-        jnp.zeros((LAYERS, 2, head, TP, width), jnp.float32), qv, places.role, 3
-    )
-    inner_full = lax.dynamic_update_index_in_dim(
-        jnp.zeros((LAYERS, head, TP, units), jnp.float32), inner, places.role, 2
-    )
-    vector = jnp.concatenate([by_feature.reshape(-1) / TP, qv_full.reshape(-1), inner_full.reshape(-1)])
-    vector = lax.psum(vector, AXES)
-    f, h = lax.axis_index("fsdp"), lax.axis_index("head")
-    a, b = by_feature.size, by_feature.size + qv_full.size
-    by_feature = vector[:a].reshape(LAYERS, 6, fsdp, cols)
-    by_feature = lax.dynamic_index_in_dim(by_feature, f, 2, False)
-    qv = vector[a:b].reshape(LAYERS, 2, head, -1, fsdp)
-    qv = lax.dynamic_index_in_dim(lax.dynamic_index_in_dim(qv, h, 2, False), f, 3, True)
-    inner = vector[b:].reshape(LAYERS, head, -1, fsdp)
-    inner = lax.dynamic_index_in_dim(lax.dynamic_index_in_dim(inner, h, 1, False), f, 2, True)
+    kept = forward_call(fsdp, head, tokens, rows, direct, own_image, own_cot, packed, extras)
+    block_out, input_grad, grads, small = backward_call(fsdp, head, tokens, rows, direct, kept)
+    if not direct:
+        grads, small = scatter_roles(places, grads), scatter_roles(places, small)
+    grads = grads.astype(f32).reshape(LAYERS, 3, TP, 256, cols)
+    attn = grads[:, 0].reshape(LAYERS, TP, 4, HD, cols).transpose(0, 2, 1, 3, 4).reshape(LAYERS, 4, TP * HD, cols)
+    small = small.astype(f32).reshape(TP, LAYERS, 16, cols)
+    features = small[0, :, 0:6]
+    units = small[:, :, 6].transpose(1, 0, 2)
+    qv = units[:, :, 0 : 2 * per].reshape(LAYERS, TP, 2, per).transpose(0, 2, 1, 3).reshape(LAYERS, 2, TP * per, 1)
+    inner = units[:, :, 2 * per : 6 * per].reshape(LAYERS, TP * 4 * per, 1)
     return (
-        block_out, input_grad, grad_qkv, grad_out, grad_in, grad_down,
-        qv, inner, by_feature[:, :2], by_feature[:, 2:],
+        block_out[:, :tokens].astype(f32),
+        input_grad[:, :tokens].astype(f32),
+        attn[:, :3].transpose(0, 1, 3, 2),
+        attn[:, 3],
+        grads[:, 1].reshape(LAYERS, TP * 256, cols).transpose(0, 2, 1),
+        grads[:, 2].reshape(LAYERS, TP * 256, cols),
+        qv,
+        inner,
+        features[:, 0:2],
+        features[:, 2:6],
     )
 
 

time: 1170 us -> 606 us (0.52)
  Pallas kernels: 253 us -> 552 us
  waiting for transfers between devices: 277 us -> 0 us
  local copies, waits for them, and re-layouts: 227 us -> 41.2 us
  other arithmetic: 152 us -> 4.37 us
  matrix products: 143 us -> 0 us
  starting transfers between devices: 90.8 us -> 0 us
  between operations: 17.5 us -> 1.05 us
    pallas_call x0 -> x1, Pallas kernels: none -> 299 us  [backward_call(): pl.pallas_call(functools.partial(backward_kernel, (fsdp, head, tokens, ro...]
    psum x1 -> x0, waiting for transfers between devices: 149 us -> none  [body(): vector = lax.psum(vector, AXES)]
    dot_general x68 -> x0, matrix products: 143 us -> none  [product(): return jnp.einsum(form, left, right, preferred_element_type=jnp.float32)]
    ppermute x62 -> x0, waiting for transfers between devices: 129 us -> none  [the longest x18 81.5 us: plane_xor(): lax.ppermute(v, AXES, self.pairs(lambda b, r, p: (b, r, p ^ bits), sends))]
    ppermute x62 -> x0, starting transfers between devices: 90.7 us -> none  [the longest x40 44.2 us: role_xor(): lax.ppermute(v, AXES, self.pairs(lambda b, r, p: (b, r ^ bits, p), sends))]
    dot_general x23 -> x0, local copies, waits for them, and re-layouts: 74 us -> none  [product(): return jnp.einsum(form, left, right, preferred_element_type=jnp.float32)]
    reduce_sum x10 -> x0, other arithmetic: 41.8 us -> none  [the longest x2 11.8 us: layer_backward(): shift_down = jnp.sum(upstream, axis=0)]
    slice x24 -> x7, local copies, waits for them, and re-layouts: 38.2 us -> 3.3 us  [the longest x1 1.31 us: body(): grads[:, 2].reshape(LAYERS, TP * 256, cols)]
  transfers between devices with their start and end apart: 63 -> 0, of which waited for: 18 -> 0; matrix products, arithmetic and copies ran while one was open for 36% -> 0% of each run, Pallas kernels for 0% -> 0%
where the time goes in v3:
time: 606 us; the launch traced here: 599 us
  Pallas kernels  552 us (91%)
  local copies, waits for them, and re-layouts  41.2 us (7%)
    pallas_call x1, Pallas kernels, backward_call(): pl.pallas_call(functools.partial(backward_kernel, (fsdp, head, tokens, ro...  299 us
    pallas_call x1, Pallas kernels, forward_call(): pl.pallas_call(functools.partial(forward_kernel, (fsdp, head, tokens, row...  253 us
    unnamed x22, local copies, waits for them, and re-layouts  17.6 us

profile of v3, /device:TPU:1, one launch (start us, length us, event | category | flops | bytes accessed | tf_op | source)
XLA Modules:
  0.0 598.5 jit_solution(307832921870613057)
XLA Ops:
  0.7 0.7 fusion.18
  1.4 0.7 slice_reduce_fusion.1
  2.1 0.1 reshape_squeeze.22
  2.2 0.1 reshape_squeeze.24
  2.3 0.7 slice_bitcast_fusion.8
  3.0 0.1 reshape_squeeze.21
  3.1 0.1 reshape.60
  3.3 0.1 reshape_squeeze.23
  3.4 0.1 reshape.61
  3.4 0.1 fusion.13
  3.5 0.7 slice_bitcast_fusion.6
  4.3 0.6 maximum_bitcast_fusion.refs_3_
  4.9 0.9 fusion.17
  5.8 1.1 fusion.16
  6.9 0.2 copy.62
  7.0 0.2 copy.61
  7.3 0.7 slice_bitcast_fusion.2
  8.1 0.2 copy.43
  8.2 1.3 copy.40
  9.5 1.2 fusion.15
  10.8 0.7 constant_dynamic-update-slice_fusion.5
  11.5 0.7 constant_dynamic-update-slice_fusion.4
  12.2 0.7 constant_dynamic-update-slice_fusion.3
  12.9 0.7 constant_dynamic-update-slice_fusion.2
  13.6 0.7 constant_dynamic-update-slice_fusion.1
  14.4 0.7 constant_dynamic-update-slice_fusion.refs_2_
  15.1 4.9 constant_dynamic-slice_fusion
  20.0 0.4 copy.65
  20.4 1.2 pad.22.refs_1_
  21.6 0.4 copy.66
  22.0 1.1 pad.21.refs_0_
  23.1 252.5 %forward_layers.1 = (bf16[6,4,256,1024]{3,2,1,0:T(8,128)(2,1)}, f32[2,8,1024]{2,1,0:T(8,128)}, bf16[2,2,2,608,1024]{4,3,2,1,0:T(8,128)(2,1)}, bf16[2,2,2,608,102...) custom-call(bf16[608,1024]{1,0:T(8,128)(2,1)} %pad.21.refs_0_, ...), custom_call_target="tpu_custom_call" | custom-call | tf_op jit(solution)/shard_map/forward_layers/pallas_call | solution.py:632
  275.7 299.4 %backward_layers.1 = (bf16[2,608,1024]{2,1,0:T(8,128)(2,1)}, bf16[2,608,1024]{2,1,0:T(8,128)(2,1)}, bf16[6,4,256,128]{3,2,1,0:T(8,128)(2,1)}, bf16[1,4,32,128]{3,2,1,0:T(8,128)(2,1)}) custom-call(bf16[6,4,256,1024]{3,2,1,0:T(8,128)(2,1)} %get-tuple-element.26.refs_0_, f32[2,8,1024]{2,1,0:T(8,128)} %get-tuple-element.27.refs_1_, ...), custom_call_target="tpu_custom_call" | custom-call | tf_op jit(solution)/shard_map/backward_layers/pallas_call | solution.py:1279
  575.1 0.7 slice.121
  575.9 0.1 reshape.67
  576.0 0.7 reshape.68
  576.7 0.6 reshape.69
  577.3 0.8 convert.3
  578.1 0.6 slice.125
  578.7 0.6 slice.126
  579.3 2.2 slice_convert_fusion.1
  581.5 5.8 copy.53
  587.4 1.3 fusion.14
  588.7 1.3 copy.58
  590.0 0.7 slice_bitcast_fusion.1
  590.8 1.1 copy.55
  592.0 0.5 slice_convert_fusion
  592.5 5.8 copy.54
  (30 shorter events, 0.5 us)
Async XLA Ops:
  0.6 6.7 %copy-start.4 = (bf16[2,128,1024]{2,1,0:T(8,128)(2,1)S(1)}, bf16[2,128,1024]{2,1,0:T(8,128)(2,1)}, u32[]{:S(2)}) copy-start(bf16[2,128,1024]{2,1,0:T(8,128)(2,1)} %param.14) | copy-start | bytes 1572868
  8.2 6.9 %copy-start.1 = (bf16[2,577,1024]{2,0,1:T(2,128)(2,1)S(1)}, bf16[2,577,1024]{2,0,1:T(2,128)(2,1)}, u32[]{:S(2)}) copy-start(bf16[2,577,1024]{2,0,1:T(2,128)(2,1)} %param.11) | copy-start | bytes 7090180
  9.5 5.6 copy-start.2
  581.5 5.8 copy-start
  590.0 2.0 copy-start.3

commit v4 on v3

--- a/solution.py
+++ b/solution.py
@@ -127,34 +127,33 @@
         ]
         return send(place, place, self.role_sems, (self.base + g, o), spot.at(role=other))
 
-    def to_plane(self, g, o):
+    def hop(self, g, d, up, taken):
+        plane = self.spot.plane
+        step = 1 if up else -1
+        piece = plane - step * d if taken else plane - step * (d - 1)
+        place = self.piece(g, piece, self.spot.block)
+        other = plane - step if taken else plane + step
+        return send(
+            place, place, self.plane_sems, (self.base + g, d - 1 + (0 if up else 3)), self.spot.at(plane=other)
+        )
+
+    def has(self, d, up):
+        return self.spot.plane >= d if up else self.spot.plane + d < self.spot.planes
+
+    def goes(self, d, up):
+        plane, last = self.spot.plane, self.spot.planes - 1
+        if up:
+            return jnp.logical_and(plane >= d, plane < last)
+        return jnp.logical_and(plane + d <= last, plane > 0)
+
+    def to_block(self, g, s, d, up, taken=False):
         spot = self.spot
-        place = self.piece(g, spot.plane, spot.block)
-        return send(
-            place, place, self.plane_sems, (self.base + g, o), spot.at(plane=flip(spot.plane, o))
-        )
-
-    def from_plane(self, g, o):
-        spot = self.spot
-        other = flip(spot.plane, o)
-        place = self.piece(g, other, spot.block)
-        return send(place, place, self.plane_sems, (self.base + g, o), spot.at(plane=other))
-
-    def to_block(self, g, s, o):
-        spot = self.spot
-        place = self.piece(g, flip(spot.plane, o), spot.block)
-        block = (spot.block + s) % spot.blocks
-        return send(
-            place, place, self.block_sems, (self.base + g, s, o), spot.at(block=block)
-        )
-
-    def from_block(self, g, s, o):
-        spot = self.spot
-        block = (spot.block + spot.blocks - s) % spot.blocks
-        place = self.piece(g, flip(spot.plane, o), block)
-        return send(
-            place, place, self.block_sems, (self.base + g, s, o), spot.at(block=block)
-        )
+        plane = spot.plane - d if up else spot.plane + d
+        shift = spot.blocks - s if taken else s
+        block = (spot.block + shift) % spot.blocks
+        place = self.piece(g, plane, block if taken else spot.block)
+        where = (self.base + g, s, d + (0 if up or d == 0 else 3))
+        return send(place, place, self.block_sems, where, spot.at(block=block))
 
     def begin(self, g):
         self.own(g).start()
@@ -162,34 +161,59 @@
             for o in (1, 2, 3):
                 self.to_role(g, o).start()
 
+    def onward(self, g, d):
+        for up in (True, False):
+            if d < self.spot.planes - 1:
+                @pl.when(self.goes(d, up))
+                def _():
+                    self.hop(g, d + 1, up, False).start()
+
     def spread(self, g):
         self.own(g).wait()
         if self.direct:
             for o in (1, 2, 3):
                 self.from_role(g, o).wait_recv()
-        for o in (1, 2, 3):
-            self.to_plane(g, o).start()
+        self.onward(g, 0)
         for s in range(1, self.spot.blocks):
-            self.to_block(g, s, 0).start()
-
-    def relay(self, g, o):
-        self.from_plane(g, o).wait_recv()
-        for s in range(1, self.spot.blocks):
-            self.to_block(g, s, o).start()
+            self.to_block(g, s, 0, True).start()
+
+    def relay(self, g, d):
+        for up in (True, False):
+            @pl.when(self.has(d, up))
+            def _():
+                self.hop(g, d, up, True).wait_recv()
+        self.onward(g, d)
+        for up in (True, False):
+            @pl.when(self.has(d, up))
+            def _():
+                for s in range(1, self.spot.blocks):
+                    self.to_block(g, s, d, up).start()
 
     def complete(self, g):
         for s in range(1, self.spot.blocks):
-            for o in range(4):
-                self.from_block(g, s, o).wait_recv()
+            self.to_block(g, s, 0, True, True).wait_recv()
+            for d in (1, 2, 3):
+                for up in (True, False):
+                    @pl.when(self.has(d, up))
+                    def _():
+                        self.to_block(g, s, d, up, True).wait_recv()
 
     def drain(self, g):
-        for o in (1, 2, 3):
-            if self.direct:
-                self.to_role(g, o).wait_send()
-            self.to_plane(g, o).wait_send()
+        for d in (0, 1, 2, 3):
+            if self.direct and d > 0:
+                self.to_role(g, d).wait_send()
+            for up in (True, False):
+                if d < 3:
+                    @pl.when(self.goes(d, up))
+                    def _():
+                        self.hop(g, d + 1, up, False).wait_send()
+                if d > 0:
+                    @pl.when(self.has(d, up))
+                    def _():
+                        for s in range(1, self.spot.blocks):
+                            self.to_block(g, s, d, up).wait_send()
         for s in range(1, self.spot.blocks):
-            for o in range(4):
-                self.to_block(g, s, o).wait_send()
+            self.to_block(g, s, 0, True).wait_send()
 
 
 class Exchange:
@@ -221,33 +245,19 @@
         return send(place, place, self.back_sems, (i,), self.spot.at(role=flip1(self.spot.role)))
 
     def reduce(self, i, product, kept):
-        rows = kept.shape[0]
         self.sent[i] = product(self.theirs).astype(bf16)
         self.core_copy(i).start()
         kept[...] = product(self.mine)
         copy = self.core_copy(i)
         copy.wait_recv()
-
-        def add(c, carry):
-            r = pl.ds(pl.multiple_of(c * 16, 16), 16)
-            self.chip[i, r] = (kept[r] + self.core_in[i, r].astype(f32)).astype(bf16)
-            return carry
-
-        lax.fori_loop(0, rows // 16, add, 0, unroll=2)
+        self.chip[i] = (kept[...] + self.core_in[i].astype(f32)).astype(bf16)
         copy.wait_send()
 
     def finish(self, i, slot):
         copy = self.side_copy(i, slot)
         copy.wait_recv()
-        rows = self.chip.shape[1]
-
-        def add(c, carry):
-            r = pl.ds(pl.multiple_of(c * 16, 16), 16)
-            total = self.chip[i, r].astype(f32) + self.side_in[i, slot, r].astype(f32)
-            self.full[i, r, self.mine] = total.astype(bf16)
-            return carry
-
-        lax.fori_loop(0, rows // 16, add, 0, unroll=2)
+        total = self.chip[i].astype(f32) + self.side_in[i, slot].astype(f32)
+        self.full[i, :, self.mine] = total.astype(bf16)
         self.back_copy(i).start()
         copy.wait_send()
         self.back_in(i).wait_recv()
@@ -260,6 +270,17 @@
         return carry
 
     lax.fori_loop(0, rows // size, one, 0, unroll=unroll)
+
+
+def unit_picks(held, fsdp):
+    cols = D // fsdp
+    per = HD // fsdp
+    for first, count, offset in ((0, 256, 2 * per), (256, HD, 0), (256 + HD, HD, per)):
+        unit = lax.broadcasted_iota(jnp.int32, (count, D), 0)
+        place = lax.broadcasted_iota(jnp.int32, (count, D), 1)
+        bits = fsdp.bit_length() - 1
+        wanted = (unit & (fsdp - 1)) * cols + offset + (unit >> bits)
+        held[first : first + count] = jnp.where(place == wanted, 1.0, 0.0).astype(bf16)
 
 
 def forward_kernel(cfg, *refs):
@@ -269,7 +290,7 @@
         weights_out, vec_out, normed_out, unit_out, inverse_out, qkv_out, att_out, lse_out, hidden_out,
         stream_out, chip_out, cot_out,
         whole, extra, vec, pair, cots, stream, normed, unit, inverse, qkv, scores, soft, att_sum, att,
-        row_scale, lse, lse_rows, hidden, low_hidden, active, kept,
+        values, lse_rows, low_hidden, active, kept,
         sent, core_in, chip, side_in, full,
         role_s, role_r, plane_s, plane_r, block_s, block_r, local_sem,
         core_s, core_r, side_s, side_r, back_s, back_r,
@@ -335,42 +356,36 @@
         large.begin(g)
     small.spread(0)
     large.spread(0)
+    small.relay(0, 1)
+    large.relay(0, 1)
     large.spread(1)
-    for o in (1, 2, 3):
-        small.relay(0, o)
-    for o in (1, 2, 3):
-        large.relay(0, o)
+    small.relay(0, 2)
+    large.relay(0, 2)
+    small.relay(0, 3)
+    large.relay(0, 3)
+    large.relay(1, 1)
     large.spread(2)
     share_end(own_image, pair, 0)
     small.complete(0)
 
-    cols = D // fsdp
-    quarter = 64
+    unit_picks(active, fsdp)
     for l in range(LAYERS):
         vec[l, 0:6] = extra[0, 0, 16 * l : 16 * l + 16].astype(f32)[0:6]
-
-        def selector(width, offset):
-            c = lax.broadcasted_iota(jnp.int32, (D, width), 0)
-            j = lax.broadcasted_iota(jnp.int32, (D, width), 1)
-            return jnp.where((c // cols == j % fsdp) & (c % cols == offset + j // fsdp), 1.0, 0.0).astype(bf16)
-
-        per = quarter // fsdp
         for plane in range(4):
-            block = extra[0, plane, 16 * l : 16 * l + 16]
-            vec[l, 6:7, plane * 256 : plane * 256 + 256] = dot(block, selector(256, 2 * per), 1, 0)[6:7]
+            units = dot(extra[0, plane, 16 * l : 16 * l + 16], active[0:384], 1, 1)[6:7]
+            vec[l, 6:7, plane * 256 : plane * 256 + 256] = units[:, 0:256]
             if plane % 2 == 0:
-                following = extra[0, plane + 1, 16 * l : 16 * l + 16]
+                before = units
+            else:
                 for k in range(2):
-                    pick = selector(quarter, k * per)
-                    two = jnp.concatenate([dot(block, pick, 1, 0), dot(following, pick, 1, 0)], axis=1)
-                    at = k * 256 + plane * quarter
-                    vec[l, 7:8, at : at + 128] = two[6:7]
+                    at = slice(256 + k * HD, 256 + k * HD + HD)
+                    to = k * 256 + (plane - 1) * HD
+                    vec[l, 7:8, to : to + 128] = jnp.concatenate([before[:, at], units[:, at]], axis=1)
     store_vec = pltpu.make_async_copy(vec, vec_out, store_sem.at[28])
     store_vec.start()
     large.complete(0)
 
     lane_head = lax.broadcasted_iota(jnp.int32, (1, 256), 1) // HD
-    key_bias = jnp.where(lax.broadcasted_iota(jnp.int32, (1, rows), 1) < tokens, 0.0, -1e30)
 
     def stores(l, n, i):
         return [
@@ -379,19 +394,15 @@
             pltpu.make_async_copy(inverse.at[i], inverse_out.at[l, n, i], store_sem.at[4 + i]),
         ]
 
-    def norm(l, n, i, read):
-        def step(r):
-            v = read(r)
-            stream[i, r] = v
-            average = jnp.mean(v, axis=-1, keepdims=True)
-            centred = v - average
-            scale = lax.rsqrt(jnp.mean(centred * centred, axis=-1, keepdims=True) + epsilon)
-            u = centred * scale
-            unit[i, r] = u.astype(bf16)
-            inverse[i, r] = jnp.broadcast_to(scale, (16, 128))
-            normed[i, r] = (u * vec[l, n : n + 1] + vec[l, 2 + n : 3 + n]).astype(bf16)
-
-        each_rows(rows, 16, step, unroll=2)
+    def norm(l, n, i, v):
+        stream[i] = v
+        average = jnp.mean(v, axis=-1, keepdims=True)
+        centred = v - average
+        scale = lax.rsqrt(jnp.mean(centred * centred, axis=-1, keepdims=True) + epsilon)
+        u = centred * scale
+        unit[i] = u.astype(bf16)
+        inverse[i] = jnp.broadcast_to(scale, (rows, 128))
+        normed[i] = (u * vec[l, n : n + 1] + vec[l, 2 + n : 3 + n]).astype(bf16)
         for copy in stores(l, n, i):
             copy.start()
 
@@ -404,11 +415,11 @@
             for copy in stores(l - 1, 1, i):
                 copy.wait()
             before = jnp.maximum(l - 1, 0)
-            norm(l, 0, i, lambda r: stream[i, r] + full[i, r].astype(f32) + vec[before, 5:6])
+            norm(l, 0, i, stream[i] + full[i].astype(f32) + vec[before, 5:6])
 
         @pl.when(l == 0)
         def _():
-            norm(l, 0, i, lambda r: pair[i, r].astype(f32))
+            norm(l, 0, i, pair[i].astype(f32))
 
         store_qkv = pltpu.make_async_copy(qkv, qkv_out.at[l, i], store_sem.at[6])
         store_att = pltpu.make_async_copy(att.at[i], att_out.at[l, i], store_sem.at[8 + i])
@@ -430,36 +441,27 @@
                 part = part + vec[l, 7:8, 0:256]
             if k == 2:
                 part = part + vec[l, 7:8, 256:512]
+                values[...] = jnp.transpose(part).astype(bf16)
             qkv[:, k * 256 : k * 256 + 256] = part.astype(bf16)
         store_qkv.start()
-
-        att_sum[...] = jnp.zeros_like(att_sum)
-        lse[...] = jnp.zeros_like(lse)
+        edge = tokens // 16 * 16
+        late = lax.broadcasted_iota(jnp.int32, (rows - edge, 1), 0) + edge >= tokens
 
         def one_head(h, carry):
-            mask = jnp.where(lane_head == h, 1.0, 0.0)
-            q = qkv[:, 0:256] * (mask * HD ** (-0.5)).astype(bf16)
-            scores[...] = dot(q, qkv[:, 256:512], 1, 1)
-            here = lax.broadcasted_iota(jnp.int32, (1, 128), 1) == h
-
-            def step(r):
-                s = scores[r] + key_bias
-                largest = jnp.max(s, axis=-1, keepdims=True)
-                e = jnp.exp(s - largest)
-                total = jnp.sum(e, axis=-1, keepdims=True)
-                soft[r] = e.astype(bf16)
-                row_scale[r] = jnp.broadcast_to(1.0 / total, (16, 128))
-                lse[r] = jnp.where(here, largest + jnp.log(total), lse[r])
-
-            each_rows(rows, 16, step, unroll=2)
-            o = dot(soft[...], qkv[:, 512:768], 1, 0)
-            scale = row_scale[...]
-            att_sum[...] += o * jnp.concatenate([scale, scale], axis=1) * mask
+            low_mask = jnp.where(lane_head == h, HD ** (-0.5), 0.0).astype(bf16)
+            scores[...] = dot(qkv[:, 256:512], qkv[:, 0:256] * low_mask, 1, 1)
+            scores[edge:rows] = jnp.where(late, -1e30, scores[edge:rows])
+            largest = jnp.max(scores[...], axis=0, keepdims=True)
+            e = jnp.exp(scores[...] - largest)
+            total = jnp.sum(e, axis=0, keepdims=True)
+            soft[...] = e.astype(bf16)
+            lse_rows[i, pl.ds(h, 1)] = largest + jnp.log(total)
+            at = pl.ds(pl.multiple_of(h * HD, HD), HD)
+            att_sum[at] = dot(values[at], soft[...], 1, 0) * (1.0 / total)
             return carry
 
         lax.fori_loop(0, 4, one_head, 0)
-        att[i] = att_sum[...].astype(bf16)
-        lse_rows[i] = jnp.transpose(lse[...])[0:8]
+        att[i] = jnp.transpose(att_sum[...]).astype(bf16)
         store_att.start()
         store_lse.start()
         exchange.reduce(
@@ -472,21 +474,18 @@
         exchange.finish(i, 0)
         for copy in stores(l, 0, i):
             copy.wait()
-        norm(l, 1, i, lambda r: stream[i, r] + full[i, r].astype(f32) + vec[l, 4:5])
+        norm(l, 1, i, stream[i] + full[i].astype(f32) + vec[l, 4:5])
         store_hidden = pltpu.make_async_copy(low_hidden.at[i], hidden_out.at[l, i], store_sem.at[12 + i])
 
         @pl.when(l > 0)
         def _():
             store_hidden.wait()
 
-        hidden[...] = dot(normed[i], whole[g + 1].reshape(D, D), 1, 1)
-
-        def step(r):
-            v = hidden[r] + vec[l, 6:7]
-            low_hidden[i, r] = v.astype(bf16)
-            active[r] = (v * (0.5 + 0.5 * lax.erf(v * (0.5**0.5)))).astype(bf16)
-
-        each_rows(rows, 16, step, unroll=2)
+        for k in range(4):
+            at = slice(k * 256, k * 256 + 256)
+            v = dot(normed[i], whole[g + 1, k], 1, 1) + vec[l, 6:7, at]
+            low_hidden[i, :, at] = v.astype(bf16)
+            active[:, at] = (v * (0.5 + 0.5 * lax.erf(v * (0.5**0.5)))).astype(bf16)
         store_hidden.start()
 
         @pl.when(i == 0)
@@ -519,29 +518,43 @@
         @pl.when(l == 0)
         def _():
             share_begin(own_cot, cots, 1)
+            large.relay(1, 2)
+            large.relay(2, 1)
             large.spread(3)
 
-        for o in (1, 2, 3):
-            large.relay(g + 1, o)
+        @pl.when(l > 0)
+        def _():
+            large.relay(5, 3)
+
         attn_stage(l, 1)
 
-        for o in (1, 2, 3):
-            large.relay(g + 2, o)
-
         @pl.when(l == 0)
         def _():
+            large.relay(1, 3)
+            large.relay(2, 2)
+            large.relay(3, 1)
             large.spread(4)
+            large.relay(2, 3)
 
         large.complete(g + 1)
         mlp_stage(l, 0)
 
         @pl.when(l == 0)
         def _():
-            for o in (1, 2, 3):
-                large.relay(3, o)
+            large.relay(3, 2)
+            large.relay(4, 1)
             large.spread(5)
+            large.relay(3, 3)
 
         mlp_stage(l, 1)
+
+        @pl.when(l == 0)
+        def _():
+            large.relay(4, 2)
+            large.relay(5, 1)
+            large.relay(4, 3)
+            large.relay(5, 2)
+
         for k in range(3):
             store_weights(g + k).start()
         return carry
@@ -605,12 +618,10 @@
         pltpu.VMEM((rows, 768), bf16),
         pltpu.VMEM((rows, rows), f32),
         pltpu.VMEM((rows, rows), bf16),
-        pltpu.VMEM((rows, 256), f32),
+        pltpu.VMEM((256, rows), f32),
         pltpu.VMEM((2, rows, 256), bf16),
-        pltpu.VMEM((rows, 128), f32),
-        pltpu.VMEM((rows, 128), f32),
+        pltpu.VMEM((256, rows), bf16),
         pltpu.VMEM((2, 8, rows), f32),
-        pltpu.VMEM((rows, D), f32),
         pltpu.VMEM((2, rows, D), bf16),
         pltpu.VMEM((rows, D), bf16),
         pltpu.VMEM((rows, HALF), f32),
@@ -620,8 +631,8 @@
         pltpu.VMEM((2, 2, rows, HALF), bf16),
         pltpu.VMEM((2, rows, D), bf16),
         dma((groups + 1, 4)), dma((groups + 1, 4)),
-        dma((groups + 1, 4)), dma((groups + 1, 4)),
-        dma((groups + 1, blocks, 4)), dma((groups + 1, blocks, 4)),
+        dma((groups + 1, 6)), dma((groups + 1, 6)),
+        dma((groups + 1, blocks, 7)), dma((groups + 1, blocks, 7)),
         dma((groups + 1,)),
         dma((2,)), dma((2,)),
         dma((2, 2)), dma((2, 2)),
@@ -643,146 +654,180 @@
 
 
 class Scatter:
-    def __init__(self, spot, term, block_in, total, plane_in, mine, out, block_sems, plane_sems, role_sems, local_sem, block_free, plane_free, direct):
-        self.spot, self.direct = spot, direct
+    def __init__(self, spot, count, term, block_in, total, plane_in, mine, out, block_sems, plane_sems, role_sems, local_sem, block_free, plane_free, direct):
+        self.spot, self.count, self.direct = spot, count, direct
         self.term, self.block_in, self.total = term, block_in, total
         self.plane_in, self.mine, self.out = plane_in, mine, out
         self.block_sems, self.plane_sems, self.role_sems, self.local_sem = block_sems, plane_sems, role_sems, local_sem
         self.block_free, self.plane_free = block_free, plane_free
         self.span = D // spot.blocks
         self.cols = self.span // TP
-
-    def to_block(self, k, s):
+        self.own = lanes(spot.block * self.span, self.span)
+
+    def slot(self, n):
+        return n % self.term.shape[0]
+
+    def third(self, n):
+        return n % self.total.shape[0]
+
+    def to_block(self, n, s):
         block = (self.spot.block + s) % self.spot.blocks
+        a = self.slot(n)
         return send(
-            self.term.at[k, :, :, lanes(block * self.span, self.span)],
-            self.block_in.at[k, s - 1],
-            self.block_sems, (k, s - 1), self.spot.at(block=block),
+            self.term.at[a, :, :, lanes(block * self.span, self.span)],
+            self.block_in.at[a, s - 1],
+            self.block_sems, (a, s - 1), self.spot.at(block=block),
         )
 
-    def to_plane(self, k, o):
-        other = flip(self.spot.plane, o)
+    def along(self, n, plane, up):
+        planes = self.spot.planes
+        a, c = self.slot(n), self.third(n)
+        first, number = (plane + 1, planes - 1 - plane) if up else (0, plane)
+        way = 0 if up else 1
         return send(
-            self.total.at[k, other], self.plane_in.at[k, o - 1],
-            self.plane_sems, (k, o - 1), self.spot.at(plane=other),
+            self.total.at[c, first : first + number], self.plane_in.at[a, way, 0:number],
+            self.plane_sems, (c, way), self.spot.at(plane=plane + (1 if up else -1)),
         )
 
-    def to_role(self, g, k, o):
+    def to_role(self, n, o):
         other = flip(self.spot.role, o)
+        g = self.count - 1 - n
         return send(
-            self.mine.at[k, :, lanes(other * self.cols, self.cols)], self.out.at[g, self.spot.role],
+            self.mine.at[self.slot(n), :, lanes(other * self.cols, self.cols)], self.out.at[g, self.spot.role],
             self.role_sems, (g, o), self.spot.at(role=other),
         )
 
-    def from_role(self, g, k, o):
+    def from_role(self, g, o):
         other = flip(self.spot.role, o)
         place = self.out.at[g, other]
         return send(place, place, self.role_sems, (g, o), self.spot.at(role=other))
 
-    def keep(self, g, k):
+    def keep(self, n):
+        g = self.count - 1 - n
         if self.direct:
             return pltpu.make_async_copy(
-                self.mine.at[k, :, lanes(self.spot.role * self.cols, self.cols)],
+                self.mine.at[self.slot(n), :, lanes(self.spot.role * self.cols, self.cols)],
                 self.out.at[g, self.spot.role], self.local_sem.at[g],
             )
-        return pltpu.make_async_copy(self.mine.at[k], self.out.at[g], self.local_sem.at[g])
-
-    def send_terms(self, k, again):
+        return pltpu.make_async_copy(self.mine.at[self.slot(n)], self.out.at[g], self.local_sem.at[g])
+
+    def before_terms(self, n):
+        @pl.when(n >= 2)
+        def _():
+            for s in range(1, self.spot.blocks):
+                self.to_block(n - 2, s).wait_send()
+
+    def send_terms(self, n):
         for s in range(1, self.spot.blocks):
-            @pl.when(again)
+            @pl.when(n >= 2)
             def _():
-                pl.semaphore_wait(self.block_free.at[k, s - 1], 1)
-
-            self.to_block(k, s).start()
-
-    def before_terms(self, k, again):
-        @pl.when(again)
-        def _():
+                pl.semaphore_wait(self.block_free.at[self.slot(n), s - 1], 1)
+
+            self.to_block(n, s).start()
+
+    def pass_on(self, n, plane, up):
+        @pl.when(n >= 2)
+        def _():
+            pl.semaphore_wait(self.plane_free.at[self.slot(n), 0 if up else 1], 1)
+
+        self.along(n, plane, up).start()
+
+    def sent_along(self, n):
+        for plane in range(self.spot.planes):
+            @pl.when(self.spot.plane == plane)
+            def _():
+                if plane < self.spot.planes - 1:
+                    self.along(n, plane, True).wait_send()
+                if plane > 0:
+                    self.along(n, plane, False).wait_send()
+
+    def sum_blocks(self, n):
+        a, c = self.slot(n), self.third(n)
+        for s in range(1, self.spot.blocks):
+            self.to_block(n, s).wait_recv()
+
+        @pl.when(n >= 3)
+        def _():
+            self.sent_along(n - 3)
+
+        for plane in range(self.spot.planes):
+            value = self.term[a, plane, :, self.own].astype(f32)
             for s in range(1, self.spot.blocks):
-                self.to_block(k, s).wait_send()
-
-    def sum_blocks(self, k, again, more):
-        for s in range(1, self.spot.blocks):
-            self.to_block(k, s).wait_recv()
-
-        @pl.when(again)
-        def _():
-            for o in (1, 2, 3):
-                self.to_plane(k, o).wait_send()
-
-        units = self.term.shape[2]
-        own = lanes(self.spot.block * self.span, self.span)
-        for plane in range(4):
-            def step(r):
-                value = self.term[k, plane, r, own].astype(f32)
-                for s in range(1, self.spot.blocks):
-                    value = value + self.block_in[k, s - 1, plane, r].astype(f32)
-                self.total[k, plane, r] = value.astype(bf16)
-
-            each_rows(units, 16, step, unroll=2)
-
-        @pl.when(more)
+                value = value + self.block_in[a, s - 1, plane].astype(f32)
+            self.total[c, plane] = value.astype(bf16)
+
+        @pl.when(n + 2 < self.count)
         def _():
             for s in range(1, self.spot.blocks):
                 source = (self.spot.block + self.spot.blocks - s) % self.spot.blocks
                 pl.semaphore_signal(
-                    self.block_free.at[k, s - 1], inc=1, device_id=self.spot.at(block=source), device_id_type=MESH
+                    self.block_free.at[a, s - 1], inc=1, device_id=self.spot.at(block=source), device_id_type=MESH
                 )
 
-        for o in (1, 2, 3):
-            @pl.when(again)
+        last = self.spot.planes - 1
+
+        @pl.when(self.spot.plane == 0)
+        def _():
+            self.pass_on(n, 0, True)
+
+        @pl.when(self.spot.plane == last)
+        def _():
+            self.pass_on(n, last, False)
+
+    def take(self, n, plane, up):
+        a, c = self.slot(n), self.third(n)
+        before = plane - 1 if up else plane + 1
+        self.along(n, before, up).wait_recv()
+        planes = range(plane, self.spot.planes) if up else range(0, plane + 1)
+        for at, p in enumerate(planes):
+            value = self.total[c, p].astype(f32) + self.plane_in[a, 0 if up else 1, at].astype(f32)
+            self.total[c, p] = value.astype(bf16)
+
+        @pl.when(n + 2 < self.count)
+        def _():
+            pl.semaphore_signal(
+                self.plane_free.at[a, 0 if up else 1], inc=1, device_id=self.spot.at(plane=before), device_id_type=MESH
+            )
+
+        if (up and plane < self.spot.planes - 1) or (not up and plane > 0):
+            self.pass_on(n, plane, up)
+
+    def hop(self, n, d):
+        for plane, up in ((d, True), (self.spot.planes - 1 - d, False)):
+            @pl.when(self.spot.plane == plane)
             def _():
-                pl.semaphore_wait(self.plane_free.at[k, o - 1], 1)
-
-            self.to_plane(k, o).start()
-
-    def sum_planes(self, g, k, again, more):
-        for o in (1, 2, 3):
-            self.to_plane(k, o).wait_recv()
-        units = self.term.shape[2]
-
-        @pl.when(again)
-        def _():
-            before = jnp.minimum(g + 3, self.out.shape[0] - 1)
-            self.keep(before, k).wait()
+                self.take(n, plane, up)
+
+    def hand_out(self, n):
+        a = self.slot(n)
+
+        @pl.when(n >= 2)
+        def _():
+            self.keep(n - 2).wait()
             if self.direct:
                 for o in (1, 2, 3):
-                    self.to_role(before, k, o).wait_send()
-
-        def step(r):
-            value = self.total[k, self.spot.plane, r].astype(f32)
-            for o in (1, 2, 3):
-                value = value + self.plane_in[k, o - 1, r].astype(f32)
-            self.mine[k, r] = value.astype(bf16)
-
-        each_rows(units, 16, step, unroll=2)
-
-        @pl.when(more)
-        def _():
-            for o in (1, 2, 3):
-                pl.semaphore_signal(
-                    self.plane_free.at[k, o - 1], inc=1,
-                    device_id=self.spot.at(plane=flip(self.spot.plane, o)), device_id_type=MESH,
-                )
-
-        self.keep(g, k).start()
+                    self.to_role(n - 2, o).wait_send()
+
+        self.mine[a] = self.total[self.third(n), self.spot.plane]
+        self.keep(n).start()
         if self.direct:
             for o in (1, 2, 3):
-                self.to_role(g, k, o).start()
-
-    def finish(self, g, k):
-        self.keep(g, k).wait()
-        for s in range(1, self.spot.blocks):
-            self.to_block(k, s).wait_send()
-        for o in (1, 2, 3):
-            self.to_plane(k, o).wait_send()
+                self.to_role(n, o).start()
+
+    def finish(self):
+        for n in range(max(0, self.count - 3), self.count):
+            self.sent_along(n)
+        for n in range(max(0, self.count - 2), self.count):
+            self.keep(n).wait()
+            for s in range(1, self.spot.blocks):
+                self.to_block(n, s).wait_send()
             if self.direct:
-                self.to_role(g, k, o).wait_send()
-
-    def arrive(self, g, k):
+                for o in (1, 2, 3):
+                    self.to_role(n, o).wait_send()
         if self.direct:
-            for o in (1, 2, 3):
-                self.from_role(g, k, o).wait_recv()
+            for g in range(self.count):
+                for o in (1, 2, 3):
+                    self.from_role(g, o).wait_recv()
 
 
 def backward_kernel(cfg, *refs):
@@ -792,26 +837,27 @@
         stream_in, chip_in, cot_in,
         out_pair, in_pair, grads, small_grads,
         weight, vec, up, up_low, hid, gh, normed, unit, inverse, qkv, att, lse, big, soft, low_scores, gab, along,
-        kept, sent, core_in, chip, side_in, full, last_in, result, sums, unit_sums,
+        sent, core_in, chip, side_in, full, last_in, result, sums, unit_sums,
         term, block_in, total, plane_in, mine,
         small_term, small_block_in, small_total, small_plane_in, small_mine,
         core_s, core_r, side_s, side_r, back_s, back_r,
         block_s, block_r, plane_s, plane_r, role_s, role_r, local_sem, block_free, plane_free,
         small_block_s, small_block_r, small_plane_s, small_plane_r, small_role_s, small_role_r, small_local,
         small_block_free, small_plane_free,
-        last_s, last_r, out_s, out_r, load_sem, weight_sem,
+        last_s, last_r, out_s, out_r, line_s, line_r, load_sem, weight_sem,
     ) = refs
+    kept = big.at[:, 0:HALF]
     spot = Spot(fsdp, head)
     greet(spot.partners())
     exchange = Exchange(
         spot, sent, core_in, chip, side_in, full, (core_s, core_r), (side_s, side_r), (back_s, back_r)
     )
     scatter = Scatter(
-        spot, term, block_in, total, plane_in, mine, grads, (block_s, block_r), (plane_s, plane_r),
+        spot, 3 * LAYERS, term, block_in, total, plane_in, mine, grads, (block_s, block_r), (plane_s, plane_r),
         (role_s, role_r), local_sem, block_free, plane_free, direct,
     )
     small = Scatter(
-        spot, small_term, small_block_in, small_total, small_plane_in, small_mine, small_grads,
+        spot, 1, small_term, small_block_in, small_total, small_plane_in, small_mine, small_grads,
         (small_block_s, small_block_r), (small_plane_s, small_plane_r), (small_role_s, small_role_r),
         small_local, small_block_free, small_plane_free, direct,
     )
@@ -871,71 +917,128 @@
     load_cot.wait()
 
     def eights(v):
-        return v[0:8] + v[8:16]
+        return jnp.sum(v.reshape(v.shape[0] // 8, 8, v.shape[1]), axis=0)
 
     for i in range(2):
-        def widen(r):
+        for start in range(0, rows, 128):
+            r = slice(start, min(rows, start + 128))
             v = up_low[i, r].astype(f32)
             up[i, r] = v
             sums[(top + 1) * 6 + 5] += eights(v)
-
-        each_rows(rows, 16, widen, unroll=2)
     load_vec.wait()
 
-    def return_copies(n, pair_out):
+    def return_copies(pair_out):
         slot = spot.plane // 2
-        source = result if n == 0 else up_low.at[spot.side]
-        mine_copy = pltpu.make_async_copy(source, pair_out.at[slot], load_sem.at[12 + n])
+        mine_copy = pltpu.make_async_copy(result, pair_out.at[slot], load_sem.at[12])
         outs = [
-            send(
-                source, pair_out.at[slot], (out_s, out_r), (n, o), spot.at(plane=flip(spot.plane, o))
-            )
+            send(result, pair_out.at[slot], (out_s, out_r), (o,), spot.at(plane=flip(spot.plane, o)))
             for o in (1, 2, 3)
         ]
         return mine_copy, outs
 
-    def return_begin(n, pair_out):
+    def return_begin(pair_out):
         @pl.when(owner)
         def _():
-            mine_copy, outs = return_copies(n, pair_out)
+            mine_copy, outs = return_copies(pair_out)
             mine_copy.start()
             for copy in outs:
                 copy.start()
 
-    def return_end(n, pair_out):
+    def return_end(pair_out):
         for o in (1, 2, 3):
             other = flip(spot.plane, o)
 
             @pl.when(spot.core == other % 2)
             def _():
                 place = pair_out.at[other // 2]
-                send(place, place, (out_s, out_r), (n, o), spot.at(plane=other)).wait_recv()
+                send(place, place, (out_s, out_r), (o,), spot.at(plane=other)).wait_recv()
 
         @pl.when(owner)
         def _():
-            mine_copy, outs = return_copies(n, pair_out)
+            mine_copy, outs = return_copies(pair_out)
             mine_copy.wait()
             for copy in outs:
                 copy.wait_send()
 
+    chunks = [(start, min(160, rows - start)) for start in range(0, rows, 160)]
+    last_plane = spot.planes - 1
+
+    def line_copy(s, j, up, first):
+        start, size = chunks[j]
+        target = in_pair.at[s, start : start + size]
+        source = up_low.at[spot.side, start : start + size] if first else target
+        return pltpu.make_async_remote_copy(
+            src_ref=source, dst_ref=target, send_sem=line_s.at[s, j, 0 if up else 1], recv_sem=line_r.at[s, j],
+            device_id=spot.at(plane=spot.plane + (1 if up else -1)), device_id_type=MESH,
+        )
+
+    def line_ways(s, act):
+        source = 2 * s + spot.core
+        for up, edge in ((True, last_plane), (False, 0)):
+            beyond = spot.plane > source if up else spot.plane < source
+
+            @pl.when(jnp.logical_and(spot.plane == source, spot.plane != edge))
+            def _():
+                act(up, True)
+
+            @pl.when(jnp.logical_and(beyond, spot.plane != edge))
+            def _():
+                act(up, False)
+
+    def line_kept(s):
+        return pltpu.make_async_copy(up_low.at[spot.side], in_pair.at[s], load_sem.at[13])
+
+    def line_begin():
+        for s in range(2):
+            @pl.when(spot.plane == 2 * s + spot.core)
+            def _():
+                line_kept(s).start()
+
+            for j in range(len(chunks)):
+                def act(up, first):
+                    if first:
+                        line_copy(s, j, up, True).start()
+
+                line_ways(s, act)
+
+    def line_relay():
+        for j in range(len(chunks)):
+            for s in range(2):
+                @pl.when(spot.plane != 2 * s + spot.core)
+                def _():
+                    line_copy(s, j, True, False).wait_recv()
+
+                def act(up, first):
+                    if not first:
+                        line_copy(s, j, up, False).start()
+
+                line_ways(s, act)
+
+    def line_end():
+        for s in range(2):
+            @pl.when(spot.plane == 2 * s + spot.core)
+            def _():
+                line_kept(s).wait()
+
+            for j in range(len(chunks)):
+                line_ways(s, lambda up, first: line_copy(s, j, up, first).wait_send())
+
     def norm_back(l, n, i):
-        def step(r):
+        base = (l + 1) * 6
+        for start in range(0, rows, 128):
+            r = slice(start, min(rows, start + 128))
             g = full[i, r].astype(f32)
             u = unit[i, r].astype(f32)
             scaled = g * vec[l, n : n + 1]
             first = jnp.mean(scaled, axis=-1, keepdims=True)
             second = jnp.mean(scaled * u, axis=-1, keepdims=True)
-            scale = inverse[i, r, 0:1]
-            v = up[i, r] + scale * (scaled - first - u * second)
+            v = up[i, r] + inverse[i, r, 0:1] * (scaled - first - u * second)
             up[i, r] = v
             up_low[i, r] = v.astype(bf16)
-            base = (l + 1) * 6
             sums[base + n] += eights(g * u)
             sums[base + 2 + n] += eights(g)
             sums[base + 4 if n == 1 else base - 1] += eights(v)
 
-        each_rows(rows, 16, step, unroll=2)
-
     def mlp_stage(l, i):
         @pl.when(l < top)
         def _():
@@ -947,7 +1050,8 @@
             load_hidden(l).wait()
             load_weight(l, 2).wait()
 
-        big[:, 0:D] = dot(up_low[i], weight[2].reshape(D, D), 1, 1)
+        for k in range(4):
+            big[:, k * 256 : k * 256 + 256] = dot(up_low[i], weight[2, k], 1, 1)
 
         def step(r):
             v = hid[i, r].astype(f32)
@@ -968,6 +1072,7 @@
         exchange.side_copy(i, 0).start()
 
     lane_head = lax.broadcasted_iota(jnp.int32, (1, 256), 1) // HD
+    valid = lax.broadcasted_iota(jnp.int32, (rows, 1), 0) < tokens
     head_rows = jnp.where(
         lax.broadcasted_iota(jnp.int32, (16, 256), 1) // HD == lax.broadcasted_iota(jnp.int32, (16, 256), 0), 1.0, 0.0
     ).astype(bf16)
@@ -1003,14 +1108,10 @@
             lse_row = lse[i, pl.ds(h, 1)]
             along_row = along[pl.ds(h, 1)]
 
-            def step(r):
-                keys = lax.broadcasted_iota(jnp.int32, (16, 1), 0) + r.start
-                p = jnp.exp(big[r, 0:rows] - lse_row)
-                p = jnp.where(keys < tokens, p, 0.0)
-                soft[r] = p.astype(bf16)
-                low_scores[r] = (p * (big[r, 640 : 640 + rows] - along_row)).astype(bf16)
-
-            each_rows(rows, 16, step, unroll=2)
+            p = jnp.exp(big[:, 0:rows] - lse_row)
+            p = jnp.where(valid, p, 0.0)
+            soft[...] = p.astype(bf16)
+            low_scores[...] = (p * (big[:, 640 : 640 + rows] - along_row)).astype(bf16)
             scale = HD ** (-0.5)
             grad_q = dot(low_scores[...], qkv[i, :, 256:512], 0, 0) * (mask * scale)
             grad_k = dot(low_scores[...], q, 1, 0) * (mask * scale)
@@ -1031,10 +1132,10 @@
 
         lax.fori_loop(0, 4, one_head, 0)
 
-        def step(r):
-            unit_sums[l, 1, :, 0:768] += eights(gh[i, r, 0:768].astype(f32))
-
-        each_rows(rows, 16, step, unroll=2)
+        for m in (0, 2):
+            at = slice(m * 256, m * 256 + 256)
+            unit_sums[l, 1, :, at] += eights(gh[i, :, at].astype(f32))
+
 
         def partial(at):
             terms = [
@@ -1048,18 +1149,18 @@
 
     span = D // spot.blocks
 
-    def unit_term(k, left, right):
+    def unit_term(a, left, right):
         def one(plane, carry):
             at = lanes(plane * 256, 256)
             for b in range(spot.blocks):
                 to = slice(b * span, b * span + span)
                 part = dot(left[0, :, at], right[0, :, to], 0, 0) + dot(left[1, :, at], right[1, :, to], 0, 0)
-                term[k, plane, :, to] = part.astype(bf16)
+                term[a, plane, :, to] = part.astype(bf16)
             return carry
 
         lax.fori_loop(0, 4, one, 0)
 
-    def attn_term():
+    def attn_term(a):
         for m in range(4):
             left = gh if m < 3 else att
             right = normed if m < 3 else up_low
@@ -1067,21 +1168,25 @@
             for b in range(spot.blocks):
                 to = slice(b * span, b * span + span)
                 part = dot(left[0, :, at], right[0, :, to], 0, 0) + dot(left[1, :, at], right[1, :, to], 0, 0)
-                term[0, :, m * HD : m * HD + HD, to] = part.astype(bf16).reshape(4, HD, span)
+                term[a, :, m * HD : m * HD + HD, to] = part.astype(bf16).reshape(4, HD, span)
 
     def one_layer(step_index, carry):
         l = top - step_index
         again = l < top
         more = l > 0
-        above = jnp.minimum(l + 1, top)
-        mlp_stage(l, 0)
-
-        @pl.when(again)
-        def _():
-            scatter.sum_blocks(1, above < top, above > 0)
-            scatter.sum_planes(3 * above + 2, 2, above < top, above > 0)
-
-        mlp_stage(l, 1)
+        n = 3 * step_index
+
+        def mlp_image(i, carry):
+            mlp_stage(l, i)
+
+            @pl.when(jnp.logical_and(again, i == 0))
+            def _():
+                scatter.sum_blocks(n - 2)
+                scatter.hop(n - 3, 1)
+
+            return carry
+
+        lax.fori_loop(0, 2, mlp_image, 0)
 
         @pl.when(l == top)
         def _():
@@ -1089,11 +1194,8 @@
             load_stream = load(stream_in.at[spot.side], big.at[:, 0:D], 11)
             load_stream.start()
 
-            def add(r):
-                v = last_chip[spot.side, r].astype(f32) + last_in[r].astype(f32)
-                result[r, exchange.mine] = v.astype(bf16)
-
-            each_rows(rows, 16, add, unroll=2)
+            v = last_chip[spot.side].astype(f32) + last_in[...].astype(f32)
+            result[:, exchange.mine] = v.astype(bf16)
             load_stream.wait()
 
             @pl.when(jnp.logical_not(owner))
@@ -1105,29 +1207,34 @@
             def _():
                 half_in.wait_recv()
 
-                def whole_row(r):
+                for start in range(0, rows, 128):
+                    r = slice(start, min(rows, start + 128))
                     v = big[r, 0:D] + result[r].astype(f32) + vec[top, 5:6]
                     result[r] = v.astype(bf16)
-
-                each_rows(rows, 16, whole_row, unroll=2)
 
             last_copy.wait_send()
             for copy in load_attn(top):
                 copy.start()
-            return_begin(0, out_pair)
+            return_begin(out_pair)
 
         @pl.when(again)
         def _():
             for copy in load_unit(l, 1):
                 copy.start()
 
-        scatter.before_terms(2, again)
-        unit_term(2, hid, up_low)
-        scatter.send_terms(2, again)
+        @pl.when(again)
+        def _():
+            scatter.hop(n - 3, 2)
+            scatter.sum_blocks(n - 1)
+            scatter.hop(n - 2, 1)
+
+        scatter.before_terms(n)
+        unit_term(scatter.slot(n), hid, up_low)
+        scatter.send_terms(n)
         load_normed(l, 1).wait()
-        scatter.before_terms(1, again)
-        unit_term(1, gh, normed)
-        scatter.send_terms(1, again)
+        scatter.before_terms(n + 1)
+        unit_term(scatter.slot(n + 1), gh, normed)
+        scatter.send_terms(n + 1)
 
         @pl.when(more)
         def _():
@@ -1140,17 +1247,34 @@
 
         @pl.when(again)
         def _():
-            scatter.sum_blocks(0, above < top, above > 0)
-            scatter.sum_planes(3 * above + 1, 1, above < top, above > 0)
-
-        attn_stage(l, 0)
-        attn_stage(l, 1)
+            scatter.hop(n - 3, 3)
+            scatter.hand_out(n - 3)
+
+        def attn_image(i, carry):
+            attn_stage(l, i)
+
+            @pl.when(jnp.logical_and(again, i == 0))
+            def _():
+                scatter.hop(n - 2, 2)
+                scatter.hop(n - 1, 1)
+
+            return carry
+
+        lax.fori_loop(0, 2, attn_image, 0)
         for copy in load_unit(l, 0):
             copy.start()
         load_normed(l, 0).wait()
-        scatter.before_terms(0, again)
-        attn_term()
-        scatter.send_terms(0, again)
+
+        @pl.when(again)
+        def _():
+            scatter.hop(n - 2, 3)
+            scatter.hand_out(n - 2)
+            scatter.hop(n - 1, 2)
+
+        scatter.sum_blocks(n)
+        scatter.before_terms(n + 2)
+        attn_term(scatter.slot(n + 2))
+        scatter.send_terms(n + 2)
 
         @pl.when(more)
         def _():
@@ -1160,59 +1284,64 @@
             for copy in load_attn(below):
                 copy.start()
 
-        @pl.when(again)
-        def _():
-            scatter.sum_planes(3 * above, 0, above < top, above > 0)
-
-        scatter.sum_blocks(2, again, more)
         for copy in load_unit(l, 0):
             copy.wait()
         return carry
 
     lax.fori_loop(0, LAYERS, one_layer, 0)
 
-    for i in range(2):
+    end = 3 * LAYERS
+    scatter.hop(end - 4, 3)
+    scatter.hand_out(end - 4)
+    scatter.sum_blocks(end - 2)
+
+    def last_image(i, carry):
         exchange.finish(i, 1)
         norm_back(0, 0, i)
-
-    return_begin(1, in_pair)
-
-    cols = D // fsdp
-    per = HD // fsdp
+        return carry
+
+    lax.fori_loop(0, 2, last_image, 0)
+    line_begin()
+    picks = normed.at[0]
+    unit_picks(picks, fsdp)
     for l in range(LAYERS):
         features = [jnp.sum(sums[(l + 1) * 6 + n], axis=0, keepdims=True) for n in range(6)]
-
-        def placed(values, width, offset):
-            c = lax.broadcasted_iota(jnp.int32, (D, width), 0)
-            j = lax.broadcasted_iota(jnp.int32, (D, width), 1)
-            pick = jnp.where((c // cols == j % fsdp) & (c % cols == offset + j // fsdp), 1.0, 0.0).astype(bf16)
-            return dot(jnp.broadcast_to(values, (16, width)).astype(bf16), pick, 1, 1)[0:1]
-
         inner = jnp.sum(unit_sums[l, 0], axis=0, keepdims=True)
         qkv_sums = jnp.sum(unit_sums[l, 1], axis=0, keepdims=True)
         for plane in range(4):
-            row = placed(inner[:, plane * 256 : plane * 256 + 256], 256, 2 * per)
-            row = row + placed(qkv_sums[:, plane * HD : plane * HD + HD], HD, 0)
-            row = row + placed(qkv_sums[:, 512 + plane * HD : 512 + plane * HD + HD], HD, per)
+            parts = [
+                inner[:, plane * 256 : plane * 256 + 256],
+                qkv_sums[:, plane * HD : plane * HD + HD],
+                qkv_sums[:, 512 + plane * HD : 512 + plane * HD + HD],
+            ]
+            values = jnp.broadcast_to(jnp.concatenate(parts, axis=1), (16, 384)).astype(bf16)
+            row = dot(values, picks[0:384], 1, 0)[0:1]
             block = jnp.concatenate(features + [row, jnp.zeros((9, D), f32)], axis=0)
             small_term[0, plane, 16 * l : 16 * l + 16] = block.astype(bf16)
-    never = spot.plane < 0
-    small.send_terms(0, never)
-    scatter.sum_blocks(1, LAYERS > 1, False)
-    scatter.sum_planes(2, 2, LAYERS > 1, False)
-    scatter.sum_blocks(0, LAYERS > 1, False)
-    small.sum_blocks(0, never, never)
-    scatter.sum_planes(1, 1, LAYERS > 1, False)
-    scatter.sum_planes(0, 0, LAYERS > 1, False)
-    small.sum_planes(0, 0, never, never)
-    for k in range(3):
-        scatter.finish(k, k)
-    small.finish(0, 0)
-    for g in range(3 * LAYERS):
-        scatter.arrive(g, g % 3)
-    small.arrive(0, 0)
-    return_end(0, out_pair)
-    return_end(1, in_pair)
+    small.send_terms(0)
+    scatter.hop(end - 3, 1)
+    scatter.hop(end - 2, 1)
+    scatter.hop(end - 3, 2)
+    scatter.sum_blocks(end - 1)
+    small.sum_blocks(0)
+    scatter.hop(end - 3, 3)
+    scatter.hand_out(end - 3)
+    scatter.hop(end - 2, 2)
+    scatter.hop(end - 1, 1)
+    small.hop(0, 1)
+    scatter.hop(end - 2, 3)
+    scatter.hand_out(end - 2)
+    scatter.hop(end - 1, 2)
+    small.hop(0, 2)
+    scatter.hop(end - 1, 3)
+    scatter.hand_out(end - 1)
+    small.hop(0, 3)
+    small.hand_out(0)
+    line_relay()
+    scatter.finish()
+    small.finish()
+    return_end(out_pair)
+    line_end()
 
 
 def backward_call(fsdp, head, tokens, rows, direct, kept):
@@ -1247,7 +1376,6 @@
         pltpu.VMEM((rows, rows), bf16),
         pltpu.VMEM((rows, 256), bf16),
         pltpu.VMEM((16, rows), f32),
-        pltpu.VMEM((rows, HALF), f32),
         pltpu.VMEM((2, rows, HALF), bf16),
         pltpu.VMEM((2, rows, HALF), bf16),
         pltpu.VMEM((2, rows, HALF), bf16),
@@ -1258,24 +1386,24 @@
         pltpu.VMEM((6 * (LAYERS + 1), 8, D), f32),
         pltpu.VMEM((LAYERS, 2, 8, D), f32),
     ]
-    for slots, units in ((3, 256), (1, 32)):
+    for slots, thirds, units in ((2, 3, 256), (1, 1, 32)):
         scratch += [
             pltpu.VMEM((slots, 4, units, D), bf16),
             pltpu.VMEM((slots, blocks - 1, 4, units, span), bf16),
-            pltpu.VMEM((slots, 4, units, span), bf16),
-            pltpu.VMEM((slots, 3, units, span), bf16),
+            pltpu.VMEM((thirds, 4, units, span), bf16),
+            pltpu.VMEM((slots, 2, 3, units, span), bf16),
             pltpu.VMEM((slots, units, span), bf16),
         ]
     scratch += [dma((2,)), dma((2,)), dma((2, 2)), dma((2, 2)), dma((2,)), dma((2,))]
-    for slots, count in ((3, groups), (1, 1)):
+    for slots, thirds, count in ((2, 3, groups), (1, 1, 1)):
         scratch += [
             dma((slots, blocks - 1)), dma((slots, blocks - 1)),
-            dma((slots, 3)), dma((slots, 3)),
+            dma((thirds, 2)), dma((thirds, 2)),
             dma((count, 4)), dma((count, 4)),
             dma((count,)),
-            plain((slots, blocks - 1)), plain((slots, 3)),
+            plain((slots, blocks - 1)), plain((slots, 2)),
         ]
-    scratch += [dma((2,)), dma((2,)), dma((2, 4)), dma((2, 4)), dma((16,)), dma((3,))]
+    scratch += [dma((2,)), dma((2,)), dma((4,)), dma((4,)), dma((2, 4, 2)), dma((2, 4)), dma((16,)), dma((3,))]
     return pl.pallas_call(
         functools.partial(backward_kernel, (fsdp, head, tokens, rows, direct)),
         out_shape=out_shape,

time: 606 us -> 494 us (0.82)
  Pallas kernels: 552 us -> 440 us
    pallas_call x1, Pallas kernels: 253 us -> 192 us  [forward_call(): pl.pallas_call(functools.partial(forward_kernel, (fsdp, head, tokens, row...]
    pallas_call x1, Pallas kernels: 299 us -> 249 us  [backward_call(): pl.pallas_call(functools.partial(backward_kernel, (fsdp, head, tokens, ro...]
where the time goes in v4:
time: 494 us; the launch traced here: 487 us
  Pallas kernels  440 us (89%)
  local copies, waits for them, and re-layouts  41.2 us (8%)
    pallas_call x1, Pallas kernels, backward_call(): pl.pallas_call(functools.partial(backward_kernel, (fsdp, head, tokens, ro...  249 us
    pallas_call x1, Pallas kernels, forward_call(): pl.pallas_call(functools.partial(forward_kernel, (fsdp, head, tokens, row...  192 us
    unnamed x22, local copies, waits for them, and re-layouts  17.6 us

profile of v4, /device:TPU:1, one launch (start us, length us, event | category | flops | bytes accessed | tf_op | source)
XLA Modules:
  0.0 487.2 jit_solution(5837702079684394045)
XLA Ops:
  0.7 0.7 fusion.18
  1.4 0.7 slice_reduce_fusion.1
  2.1 0.1 reshape_squeeze.22
  2.2 0.1 reshape_squeeze.24
  2.3 0.7 slice_bitcast_fusion.8
  3.0 0.1 reshape_squeeze.21
  3.1 0.1 reshape.60
  3.2 0.1 fusion.11
  3.3 0.1 reshape_squeeze.23
  3.4 0.1 reshape.61
  3.5 0.7 slice_bitcast_fusion.6
  4.3 0.6 maximum_bitcast_fusion.refs_3_
  4.9 0.9 fusion.17
  5.8 1.1 fusion.16
  6.9 0.2 copy.62
  7.0 0.2 copy.61
  7.3 0.7 slice_bitcast_fusion.2
  8.1 0.2 copy.43
  8.2 1.3 copy.40
  9.5 1.2 fusion.15
  10.8 0.7 constant_dynamic-update-slice_fusion.5
  11.5 0.7 constant_dynamic-update-slice_fusion.4
  12.2 0.7 constant_dynamic-update-slice_fusion.3
  12.9 0.7 constant_dynamic-update-slice_fusion.2
  13.6 0.7 constant_dynamic-update-slice_fusion.1
  14.4 0.7 constant_dynamic-update-slice_fusion.refs_2_
  15.1 4.9 constant_dynamic-slice_fusion
  20.0 0.4 copy.65
  20.4 1.2 pad.22.refs_1_
  21.6 0.4 copy.66
  22.0 1.1 pad.21.refs_0_
  23.1 191.8 %forward_layers.1 = (bf16[6,4,256,1024]{3,2,1,0:T(8,128)(2,1)}, f32[2,8,1024]{2,1,0:T(8,128)}, bf16[2,2,2,608,1024]{4,3,2,1,0:T(8,128)(2,1)}, bf16[2,2,2,608,102...) custom-call(bf16[608,1024]{1,0:T(8,128)(2,1)} %pad.21.refs_0_, ...), custom_call_target="tpu_custom_call" | custom-call | tf_op jit(solution)/shard_map/forward_layers/pallas_call | solution.py:643
  214.9 248.7 %backward_layers.1 = (bf16[2,608,1024]{2,1,0:T(8,128)(2,1)}, bf16[2,608,1024]{2,1,0:T(8,128)(2,1)}, bf16[6,4,256,128]{3,2,1,0:T(8,128)(2,1)}, bf16[1,4,32,128]{3,2,1,0:T(8,128)(2,1)}) custom-call(bf16[6,4,256,1024]{3,2,1,0:T(8,128)(2,1)} %get-tuple-element.26.refs_0_, f32[2,8,1024]{2,1,0:T(8,128)} %get-tuple-element.27.refs_1_, ...), custom_call_target="tpu_custom_call" | custom-call | tf_op jit(solution)/shard_map/backward_layers/pallas_call | solution.py:1407
  463.6 0.7 slice.121
  464.3 0.1 reshape.67
  464.4 0.7 reshape.68
  465.2 0.6 reshape.69
  465.8 0.8 convert.3
  466.6 0.6 slice.125
  467.2 0.6 slice.126
  467.8 2.2 slice_convert_fusion.1
  470.0 5.8 %copy.53 = f32[2,577,1024]{2,0,1:T(2,128)} copy(f32[2,577,1024]{2,1,0:T(8,128)S(1)} %slice_convert_fusion.1) | data formatting | bytes 9453568
  475.8 1.3 fusion.14
  477.2 1.3 copy.58
  478.5 0.7 slice_bitcast_fusion.1
  479.3 1.1 copy.55
  480.5 0.5 slice_convert_fusion
  481.0 5.8 %copy.54 = f32[2,577,1024]{2,0,1:T(2,128)} copy(f32[2,577,1024]{2,1,0:T(8,128)S(1)} %slice_convert_fusion) | data formatting | bytes 9453568
  (30 shorter events, 0.5 us)
Async XLA Ops:
  0.6 6.7 %copy-start.4 = (bf16[2,128,1024]{2,1,0:T(8,128)(2,1)S(1)}, bf16[2,128,1024]{2,1,0:T(8,128)(2,1)}, u32[]{:S(2)}) copy-start(bf16[2,128,1024]{2,1,0:T(8,128)(2,1)} %param.14) | copy-start | bytes 1572868
  8.2 6.9 %copy-start.1 = (bf16[2,577,1024]{2,0,1:T(2,128)(2,1)S(1)}, bf16[2,577,1024]{2,0,1:T(2,128)(2,1)}, u32[]{:S(2)}) copy-start(bf16[2,577,1024]{2,0,1:T(2,128)(2,1)} %param.11) | copy-start | bytes 7090180
  9.5 5.6 %copy-start.2 = (bf16[2,577,1024]{2,0,1:T(2,128)(2,1)S(1)}, bf16[2,577,1024]{2,0,1:T(2,128)(2,1)}, u32[]{:S(2)}) copy-start(bf16[2,577,1024]{2,0,1:T(2,128)(2,1)} %param.10) | copy-start | bytes 7090180
  470.0 5.8 %copy-start = (bf16[6,4,256,128]{3,2,1,0:T(8,128)(2,1)S(1)}, bf16[6,4,256,128]{3,2,1,0:T(8,128)(2,1)}, u32[]{:S(2)}) copy-start(bf16[6,4,256,128]{3,2,1,0:T(8,128)(2,1)} %get-tuple-element.40) | copy-start | bytes 4718596
  478.5 2.0 copy-start.3

commit v5 on v4

--- a/solution.py
+++ b/solution.py
@@ -86,34 +86,35 @@
 
 
 class Gather:
-    def __init__(self, spot, packed, whole, role_sems, plane_sems, block_sems, base, local_sem, direct):
-        self.spot, self.packed, self.whole, self.direct = spot, packed, whole, direct
+    def __init__(self, spot, source, whole, role_sems, plane_sems, block_sems, base, local_sem, direct):
+        self.spot, self.source, self.whole, self.direct = spot, source, whole, direct
         self.role_sems, self.plane_sems, self.block_sems = role_sems, plane_sems, block_sems
         self.base, self.local_sem = base, local_sem
+        self.blocks_first = ()
         self.cols = D // spot.blocks // TP
         self.span = D // spot.blocks
 
     def piece(self, g, plane, block):
-        return self.whole.at[g, plane, :, lanes(block * self.span, self.span)]
+        return self.whole.at[g, plane, :, :, lanes(block * self.span, self.span)]
 
     def own(self, g):
         spot = self.spot
         if self.direct:
             return pltpu.make_async_copy(
-                self.packed.at[g, spot.role],
-                self.whole.at[g, spot.plane, :, lanes(spot.index * self.cols, self.cols)],
+                self.source(g, spot.role),
+                self.whole.at[g, spot.plane, :, :, lanes(spot.index * self.cols, self.cols)],
                 self.local_sem.at[self.base + g],
             )
         return pltpu.make_async_copy(
-            self.packed.at[g], self.piece(g, spot.plane, spot.block), self.local_sem.at[self.base + g]
+            self.source(g, None), self.piece(g, spot.plane, spot.block), self.local_sem.at[self.base + g]
         )
 
     def to_role(self, g, o):
         spot = self.spot
         other = flip(spot.role, o)
         return send(
-            self.packed.at[g, other],
-            self.whole.at[g, spot.plane, :, lanes(spot.index * self.cols, self.cols)],
+            self.source(g, other),
+            self.whole.at[g, spot.plane, :, :, lanes(spot.index * self.cols, self.cols)],
             self.role_sems,
             (self.base + g, o),
             spot.at(role=other),
@@ -123,7 +124,7 @@
         spot = self.spot
         other = flip(spot.role, o)
         place = self.whole.at[
-            g, spot.plane, :, lanes((spot.block * TP + other) * self.cols, self.cols)
+            g, spot.plane, :, :, lanes((spot.block * TP + other) * self.cols, self.cols)
         ]
         return send(place, place, self.role_sems, (self.base + g, o), spot.at(role=other))
 
@@ -131,7 +132,7 @@
         plane = self.spot.plane
         step = 1 if up else -1
         piece = plane - step * d if taken else plane - step * (d - 1)
-        place = self.piece(g, piece, self.spot.block)
+        place = self.whole.at[g, piece] if g in self.blocks_first else self.piece(g, piece, self.spot.block)
         other = plane - step if taken else plane + step
         return send(
             place, place, self.plane_sems, (self.base + g, d - 1 + (0 if up else 3)), self.spot.at(plane=other)
@@ -173,9 +174,15 @@
         if self.direct:
             for o in (1, 2, 3):
                 self.from_role(g, o).wait_recv()
-        self.onward(g, 0)
+        if g not in self.blocks_first:
+            self.onward(g, 0)
         for s in range(1, self.spot.blocks):
             self.to_block(g, s, 0, True).start()
+
+    def lift(self, g):
+        for s in range(1, self.spot.blocks):
+            self.to_block(g, s, 0, True, True).wait_recv()
+        self.onward(g, 0)
 
     def relay(self, g, d):
         for up in (True, False):
@@ -183,6 +190,8 @@
             def _():
                 self.hop(g, d, up, True).wait_recv()
         self.onward(g, d)
+        if g in self.blocks_first:
+            return
         for up in (True, False):
             @pl.when(self.has(d, up))
             def _():
@@ -207,7 +216,7 @@
                     @pl.when(self.goes(d, up))
                     def _():
                         self.hop(g, d + 1, up, False).wait_send()
-                if d > 0:
+                if d > 0 and g not in self.blocks_first:
                     @pl.when(self.has(d, up))
                     def _():
                         for s in range(1, self.spot.blocks):
@@ -272,24 +281,26 @@
     lax.fori_loop(0, rows // size, one, 0, unroll=unroll)
 
 
-def unit_picks(held, fsdp):
+def unit_picks(held, fsdp, role):
     cols = D // fsdp
     per = HD // fsdp
-    for first, count, offset in ((0, 256, 2 * per), (256, HD, 0), (256 + HD, HD, per)):
+    bits = fsdp.bit_length() - 1
+    for first, count, offset in (
+        (0, 256, role * (4 * per)), (256, HD, role * per), (256 + HD, HD, TP * per + role * per)
+    ):
         unit = lax.broadcasted_iota(jnp.int32, (count, D), 0)
         place = lax.broadcasted_iota(jnp.int32, (count, D), 1)
-        bits = fsdp.bit_length() - 1
-        wanted = (unit & (fsdp - 1)) * cols + offset + (unit >> bits)
+        wanted = (unit & (fsdp - 1)) * cols + (unit >> bits) + offset
         held[first : first + count] = jnp.where(place == wanted, 1.0, 0.0).astype(bf16)
 
 
 def forward_kernel(cfg, *refs):
     fsdp, head, tokens, rows, direct = cfg
     (
-        own_image, own_cot, packed, extras,
+        images, cotangents, attn_source, in_source, down_source, extras,
         weights_out, vec_out, normed_out, unit_out, inverse_out, qkv_out, att_out, lse_out, hidden_out,
         stream_out, chip_out, cot_out,
-        whole, extra, vec, pair, cots, stream, normed, unit, inverse, qkv, scores, soft, att_sum, att,
+        whole, extra, vec, pair, cots, stream, normed, unit, inverse, qkv, att_sum, att,
         values, lse_rows, low_hidden, active, kept,
         sent, core_in, chip, side_in, full,
         role_s, role_r, plane_s, plane_r, block_s, block_r, local_sem,
@@ -300,8 +311,18 @@
     groups = 3 * LAYERS
     greet(spot.partners())
     sems = ((role_s, role_r), (plane_s, plane_r), (block_s, block_r))
-    small = Gather(spot, extras, extra, *sems, groups, local_sem, direct)
-    large = Gather(spot, packed, whole, *sems, 0, local_sem, direct)
+
+    def source(g, role):
+        l, k = g // 3, g % 3
+        held = (attn_source, in_source, down_source)[k]
+        if role is None:
+            return held.at[l]
+        return held.at[l, :, role] if k == 0 else held.at[l, role]
+
+    small = Gather(spot, lambda g, role: extras, extra, *sems, groups, local_sem, direct)
+    large = Gather(spot, source, whole, *sems, 0, local_sem, direct)
+    large.blocks_first = (groups - 1,)
+    own_image, own_cot = images.at[spot.plane // 2], cotangents.at[spot.plane // 2]
     exchange = Exchange(
         spot, sent, core_in, chip, side_in, full, (core_s, core_r), (side_s, side_r), (back_s, back_r)
     )
@@ -365,27 +386,29 @@
     large.relay(0, 3)
     large.relay(1, 1)
     large.spread(2)
+    large.spread(5)
     share_end(own_image, pair, 0)
     small.complete(0)
 
-    unit_picks(active, fsdp)
+    unit_picks(active, fsdp, spot.role)
     for l in range(LAYERS):
-        vec[l, 0:6] = extra[0, 0, 16 * l : 16 * l + 16].astype(f32)[0:6]
+        vec[l, 0:6] = extra[0, 0, 0, 16 * l : 16 * l + 16].astype(f32)[0:6]
         for plane in range(4):
-            units = dot(extra[0, plane, 16 * l : 16 * l + 16], active[0:384], 1, 1)[6:7]
-            vec[l, 6:7, plane * 256 : plane * 256 + 256] = units[:, 0:256]
+            units = dot(extra[0, plane, 0, 16 * l : 16 * l + 16], active[0:384], 1, 1)
+            vec[l, 6:7, plane * 256 : plane * 256 + 256] = units[6:7, 0:256]
             if plane % 2 == 0:
                 before = units
             else:
                 for k in range(2):
                     at = slice(256 + k * HD, 256 + k * HD + HD)
                     to = k * 256 + (plane - 1) * HD
-                    vec[l, 7:8, to : to + 128] = jnp.concatenate([before[:, at], units[:, at]], axis=1)
+                    vec[l, 7:8, to : to + 128] = jnp.concatenate([before[7:8, at], units[7:8, at]], axis=1)
     store_vec = pltpu.make_async_copy(vec, vec_out, store_sem.at[28])
     store_vec.start()
     large.complete(0)
 
-    lane_head = lax.broadcasted_iota(jnp.int32, (1, 256), 1) // HD
+    lane_pair = lax.broadcasted_iota(jnp.int32, (1, 128), 1) // HD
+    valid = lax.broadcasted_iota(jnp.int32, (rows, 1), 0) < tokens
 
     def stores(l, n, i):
         return [
@@ -435,7 +458,7 @@
             store_lse.wait()
 
         for k in range(3):
-            w = whole[g, :, k * HD : k * HD + HD].reshape(256, D)
+            w = whole[g, :, k].reshape(256, D)
             part = dot(normed[i], w, 1, 1)
             if k == 0:
                 part = part + vec[l, 7:8, 0:256]
@@ -444,20 +467,18 @@
                 values[...] = jnp.transpose(part).astype(bf16)
             qkv[:, k * 256 : k * 256 + 256] = part.astype(bf16)
         store_qkv.start()
-        edge = tokens // 16 * 16
-        late = lax.broadcasted_iota(jnp.int32, (rows - edge, 1), 0) + edge >= tokens
-
         def one_head(h, carry):
-            low_mask = jnp.where(lane_head == h, HD ** (-0.5), 0.0).astype(bf16)
-            scores[...] = dot(qkv[:, 256:512], qkv[:, 0:256] * low_mask, 1, 1)
-            scores[edge:rows] = jnp.where(late, -1e30, scores[edge:rows])
-            largest = jnp.max(scores[...], axis=0, keepdims=True)
-            e = jnp.exp(scores[...] - largest)
+            two = lanes(h // 2 * 128, 128)
+            key_two = lanes(256 + h // 2 * 128, 128)
+            low_mask = jnp.where(lane_pair == h % 2, HD ** (-0.5), 0.0).astype(bf16)
+            s = dot(qkv[:, key_two], qkv[:, two] * low_mask, 1, 1)
+            s = jnp.where(valid, s, -1e30)
+            largest = jnp.max(s, axis=0, keepdims=True)
+            e = jnp.exp(s - largest)
             total = jnp.sum(e, axis=0, keepdims=True)
-            soft[...] = e.astype(bf16)
             lse_rows[i, pl.ds(h, 1)] = largest + jnp.log(total)
             at = pl.ds(pl.multiple_of(h * HD, HD), HD)
-            att_sum[at] = dot(values[at], soft[...], 1, 0) * (1.0 / total)
+            att_sum[at] = dot(values[at], e.astype(bf16), 1, 0) * (1.0 / total)
             return carry
 
         lax.fori_loop(0, 4, one_head, 0)
@@ -465,7 +486,7 @@
         store_att.start()
         store_lse.start()
         exchange.reduce(
-            i, lambda at: dot(att[i], whole[g, :, 192:256, at].reshape(256, HALF), 1, 0), kept
+            i, lambda at: dot(att[i], whole[g, :, 3, :, at].reshape(256, HALF), 1, 0), kept
         )
         exchange.side_copy(i, 0).start()
 
@@ -483,16 +504,17 @@
 
         for k in range(4):
             at = slice(k * 256, k * 256 + 256)
-            v = dot(normed[i], whole[g + 1, k], 1, 1) + vec[l, 6:7, at]
+            v = dot(normed[i], whole[g + 1, k].reshape(256, D), 1, 1) + vec[l, 6:7, at]
             low_hidden[i, :, at] = v.astype(bf16)
             active[:, at] = (v * (0.5 + 0.5 * lax.erf(v * (0.5**0.5)))).astype(bf16)
         store_hidden.start()
 
-        @pl.when(i == 0)
+        @pl.when(jnp.logical_and(i == 0, l < LAYERS - 1))
         def _():
             large.complete(g + 2)
 
-        exchange.reduce(i, lambda at: dot(active[...], whole[g + 2, :, :, at].reshape(D, HALF), 1, 0), kept)
+
+        exchange.reduce(i, lambda at: dot(active[...], whole[g + 2, :, :, :, at].reshape(D, HALF), 1, 0), kept)
 
         @pl.when(l < LAYERS - 1)
         def _():
@@ -513,20 +535,23 @@
         def _():
             large.complete(g)
 
-        attn_stage(l, 0)
-
-        @pl.when(l == 0)
-        def _():
-            share_begin(own_cot, cots, 1)
-            large.relay(1, 2)
-            large.relay(2, 1)
-            large.spread(3)
-
-        @pl.when(l > 0)
-        def _():
-            large.relay(5, 3)
-
-        attn_stage(l, 1)
+        def attn_image(i, carry):
+            attn_stage(l, i)
+
+            @pl.when(jnp.logical_and(l == 0, i == 0))
+            def _():
+                share_begin(own_cot, cots, 1)
+                large.relay(1, 2)
+                large.relay(2, 1)
+                large.spread(3)
+
+            @pl.when(jnp.logical_and(l > 0, i == 0))
+            def _():
+                large.relay(5, 3)
+
+            return carry
+
+        lax.fori_loop(0, 2, attn_image, 0)
 
         @pl.when(l == 0)
         def _():
@@ -535,23 +560,27 @@
             large.relay(3, 1)
             large.spread(4)
             large.relay(2, 3)
+            large.lift(5)
 
         large.complete(g + 1)
-        mlp_stage(l, 0)
+
+        def mlp_image(i, carry):
+            mlp_stage(l, i)
+
+            @pl.when(jnp.logical_and(l == 0, i == 0))
+            def _():
+                large.relay(3, 2)
+                large.relay(4, 1)
+                large.relay(3, 3)
+                large.relay(5, 1)
+
+            return carry
+
+        lax.fori_loop(0, 2, mlp_image, 0)
 
         @pl.when(l == 0)
         def _():
-            large.relay(3, 2)
-            large.relay(4, 1)
-            large.spread(5)
-            large.relay(3, 3)
-
-        mlp_stage(l, 1)
-
-        @pl.when(l == 0)
-        def _():
             large.relay(4, 2)
-            large.relay(5, 1)
             large.relay(4, 3)
             large.relay(5, 2)
 
@@ -576,23 +605,20 @@
     store_vec.wait()
     store_cots.wait()
 
-    def finish_group(g, carry):
+    for g in range(groups):
         store_weights(g).wait()
         large.drain(g)
-        return carry
-
-    lax.fori_loop(0, groups, finish_group, 0)
     small.drain(0)
 
 
-def forward_call(fsdp, head, tokens, rows, direct, own_image, own_cot, packed, extras):
+def forward_call(fsdp, head, tokens, rows, direct, *operands):
     groups = 3 * LAYERS
     blocks = fsdp // TP
     anyspace = pl.BlockSpec(memory_space=pl.ANY)
     shape = jax.ShapeDtypeStruct
     dma = pltpu.SemaphoreType.DMA
     out_shape = (
-        shape((groups, 4, 256, D), bf16),
+        shape((groups, 4, 4, HD, D), bf16),
         shape((LAYERS, 8, D), f32),
         shape((LAYERS, 2, 2, rows, D), bf16),
         shape((LAYERS, 2, 2, rows, D), bf16),
@@ -606,8 +632,8 @@
         shape((2, rows, D), bf16),
     )
     scratch = [
-        pltpu.VMEM((groups, 4, 256, D), bf16),
-        pltpu.VMEM((1, 4, 32, D), bf16),
+        pltpu.VMEM((groups, 4, 4, HD, D), bf16),
+        pltpu.VMEM((1, 4, 1, 32, D), bf16),
         pltpu.VMEM((LAYERS, 8, D), f32),
         pltpu.VMEM((2, rows, D), bf16),
         pltpu.VMEM((2, rows, D), bf16),
@@ -616,8 +642,6 @@
         pltpu.VMEM((2, rows, D), bf16),
         pltpu.VMEM((2, rows, 128), f32),
         pltpu.VMEM((rows, 768), bf16),
-        pltpu.VMEM((rows, rows), f32),
-        pltpu.VMEM((rows, rows), bf16),
         pltpu.VMEM((256, rows), f32),
         pltpu.VMEM((2, rows, 256), bf16),
         pltpu.VMEM((256, rows), bf16),
@@ -643,14 +667,14 @@
     return pl.pallas_call(
         functools.partial(forward_kernel, (fsdp, head, tokens, rows, direct)),
         out_shape=out_shape,
-        in_specs=[anyspace] * 4,
+        in_specs=[anyspace] * len(operands),
         out_specs=tuple(anyspace for _ in out_shape),
         scratch_shapes=scratch,
         compiler_params=pltpu.CompilerParams(
             collective_id=0, has_side_effects=True, vmem_limit_bytes=60 << 20
         ),
         name="forward_layers",
-    )(own_image, own_cot, packed, extras)
+    )(*operands)
 
 
 class Scatter:
@@ -670,46 +694,53 @@
     def third(self, n):
         return n % self.total.shape[0]
 
-    def to_block(self, n, s):
+    def rows(self, part):
+        units = self.term.shape[2]
+        return slice(0, units) if part is None else slice(part * units // 2, (part + 1) * units // 2)
+
+    def to_block(self, n, s, part=None):
         block = (self.spot.block + s) % self.spot.blocks
-        a = self.slot(n)
+        a, r = self.slot(n), self.rows(part)
         return send(
-            self.term.at[a, :, :, lanes(block * self.span, self.span)],
-            self.block_in.at[a, s - 1],
-            self.block_sems, (a, s - 1), self.spot.at(block=block),
+            self.term.at[a, :, r, lanes(block * self.span, self.span)],
+            self.block_in.at[a, s - 1, :, r],
+            self.block_sems, (a, s - 1, part or 0), self.spot.at(block=block),
         )
 
-    def along(self, n, plane, up):
+    def along(self, n, plane, up, part=None):
         planes = self.spot.planes
         a, c = self.slot(n), self.third(n)
         first, number = (plane + 1, planes - 1 - plane) if up else (0, plane)
-        way = 0 if up else 1
+        way, r = 0 if up else 1, self.rows(part)
         return send(
-            self.total.at[c, first : first + number], self.plane_in.at[a, way, 0:number],
-            self.plane_sems, (c, way), self.spot.at(plane=plane + (1 if up else -1)),
+            self.total.at[c, first : first + number, r], self.plane_in.at[a, way, 0:number, r],
+            self.plane_sems, (c, way, part or 0), self.spot.at(plane=plane + (1 if up else -1)),
         )
 
-    def to_role(self, n, o):
+    def to_role(self, n, o, part=None):
         other = flip(self.spot.role, o)
-        g = self.count - 1 - n
+        g, r = self.count - 1 - n, self.rows(part)
         return send(
-            self.mine.at[self.slot(n), :, lanes(other * self.cols, self.cols)], self.out.at[g, self.spot.role],
-            self.role_sems, (g, o), self.spot.at(role=other),
+            self.mine.at[self.slot(n), r, lanes(other * self.cols, self.cols)],
+            self.out.at[g, self.spot.role, r],
+            self.role_sems, (g, o, part or 0), self.spot.at(role=other),
         )
 
-    def from_role(self, g, o):
+    def from_role(self, g, o, part=None):
         other = flip(self.spot.role, o)
-        place = self.out.at[g, other]
-        return send(place, place, self.role_sems, (g, o), self.spot.at(role=other))
-
-    def keep(self, n):
-        g = self.count - 1 - n
+        place = self.out.at[g, other, self.rows(part)]
+        return send(place, place, self.role_sems, (g, o, part or 0), self.spot.at(role=other))
+
+    def keep(self, n, part=None):
+        g, r = self.count - 1 - n, self.rows(part)
         if self.direct:
             return pltpu.make_async_copy(
-                self.mine.at[self.slot(n), :, lanes(self.spot.role * self.cols, self.cols)],
-                self.out.at[g, self.spot.role], self.local_sem.at[g],
+                self.mine.at[self.slot(n), r, lanes(self.spot.role * self.cols, self.cols)],
+                self.out.at[g, self.spot.role, r], self.local_sem.at[g, part or 0],
             )
-        return pltpu.make_async_copy(self.mine.at[self.slot(n)], self.out.at[g], self.local_sem.at[g])
+        return pltpu.make_async_copy(
+            self.mine.at[self.slot(n), r], self.out.at[g, r], self.local_sem.at[g, part or 0]
+        )
 
     def before_terms(self, n):
         @pl.when(n >= 2)
@@ -717,44 +748,47 @@
             for s in range(1, self.spot.blocks):
                 self.to_block(n - 2, s).wait_send()
 
-    def send_terms(self, n):
+    def send_terms(self, n, parts=(None,)):
         for s in range(1, self.spot.blocks):
             @pl.when(n >= 2)
             def _():
                 pl.semaphore_wait(self.block_free.at[self.slot(n), s - 1], 1)
 
-            self.to_block(n, s).start()
-
-    def pass_on(self, n, plane, up):
-        @pl.when(n >= 2)
-        def _():
-            pl.semaphore_wait(self.plane_free.at[self.slot(n), 0 if up else 1], 1)
-
-        self.along(n, plane, up).start()
-
-    def sent_along(self, n):
+            for part in parts:
+                self.to_block(n, s, part).start()
+
+    def pass_on(self, n, plane, up, part=None):
+        if not part:
+            @pl.when(n >= 2)
+            def _():
+                pl.semaphore_wait(self.plane_free.at[self.slot(n), 0 if up else 1], 1)
+
+        self.along(n, plane, up, part).start()
+
+    def sent_along(self, n, part=None):
         for plane in range(self.spot.planes):
             @pl.when(self.spot.plane == plane)
             def _():
                 if plane < self.spot.planes - 1:
-                    self.along(n, plane, True).wait_send()
+                    self.along(n, plane, True, part).wait_send()
                 if plane > 0:
-                    self.along(n, plane, False).wait_send()
-
-    def sum_blocks(self, n):
-        a, c = self.slot(n), self.third(n)
+                    self.along(n, plane, False, part).wait_send()
+
+    def sum_blocks(self, n, part=None):
+        a, c, r = self.slot(n), self.third(n), self.rows(part)
         for s in range(1, self.spot.blocks):
-            self.to_block(n, s).wait_recv()
-
-        @pl.when(n >= 3)
-        def _():
-            self.sent_along(n - 3)
+            self.to_block(n, s, part).wait_recv()
+
+        if not part:
+            @pl.when(n >= 3)
+            def _():
+                self.sent_along(n - 3)
 
         for plane in range(self.spot.planes):
-            value = self.term[a, plane, :, self.own].astype(f32)
+            value = self.term[a, plane, r, self.own].astype(f32)
             for s in range(1, self.spot.blocks):
-                value = value + self.block_in[a, s - 1, plane].astype(f32)
-            self.total[c, plane] = value.astype(bf16)
+                value = value + self.block_in[a, s - 1, plane, r].astype(f32)
+            self.total[c, plane, r] = value.astype(bf16)
 
         @pl.when(n + 2 < self.count)
         def _():
@@ -768,20 +802,20 @@
 
         @pl.when(self.spot.plane == 0)
         def _():
-            self.pass_on(n, 0, True)
+            self.pass_on(n, 0, True, part)
 
         @pl.when(self.spot.plane == last)
         def _():
-            self.pass_on(n, last, False)
-
-    def take(self, n, plane, up):
-        a, c = self.slot(n), self.third(n)
+            self.pass_on(n, last, False, part)
+
+    def take(self, n, plane, up, part):
+        a, c, r = self.slot(n), self.third(n), self.rows(part)
         before = plane - 1 if up else plane + 1
-        self.along(n, before, up).wait_recv()
+        self.along(n, before, up, part).wait_recv()
         planes = range(plane, self.spot.planes) if up else range(0, plane + 1)
         for at, p in enumerate(planes):
-            value = self.total[c, p].astype(f32) + self.plane_in[a, 0 if up else 1, at].astype(f32)
-            self.total[c, p] = value.astype(bf16)
+            value = self.total[c, p, r].astype(f32) + self.plane_in[a, 0 if up else 1, at, r].astype(f32)
+            self.total[c, p, r] = value.astype(bf16)
 
         @pl.when(n + 2 < self.count)
         def _():
@@ -790,44 +824,49 @@
             )
 
         if (up and plane < self.spot.planes - 1) or (not up and plane > 0):
-            self.pass_on(n, plane, up)
-
-    def hop(self, n, d):
+            self.pass_on(n, plane, up, part)
+
+    def hop(self, n, d, part=None):
         for plane, up in ((d, True), (self.spot.planes - 1 - d, False)):
             @pl.when(self.spot.plane == plane)
             def _():
-                self.take(n, plane, up)
-
-    def hand_out(self, n):
-        a = self.slot(n)
-
-        @pl.when(n >= 2)
-        def _():
-            self.keep(n - 2).wait()
-            if self.direct:
-                for o in (1, 2, 3):
-                    self.to_role(n - 2, o).wait_send()
-
-        self.mine[a] = self.total[self.third(n), self.spot.plane]
-        self.keep(n).start()
+                self.take(n, plane, up, part)
+
+    def hand_out(self, n, part=None):
+        a, r = self.slot(n), self.rows(part)
+
+        if not part:
+            @pl.when(n >= 2)
+            def _():
+                self.keep(n - 2).wait()
+                if self.direct:
+                    for o in (1, 2, 3):
+                        self.to_role(n - 2, o).wait_send()
+
+        self.mine[a, r] = self.total[self.third(n), self.spot.plane, r]
+        self.keep(n, part).start()
         if self.direct:
             for o in (1, 2, 3):
-                self.to_role(n, o).start()
-
-    def finish(self):
-        for n in range(max(0, self.count - 3), self.count):
-            self.sent_along(n)
-        for n in range(max(0, self.count - 2), self.count):
-            self.keep(n).wait()
-            for s in range(1, self.spot.blocks):
-                self.to_block(n, s).wait_send()
-            if self.direct:
-                for o in (1, 2, 3):
-                    self.to_role(n, o).wait_send()
+                self.to_role(n, o, part).start()
+
+    def finish(self, parts=(None,)):
+        last = self.count - 1
+        for n in range(max(0, last - 2), last + 1):
+            for part in parts if n == last else (None,):
+                self.sent_along(n, part)
+        for n in range(max(0, last - 1), last + 1):
+            for part in parts if n == last else (None,):
+                self.keep(n, part).wait()
+                for s in range(1, self.spot.blocks):
+                    self.to_block(n, s, part).wait_send()
+                if self.direct:
+                    for o in (1, 2, 3):
+                        self.to_role(n, o, part).wait_send()
         if self.direct:
             for g in range(self.count):
                 for o in (1, 2, 3):
-                    self.from_role(g, o).wait_recv()
+                    for part in parts if g == 0 else (None,):
+                        self.from_role(g, o, part).wait_recv()
 
 
 def backward_kernel(cfg, *refs):
@@ -836,7 +875,7 @@
         weights_in, vec_in, normed_in, unit_in, inverse_in, qkv_in, att_in, lse_in, hidden_in,
         stream_in, chip_in, cot_in,
         out_pair, in_pair, grads, small_grads,
-        weight, vec, up, up_low, hid, gh, normed, unit, inverse, qkv, att, lse, big, soft, low_scores, gab, along,
+        weight, vec, up, up_low, hid, gh, normed, unit, inverse, qkv, att, lse, big, grad_rows, flipped, gab, along,
         sent, core_in, chip, side_in, full, last_in, result, sums, unit_sums,
         term, block_in, total, plane_in, mine,
         small_term, small_block_in, small_total, small_plane_in, small_mine,
@@ -960,7 +999,8 @@
             for copy in outs:
                 copy.wait_send()
 
-    chunks = [(start, min(160, rows - start)) for start in range(0, rows, 160)]
+    chunks = [(start, min(160, rows - start)) for start in range(0, 640, 160)]
+    assert sum(size for _, size in chunks) == rows
     last_plane = spot.planes - 1
 
     def line_copy(s, j, up, first):
@@ -1001,18 +1041,17 @@
 
                 line_ways(s, act)
 
-    def line_relay():
-        for j in range(len(chunks)):
-            for s in range(2):
-                @pl.when(spot.plane != 2 * s + spot.core)
-                def _():
-                    line_copy(s, j, True, False).wait_recv()
-
-                def act(up, first):
-                    if not first:
-                        line_copy(s, j, up, False).start()
-
-                line_ways(s, act)
+    def line_relay(j):
+        for s in range(2):
+            @pl.when(spot.plane != 2 * s + spot.core)
+            def _():
+                line_copy(s, j, True, False).wait_recv()
+
+            def act(up, first):
+                if not first:
+                    line_copy(s, j, up, False).start()
+
+            line_ways(s, act)
 
     def line_end():
         for s in range(2):
@@ -1039,7 +1078,7 @@
             sums[base + 2 + n] += eights(g)
             sums[base + 4 if n == 1 else base - 1] += eights(v)
 
-    def mlp_stage(l, i):
+    def mlp_stage(l, i, n):
         @pl.when(l < top)
         def _():
             exchange.finish(i, 1)
@@ -1051,27 +1090,30 @@
             load_weight(l, 2).wait()
 
         for k in range(4):
-            big[:, k * 256 : k * 256 + 256] = dot(up_low[i], weight[2, k], 1, 1)
-
-        def step(r):
-            v = hid[i, r].astype(f32)
+            at = slice(k * 256, k * 256 + 256)
+            grad_active = dot(up_low[i], weight[2, k].reshape(256, D), 1, 1)
+            v = hid[i, :, at].astype(f32)
             below = 0.5 + 0.5 * lax.erf(v * (0.5**0.5))
             slope = below + v * jnp.exp(-0.5 * v * v) * (1.0 / math.sqrt(2.0 * math.pi))
-            hid[i, r] = (v * below).astype(bf16)
-            low_grad = (big[r, 0:D] * slope).astype(bf16)
-            gh[i, r] = low_grad
-            unit_sums[l, 0] += eights(low_grad.astype(f32))
-
-        each_rows(rows, 16, step, unroll=2)
+            hid[i, :, at] = (v * below).astype(bf16)
+            low_grad = (grad_active * slope).astype(bf16)
+            gh[i, :, at] = low_grad
+            unit_sums[l, 0, :, at] += eights(low_grad.astype(f32))
+
+        @pl.when(i == 1)
+        def _():
+            scatter.before_terms(n)
+            unit_term(scatter.slot(n), hid, up_low)
+            scatter.send_terms(n)
 
         @pl.when(i == 0)
         def _():
             load_weight(l, 1).wait()
 
-        exchange.reduce(i, lambda at: dot(gh[i], weight[1, :, :, at].reshape(D, HALF), 1, 0), kept)
+        exchange.reduce(i, lambda at: dot(gh[i], weight[1, :, :, :, at].reshape(D, HALF), 1, 0), kept)
         exchange.side_copy(i, 0).start()
 
-    lane_head = lax.broadcasted_iota(jnp.int32, (1, 256), 1) // HD
+    lane_pair = lax.broadcasted_iota(jnp.int32, (1, 128), 1) // HD
     valid = lax.broadcasted_iota(jnp.int32, (rows, 1), 0) < tokens
     head_rows = jnp.where(
         lax.broadcasted_iota(jnp.int32, (16, 256), 1) // HD == lax.broadcasted_iota(jnp.int32, (16, 256), 0), 1.0, 0.0
@@ -1093,45 +1135,32 @@
             for copy in load_attn(l):
                 copy.wait()
 
-        gab[...] = dot(up_low[i], weight[0, :, 192:256].reshape(256, D), 1, 1).astype(bf16)
+        gab[...] = dot(up_low[i], weight[0, :, 3].reshape(256, D), 1, 1).astype(bf16)
         product = gab[...].astype(f32) * att[i].astype(f32)
         high = product.astype(bf16)
         rest = (product - high.astype(f32)).astype(bf16)
         along[...] = dot(head_rows, high, 1, 1) + dot(head_rows, rest, 1, 1)
 
+        flipped[0:256] = jnp.transpose(qkv[i, :, 256:512])
+        flipped[256:512] = jnp.transpose(qkv[i, :, 0:256])
+        flipped[512:768] = jnp.transpose(gab[...])
         def one_head(h, carry):
-            mask = jnp.where(lane_head == h, 1.0, 0.0)
-            low_mask = mask.astype(bf16)
-            q = qkv[i, :, 0:256] * low_mask
-            big[:, 0:rows] = dot(qkv[i, :, 256:512], q * (HD ** (-0.5)), 1, 1)
-            big[:, 640 : 640 + rows] = dot(qkv[i, :, 512:768], gab[...] * low_mask, 1, 1)
-            lse_row = lse[i, pl.ds(h, 1)]
-            along_row = along[pl.ds(h, 1)]
-
-            p = jnp.exp(big[:, 0:rows] - lse_row)
+            two, key_two, value_two = [lanes(m * 256 + h // 2 * 128, 128) for m in range(3)]
+            low_mask = jnp.where(lane_pair == h % 2, 1.0, 0.0).astype(bf16)
+            q = qkv[i, :, two] * (low_mask * HD ** (-0.5))
+            p = jnp.exp(dot(qkv[i, :, key_two], q, 1, 1) - lse[i, pl.ds(h, 1)])
             p = jnp.where(valid, p, 0.0)
-            soft[...] = p.astype(bf16)
-            low_scores[...] = (p * (big[:, 640 : 640 + rows] - along_row)).astype(bf16)
-            scale = HD ** (-0.5)
-            grad_q = dot(low_scores[...], qkv[i, :, 256:512], 0, 0) * (mask * scale)
-            grad_k = dot(low_scores[...], q, 1, 0) * (mask * scale)
-            grad_v = dot(soft[...], gab[...], 1, 0) * mask
-            for m, part in enumerate((grad_q, grad_k, grad_v)):
-                part = part.astype(bf16)
-                at = slice(m * 256, m * 256 + 256)
-
-                @pl.when(h == 0)
-                def _():
-                    gh[i, :, at] = part
-
-                @pl.when(h > 0)
-                def _():
-                    gh[i, :, at] = gh[i, :, at] + part
-
+            grad_p = dot(qkv[i, :, value_two], gab[:, two] * low_mask, 1, 1)
+            ds = (p * (grad_p - along[pl.ds(h, 1)])).astype(bf16)
+            at = [pl.ds(pl.multiple_of(m * 256 + h * HD, HD), HD) for m in range(3)]
+            grad_rows[at[0]] = (dot(flipped[at[0]], ds, 1, 0) * HD ** (-0.5)).astype(bf16)
+            grad_rows[at[1]] = (dot(flipped[at[1]], ds, 1, 1) * HD ** (-0.5)).astype(bf16)
+            grad_rows[at[2]] = dot(flipped[at[2]], p.astype(bf16), 1, 1).astype(bf16)
             return carry
 
         lax.fori_loop(0, 4, one_head, 0)
-
+        for m in range(3):
+            gh[i, :, m * 256 : m * 256 + 256] = jnp.transpose(grad_rows[m * 256 : m * 256 + 256])
         for m in (0, 2):
             at = slice(m * 256, m * 256 + 256)
             unit_sums[l, 1, :, at] += eights(gh[i, :, at].astype(f32))
@@ -1139,7 +1168,7 @@
 
         def partial(at):
             terms = [
-                dot(gh[i, :, m * 256 : m * 256 + 256], weight[0, :, m * HD : m * HD + HD, at].reshape(256, HALF), 1, 0)
+                dot(gh[i, :, m * 256 : m * 256 + 256], weight[0, :, m, :, at].reshape(256, HALF), 1, 0)
                 for m in range(3)
             ]
             return terms[0] + terms[1] + terms[2]
@@ -1177,7 +1206,7 @@
         n = 3 * step_index
 
         def mlp_image(i, carry):
-            mlp_stage(l, i)
+            mlp_stage(l, i, n)
 
             @pl.when(jnp.logical_and(again, i == 0))
             def _():
@@ -1222,16 +1251,14 @@
             for copy in load_unit(l, 1):
                 copy.start()
 
+        load_normed(l, 1).wait()
+
         @pl.when(again)
         def _():
             scatter.hop(n - 3, 2)
             scatter.sum_blocks(n - 1)
             scatter.hop(n - 2, 1)
 
-        scatter.before_terms(n)
-        unit_term(scatter.slot(n), hid, up_low)
-        scatter.send_terms(n)
-        load_normed(l, 1).wait()
         scatter.before_terms(n + 1)
         unit_term(scatter.slot(n + 1), gh, normed)
         scatter.send_terms(n + 1)
@@ -1274,7 +1301,14 @@
         scatter.sum_blocks(n)
         scatter.before_terms(n + 2)
         attn_term(scatter.slot(n + 2))
-        scatter.send_terms(n + 2)
+
+        @pl.when(more)
+        def _():
+            scatter.send_terms(n + 2)
+
+        @pl.when(jnp.logical_not(more))
+        def _():
+            scatter.send_terms(3 * LAYERS - 1, (0, 1))
 
         @pl.when(more)
         def _():
@@ -1291,10 +1325,6 @@
     lax.fori_loop(0, LAYERS, one_layer, 0)
 
     end = 3 * LAYERS
-    scatter.hop(end - 4, 3)
-    scatter.hand_out(end - 4)
-    scatter.sum_blocks(end - 2)
-
     def last_image(i, carry):
         exchange.finish(i, 1)
         norm_back(0, 0, i)
@@ -1303,7 +1333,7 @@
     lax.fori_loop(0, 2, last_image, 0)
     line_begin()
     picks = normed.at[0]
-    unit_picks(picks, fsdp)
+    unit_picks(picks, fsdp, spot.role)
     for l in range(LAYERS):
         features = [jnp.sum(sums[(l + 1) * 6 + n], axis=0, keepdims=True) for n in range(6)]
         inner = jnp.sum(unit_sums[l, 0], axis=0, keepdims=True)
@@ -1315,30 +1345,42 @@
                 qkv_sums[:, 512 + plane * HD : 512 + plane * HD + HD],
             ]
             values = jnp.broadcast_to(jnp.concatenate(parts, axis=1), (16, 384)).astype(bf16)
-            row = dot(values, picks[0:384], 1, 0)[0:1]
-            block = jnp.concatenate(features + [row, jnp.zeros((9, D), f32)], axis=0)
+            row = dot(values[:, 0:256], picks[0:256], 1, 0)[0:1]
+            other_row = dot(values[:, 256:384], picks[256:384], 1, 0)[0:1]
+            block = jnp.concatenate(features + [row, other_row, jnp.zeros((8, D), f32)], axis=0)
             small_term[0, plane, 16 * l : 16 * l + 16] = block.astype(bf16)
     small.send_terms(0)
+    scatter.hop(end - 4, 3)
+    scatter.hand_out(end - 4)
     scatter.hop(end - 3, 1)
+    line_relay(0)
+    scatter.sum_blocks(end - 2)
+    scatter.hop(end - 3, 2)
+    line_relay(1)
+    scatter.sum_blocks(end - 1, 0)
+    small.sum_blocks(0)
+    line_relay(2)
     scatter.hop(end - 2, 1)
-    scatter.hop(end - 3, 2)
-    scatter.sum_blocks(end - 1)
-    small.sum_blocks(0)
+    scatter.sum_blocks(end - 1, 1)
     scatter.hop(end - 3, 3)
     scatter.hand_out(end - 3)
+    line_relay(3)
     scatter.hop(end - 2, 2)
-    scatter.hop(end - 1, 1)
+    scatter.hop(end - 1, 1, 0)
     small.hop(0, 1)
     scatter.hop(end - 2, 3)
     scatter.hand_out(end - 2)
-    scatter.hop(end - 1, 2)
+    scatter.hop(end - 1, 1, 1)
+    scatter.hop(end - 1, 2, 0)
     small.hop(0, 2)
-    scatter.hop(end - 1, 3)
-    scatter.hand_out(end - 1)
+    scatter.hop(end - 1, 2, 1)
+    scatter.hop(end - 1, 3, 0)
+    scatter.hand_out(end - 1, 0)
+    scatter.hop(end - 1, 3, 1)
+    scatter.hand_out(end - 1, 1)
     small.hop(0, 3)
     small.hand_out(0)
-    line_relay()
-    scatter.finish()
+    scatter.finish((0, 1))
     small.finish()
     return_end(out_pair)
     line_end()
@@ -1359,7 +1401,7 @@
         shape((1, TP, 32, cols) if direct else (1, 32, span), bf16),
     )
     scratch = [
-        pltpu.VMEM((3, 4, 256, D), bf16),
+        pltpu.VMEM((3, 4, 4, HD, D), bf16),
         pltpu.VMEM((LAYERS, 8, D), f32),
         pltpu.VMEM((2, rows, D), f32),
         pltpu.VMEM((2, rows, D), bf16),
@@ -1371,9 +1413,9 @@
         pltpu.VMEM((2, rows, 768), bf16),
         pltpu.VMEM((2, rows, 256), bf16),
         pltpu.VMEM((2, 8, rows), f32),
-        pltpu.VMEM((rows, 640 + -(-rows // 128) * 128), f32),
-        pltpu.VMEM((rows, rows), bf16),
-        pltpu.VMEM((rows, rows), bf16),
+        pltpu.VMEM((rows, D), f32),
+        pltpu.VMEM((768, rows), bf16),
+        pltpu.VMEM((768, rows), bf16),
         pltpu.VMEM((rows, 256), bf16),
         pltpu.VMEM((16, rows), f32),
         pltpu.VMEM((2, rows, HALF), bf16),
@@ -1397,10 +1439,10 @@
     scratch += [dma((2,)), dma((2,)), dma((2, 2)), dma((2, 2)), dma((2,)), dma((2,))]
     for slots, thirds, count in ((2, 3, groups), (1, 1, 1)):
         scratch += [
-            dma((slots, blocks - 1)), dma((slots, blocks - 1)),
-            dma((thirds, 2)), dma((thirds, 2)),
-            dma((count, 4)), dma((count, 4)),
-            dma((count,)),
+            dma((slots, blocks - 1, 2)), dma((slots, blocks - 1, 2)),
+            dma((thirds, 2, 2)), dma((thirds, 2, 2)),
+            dma((count, 4, 2)), dma((count, 4, 2)),
+            dma((count, 2)),
             plain((slots, blocks - 1)), plain((slots, 2)),
         ]
     scratch += [dma((2,)), dma((2,)), dma((4,)), dma((4,)), dma((2, 4, 2)), dma((2, 4)), dma((16,)), dma((3,))]
@@ -1454,25 +1496,26 @@
 
 
 def pack_inputs(pl, w_qkv, w_out, w_in, w_down, qv_bias, in_bias, gains, shifts):
-    fsdp = lax.axis_size("fsdp")
     cols = w_qkv.shape[2]
-    groups = []
-    small = []
-    for l in range(LAYERS):
-        attn = jnp.concatenate([w_qkv[l].transpose(0, 2, 1), w_out[l][None]]).reshape(4, TP, HD, cols)
-        groups.append(attn.transpose(1, 0, 2, 3).reshape(TP, 256, cols))
-        groups.append(w_in[l].T.reshape(TP, 256, cols))
-        groups.append(w_down[l].reshape(TP, 256, cols))
-        features = jnp.concatenate([gains[l], shifts[l]])
-        features = jnp.broadcast_to(features[None], (TP, 6, cols))
-        qv = qv_bias[l].reshape(2, TP, -1).transpose(1, 0, 2).reshape(TP, -1)
-        units = jnp.concatenate([qv, in_bias[l].reshape(TP, -1)], axis=1)
-        units = jnp.pad(units, ((0, 0), (0, cols - units.shape[1])))[:, None]
-        small.append(jnp.pad(jnp.concatenate([features, units], axis=1), ((0, 0), (0, 9), (0, 0))))
-    packed, extras = jnp.stack(groups), jnp.concatenate(small, axis=1)[None]
+    attn = jnp.concatenate([w_qkv.transpose(0, 1, 3, 2), w_out[:, None]], axis=1).reshape(LAYERS, 4, TP, HD, cols)
+    inner = w_in.transpose(0, 2, 1).reshape(LAYERS, TP, 4, HD, cols)
+    down = w_down.reshape(LAYERS, TP, 4, HD, cols)
+    qv = qv_bias.reshape(LAYERS, 1, -1)
+    small = jnp.concatenate(
+        [
+            gains, shifts, in_bias.reshape(LAYERS, 1, cols),
+            jnp.pad(qv, ((0, 0), (0, 0), (0, cols - qv.shape[2]))),
+            jnp.zeros((LAYERS, 8, cols), bf16),
+        ],
+        axis=1,
+    ).reshape(1, 16 * LAYERS, cols)
     if cols % 128 == 0:
-        return packed, extras, True
-    return gather_roles(pl, packed), gather_roles(pl, extras), False
+        return attn, inner, down, small, True
+    attn = gather_roles(pl, attn.transpose(0, 2, 1, 3, 4).reshape(LAYERS, TP, 256, cols))
+    inner, down = [gather_roles(pl, v.reshape(LAYERS, TP, 256, cols)) for v in (inner, down)]
+    small = gather_roles(pl, jnp.broadcast_to(small[:, None], (1, TP) + small.shape[1:]))
+    attn, inner, down = [v.reshape(LAYERS, 4, HD, TP * cols) for v in (attn, inner, down)]
+    return attn, inner, down, small, False
 
 
 def gather_roles(pl, pack):
@@ -1498,13 +1541,13 @@
     per = HD // fsdp
     tokens = images.shape[1]
     rows = -(-tokens // 32) * 32
-    packed, extras, direct = pack_inputs(
+    attn, inner, down, extras, direct = pack_inputs(
         places, w_qkv, w_out, w_in, w_down, qv_bias, in_bias, gains, shifts
     )
-    pad = ((0, rows - tokens), (0, 0))
-    own_image = jnp.pad(lax.dynamic_index_in_dim(images, places.plane // 2, 0, False), pad)
-    own_cot = jnp.pad(lax.dynamic_index_in_dim(cotangent, places.plane // 2, 0, False), pad)
-    kept = forward_call(fsdp, head, tokens, rows, direct, own_image, own_cot, packed, extras)
+    pad = ((0, 0), (0, rows - tokens), (0, 0))
+    kept = forward_call(
+        fsdp, head, tokens, rows, direct, jnp.pad(images, pad), jnp.pad(cotangent, pad), attn, inner, down, extras
+    )
     block_out, input_grad, grads, small = backward_call(fsdp, head, tokens, rows, direct, kept)
     if not direct:
         grads, small = scatter_roles(places, grads), scatter_roles(places, small)
@@ -1512,9 +1555,9 @@
     attn = grads[:, 0].reshape(LAYERS, TP, 4, HD, cols).transpose(0, 2, 1, 3, 4).reshape(LAYERS, 4, TP * HD, cols)
     small = small.astype(f32).reshape(TP, LAYERS, 16, cols)
     features = small[0, :, 0:6]
-    units = small[:, :, 6].transpose(1, 0, 2)
-    qv = units[:, :, 0 : 2 * per].reshape(LAYERS, TP, 2, per).transpose(0, 2, 1, 3).reshape(LAYERS, 2, TP * per, 1)
-    inner = units[:, :, 2 * per : 6 * per].reshape(LAYERS, TP * 4 * per, 1)
+    units = jnp.sum(small[:, :, 6:8], axis=0)
+    qv = units[:, 1, 0 : 2 * TP * per].reshape(LAYERS, 2, TP * per, 1)
+    inner = units[:, 0].reshape(LAYERS, cols, 1)
     return (
         block_out[:, :tokens].astype(f32),
         input_grad[:, :tokens].astype(f32),

time: 494 us -> 466 us (0.943)
  Pallas kernels: 440 us -> 423 us
  local copies, waits for them, and re-layouts: 41.2 us -> 32.5 us
    pallas_call x1, Pallas kernels: 249 us -> 234 us  [backward_call(): pl.pallas_call(functools.partial(backward_kernel, (fsdp, head, tokens, ro...]
    slice x9 -> x1, local copies, waits for them, and re-layouts: 5.44 us -> 0.02 us  [body(): qv = units[:, 1, 0:2 * TP * per].reshape(LAYERS, 2, TP * per, 1)]
    unnamed x22 -> x12, local copies, waits for them, and re-layouts: 17.6 us -> 15.7 us
where the time goes in v5:
time: 466 us; the launch traced here: 462 us
  Pallas kernels  423 us (91%)
  local copies, waits for them, and re-layouts  32.5 us (7%)
  other arithmetic  5.38 us (1%)
    pallas_call x1, Pallas kernels, backward_call(): pl.pallas_call(functools.partial(backward_kernel, (fsdp, head, tokens, ro...  234 us
    pallas_call x1, Pallas kernels, forward_call(): pl.pallas_call(functools.partial(forward_kernel, (fsdp, head, tokens, row...  189 us
    unnamed x12, local copies, waits for them, and re-layouts  15.7 us

profile of v5, /device:TPU:1, one launch (start us, length us, event | category | flops | bytes accessed | tf_op | source)
XLA Modules:
  0.0 461.7 jit_solution(7598541015796487720)
XLA Ops:
  0.6 0.0 copy-start
  0.7 0.9 reshape.68
  1.6 0.7 copy.36
  2.2 1.9 concatenate.14
  4.1 1.2 copy.34
  5.4 1.7 pad_maximum_fusion.refs_2_
  7.1 2.0 copy.35
  9.2 0.0 copy-done
  9.2 0.7 copy.32
  9.9 0.0 copy-start.1
  9.9 1.7 pad.11.refs_0_
  11.6 0.9 copy-done.1
  12.4 0.7 copy.33
  13.2 1.7 pad.12.refs_1_
  14.8 189.1 %forward_layers.1 = (bf16[6,4,4,64,1024]{4,3,2,1,0:T(8,128)(2,1)}, f32[2,8,1024]{2,1,0:T(8,128)}, bf16[2,2,2,608,1024]{4,3,2,1,0:T(8,128)(2,1)}, bf16[2,2,2,608,...) custom-call(bf16[2,608,1024]{2,1,0:T(8,128)(2,1)} %pad.11.refs_0_, ...), custom_call_target="tpu_custom_call" | custom-call | tf_op jit(solution)/shard_map/forward_layers/pallas_call | solution.py:667
  203.9 233.9 %backward_layers.1 = (bf16[2,608,1024]{2,1,0:T(8,128)(2,1)}, bf16[2,608,1024]{2,1,0:T(8,128)(2,1)}, bf16[6,4,256,128]{3,2,1,0:T(8,128)(2,1)}, bf16[1,4,32,128]{3,2,1,0:T(8,128)(2,1)}) custom-call(bf16[6,4,4,64,1024]{4,3,2,1,0:T(8,128)(2,1)} %get-tuple-element.26.refs_0_, f32[2,8,1024]{2,1,0:T(8,128)} %get-tuple-element.27.refs_1_, ...), custom_call_target="tpu_custom_call" | custom-call | tf_op jit(solution)/shard_map/backward_layers/pallas_call | solution.py:1449
  437.8 0.8 convert.3
  438.6 0.6 slice_bitcast_fusion.3
  439.2 0.7 reshape_squeeze.18
  439.8 0.6 slice.61
  440.4 0.6 slice.62
  441.0 2.7 fusion
  443.7 1.3 copy.45
  445.0 0.0 copy-start.2
  445.0 0.1 copy.38
  445.1 0.7 slice_bitcast_fusion.1
  445.8 0.1 slice_bitcast_fusion
  445.8 1.1 copy.42
  447.0 0.0 copy-done.2
  447.0 2.9 slice_convert_fusion
  449.8 5.8 %copy.41 = f32[2,577,1024]{2,0,1:T(2,128)} copy(f32[2,577,1024]{2,1,0:T(8,128)S(1)} %get-tuple-element.65) | data formatting | bytes 9453568
  455.7 5.8 %copy.40 = f32[2,577,1024]{2,0,1:T(2,128)} copy(f32[2,577,1024]{2,1,0:T(8,128)S(1)} %get-tuple-element.66) | data formatting | bytes 9453568
  (5 shorter events, 0.0 us)
Async XLA Ops:
  0.6 8.5 %copy-start = (bf16[2,577,1024]{2,0,1:T(2,128)(2,1)S(1)}, bf16[2,577,1024]{2,0,1:T(2,128)(2,1)}, u32[]{:S(2)}) copy-start(bf16[2,577,1024]{2,0,1:T(2,128)(2,1)} %param.10) | copy-start | bytes 7090180
  9.9 2.6 copy-start.1
  445.0 2.0 copy-start.2

commit v6 on v5

--- a/solution.py
+++ b/solution.py
@@ -48,7 +48,8 @@
         index = lax.axis_index("fsdp")
         self.index = index
         self.block, self.role, self.plane = index // TP, index % TP, lax.axis_index("head")
-        self.core, self.side = self.role % 2, self.role // 2
+        self.core = self.role % 2
+        self.image = (self.role // 2 + self.plane) % 2
 
     def at(self, block=None, role=None, plane=None):
         block = self.block if block is None else block
@@ -327,7 +328,7 @@
         spot, sent, core_in, chip, side_in, full, (core_s, core_r), (side_s, side_r), (back_s, back_r)
     )
     owner = spot.core == spot.plane % 2
-    x, other_x = spot.side, 1 - spot.side
+    x, other_x = spot.image, 1 - spot.image
 
     small.begin(0)
     large.begin(0)
@@ -372,11 +373,12 @@
             down[0].wait_recv()
             down[1].wait_recv()
 
+    large.spread(0)
+    small.spread(0)
+    large.begin(1)
     share_begin(own_image, pair, 0)
-    for g in range(1, groups):
+    for g in (2, 5, 3, 4):
         large.begin(g)
-    small.spread(0)
-    large.spread(0)
     small.relay(0, 1)
     large.relay(0, 1)
     large.spread(1)
@@ -485,6 +487,16 @@
         att[i] = jnp.transpose(att_sum[...]).astype(bf16)
         store_att.start()
         store_lse.start()
+
+        @pl.when(jnp.logical_and(l == 0, i == 0))
+        def _():
+            large.relay(1, 2)
+
+        @pl.when(jnp.logical_and(l == 0, i == 1))
+        def _():
+            large.relay(1, 3)
+            large.relay(2, 2)
+
         exchange.reduce(
             i, lambda at: dot(att[i], whole[g, :, 3, :, at].reshape(256, HALF), 1, 0), kept
         )
@@ -509,6 +521,15 @@
             active[:, at] = (v * (0.5 + 0.5 * lax.erf(v * (0.5**0.5)))).astype(bf16)
         store_hidden.start()
 
+        @pl.when(jnp.logical_and(l == 0, i == 0))
+        def _():
+            large.relay(3, 2)
+
+        @pl.when(jnp.logical_and(l == 0, i == 1))
+        def _():
+            large.relay(5, 1)
+            large.relay(4, 2)
+
         @pl.when(jnp.logical_and(i == 0, l < LAYERS - 1))
         def _():
             large.complete(g + 2)
@@ -541,7 +562,6 @@
             @pl.when(jnp.logical_and(l == 0, i == 0))
             def _():
                 share_begin(own_cot, cots, 1)
-                large.relay(1, 2)
                 large.relay(2, 1)
                 large.spread(3)
 
@@ -555,8 +575,6 @@
 
         @pl.when(l == 0)
         def _():
-            large.relay(1, 3)
-            large.relay(2, 2)
             large.relay(3, 1)
             large.spread(4)
             large.relay(2, 3)
@@ -569,10 +587,8 @@
 
             @pl.when(jnp.logical_and(l == 0, i == 0))
             def _():
-                large.relay(3, 2)
                 large.relay(4, 1)
                 large.relay(3, 3)
-                large.relay(5, 1)
 
             return carry
 
@@ -580,7 +596,6 @@
 
         @pl.when(l == 0)
         def _():
-            large.relay(4, 2)
             large.relay(4, 3)
             large.relay(5, 2)
 
@@ -938,7 +953,7 @@
         copy.start()
 
     last_copy = send(
-        last_chip.at[1 - spot.side], last_in, (last_s, last_r), (0,), spot.at(role=flip2(spot.role))
+        last_chip.at[1 - spot.image], last_in, (last_s, last_r), (0,), spot.at(role=flip2(spot.role))
     )
     half_copy = send(
         result.at[:, exchange.mine], result.at[:, exchange.mine], (last_s, last_r), (1,),
@@ -999,14 +1014,14 @@
             for copy in outs:
                 copy.wait_send()
 
-    chunks = [(start, min(160, rows - start)) for start in range(0, 640, 160)]
-    assert sum(size for _, size in chunks) == rows
+    chunk = -(-rows // 4 // 16) * 16
+    chunks = [(start, min(chunk, rows - start)) for start in range(0, rows, chunk)]
     last_plane = spot.planes - 1
 
     def line_copy(s, j, up, first):
         start, size = chunks[j]
         target = in_pair.at[s, start : start + size]
-        source = up_low.at[spot.side, start : start + size] if first else target
+        source = up_low.at[spot.image, start : start + size] if first else target
         return pltpu.make_async_remote_copy(
             src_ref=source, dst_ref=target, send_sem=line_s.at[s, j, 0 if up else 1], recv_sem=line_r.at[s, j],
             device_id=spot.at(plane=spot.plane + (1 if up else -1)), device_id_type=MESH,
@@ -1026,7 +1041,7 @@
                 act(up, False)
 
     def line_kept(s):
-        return pltpu.make_async_copy(up_low.at[spot.side], in_pair.at[s], load_sem.at[13])
+        return pltpu.make_async_copy(up_low.at[spot.image], in_pair.at[s], load_sem.at[13])
 
     def line_begin():
         for s in range(2):
@@ -1220,10 +1235,10 @@
         @pl.when(l == top)
         def _():
             last_copy.wait_recv()
-            load_stream = load(stream_in.at[spot.side], big.at[:, 0:D], 11)
+            load_stream = load(stream_in.at[spot.image], big.at[:, 0:D], 11)
             load_stream.start()
 
-            v = last_chip[spot.side].astype(f32) + last_in[...].astype(f32)
+            v = last_chip[spot.image].astype(f32) + last_in[...].astype(f32)
             result[:, exchange.mine] = v.astype(bf16)
             load_stream.wait()
 
@@ -1328,10 +1343,14 @@
     def last_image(i, carry):
         exchange.finish(i, 1)
         norm_back(0, 0, i)
+
+        @pl.when(i == spot.image)
+        def _():
+            line_begin()
+
         return carry
 
     lax.fori_loop(0, 2, last_image, 0)
-    line_begin()
     picks = normed.at[0]
     unit_picks(picks, fsdp, spot.role)
     for l in range(LAYERS):
@@ -1350,36 +1369,36 @@
             block = jnp.concatenate(features + [row, other_row, jnp.zeros((8, D), f32)], axis=0)
             small_term[0, plane, 16 * l : 16 * l + 16] = block.astype(bf16)
     small.send_terms(0)
+    scatter.hop(end - 3, 1)
     scatter.hop(end - 4, 3)
     scatter.hand_out(end - 4)
-    scatter.hop(end - 3, 1)
+    scatter.sum_blocks(end - 2)
     line_relay(0)
-    scatter.sum_blocks(end - 2)
     scatter.hop(end - 3, 2)
+    scatter.sum_blocks(end - 1, 0)
     line_relay(1)
-    scatter.sum_blocks(end - 1, 0)
     small.sum_blocks(0)
-    line_relay(2)
     scatter.hop(end - 2, 1)
     scatter.sum_blocks(end - 1, 1)
+    scatter.hop(end - 1, 1, 0)
+    line_relay(2)
+    small.hop(0, 1)
     scatter.hop(end - 3, 3)
     scatter.hand_out(end - 3)
+    scatter.hop(end - 1, 1, 1)
+    scatter.hop(end - 2, 2)
+    scatter.hop(end - 1, 2, 0)
     line_relay(3)
-    scatter.hop(end - 2, 2)
-    scatter.hop(end - 1, 1, 0)
-    small.hop(0, 1)
+    small.hop(0, 2)
+    scatter.hop(end - 1, 2, 1)
     scatter.hop(end - 2, 3)
     scatter.hand_out(end - 2)
-    scatter.hop(end - 1, 1, 1)
-    scatter.hop(end - 1, 2, 0)
-    small.hop(0, 2)
-    scatter.hop(end - 1, 2, 1)
     scatter.hop(end - 1, 3, 0)
     scatter.hand_out(end - 1, 0)
+    small.hop(0, 3)
+    small.hand_out(0)
     scatter.hop(end - 1, 3, 1)
     scatter.hand_out(end - 1, 1)
-    small.hop(0, 3)
-    small.hand_out(0)
     scatter.finish((0, 1))
     small.finish()
     return_end(out_pair)
@@ -1540,7 +1559,7 @@
     cols = w_qkv.shape[2]
     per = HD // fsdp
     tokens = images.shape[1]
-    rows = -(-tokens // 32) * 32
+    rows = -(-tokens // 16) * 16
     attn, inner, down, extras, direct = pack_inputs(
         places, w_qkv, w_out, w_in, w_down, qv_bias, in_bias, gains, shifts
     )
@@ -1559,8 +1578,8 @@
     qv = units[:, 1, 0 : 2 * TP * per].reshape(LAYERS, 2, TP * per, 1)
     inner = units[:, 0].reshape(LAYERS, cols, 1)
     return (
-        block_out[:, :tokens].astype(f32),
-        input_grad[:, :tokens].astype(f32),
+        lax.optimization_barrier(block_out[:, :tokens]).astype(f32),
+        lax.optimization_barrier(input_grad[:, :tokens]).astype(f32),
         attn[:, :3].transpose(0, 1, 3, 2),
         attn[:, 3],
         grads[:, 1].reshape(LAYERS, TP * 256, cols).transpose(0, 2, 1),

time: 466 us -> 450 us (0.966)
  Pallas kernels: 423 us -> 412 us
    pallas_call x1, Pallas kernels: 189 us -> 181 us  [forward_call(): pl.pallas_call(functools.partial(forward_kernel, (fsdp, head, tokens, row...]
    unnamed x12 -> x16, local copies, waits for them, and re-layouts: 15.7 us -> 13.2 us
where the time goes in v6:
time: 450 us; the launch traced here: 445 us
  Pallas kernels  412 us (92%)
  local copies, waits for them, and re-layouts  30.7 us (7%)
    pallas_call x1, Pallas kernels, backward_call(): pl.pallas_call(functools.partial(backward_kernel, (fsdp, head, tokens, ro...  231 us
    pallas_call x1, Pallas kernels, forward_call(): pl.pallas_call(functools.partial(forward_kernel, (fsdp, head, tokens, row...  181 us
    unnamed x16, local copies, waits for them, and re-layouts  13.2 us

profile of v6, /device:TPU:1, one launch (start us, length us, event | category | flops | bytes accessed | tf_op | source)
XLA Modules:
  0.0 445.5 jit_solution(18101724142121118611)
XLA Ops:
  0.6 0.0 copy-start.1
  0.7 0.9 reshape.68
  1.6 0.7 copy.36
  2.2 1.9 concatenate.14
  4.1 1.2 copy.34
  5.4 1.7 pad_maximum_fusion.refs_2_
  7.1 2.0 copy.35
  9.2 0.0 copy-done.1
  9.2 0.7 copy.32
  9.9 0.0 copy-start.2
  9.9 1.7 pad.11.refs_0_
  11.6 0.9 copy-done.2
  12.4 0.7 copy.33
  13.1 1.7 pad.12.refs_1_
  14.8 180.9 %forward_layers.1 = (bf16[6,4,4,64,1024]{4,3,2,1,0:T(8,128)(2,1)}, f32[2,8,1024]{2,1,0:T(8,128)}, bf16[2,2,2,592,1024]{4,3,2,1,0:T(8,128)(2,1)}, bf16[2,2,2,592,...) custom-call(bf16[2,592,1024]{2,1,0:T(8,128)(2,1)} %pad.11.refs_0_, ...), custom_call_target="tpu_custom_call" | custom-call | tf_op jit(solution)/shard_map/forward_layers/pallas_call | solution.py:682
  195.7 231.1 %backward_layers.1 = (bf16[2,592,1024]{2,1,0:T(8,128)(2,1)}, bf16[2,592,1024]{2,1,0:T(8,128)(2,1)}, bf16[6,4,256,128]{3,2,1,0:T(8,128)(2,1)}, bf16[1,4,32,128]{3,2,1,0:T(8,128)(2,1)}) custom-call(bf16[6,4,4,64,1024]{4,3,2,1,0:T(8,128)(2,1)} %get-tuple-element.26.refs_0_, f32[2,8,1024]{2,1,0:T(8,128)} %get-tuple-element.27.refs_1_, ...), custom_call_target="tpu_custom_call" | custom-call | tf_op jit(solution)/shard_map/backward_layers/pallas_call | solution.py:1468
  426.8 0.0 copy-start.4
  426.8 1.9 slice.39
  428.7 0.0 copy-done.4
  428.8 0.6 slice_bitcast_fusion.3
  429.4 0.7 reshape_squeeze.18
  430.0 0.6 slice.61
  430.6 0.6 slice.62
  431.2 0.0 copy-start.3
  431.2 4.6 %copy.40 = f32[2,577,1024]{2,0,1:T(2,128)} copy(bf16[2,577,1024]{2,1,0:T(8,128)(2,1)S(1)} %slice.39) | data formatting | bytes 7090176
  435.8 0.0 copy-done.3
  435.8 0.2 slice.40
  436.0 0.0 copy-start
  436.1 4.6 %copy.41 = f32[2,577,1024]{2,0,1:T(2,128)} copy(bf16[2,577,1024]{2,1,0:T(8,128)(2,1)S(1)} %slice.40) | data formatting | bytes 7090176
  440.7 0.0 copy-done
  440.7 1.3 fusion
  442.0 1.3 copy.45
  443.3 0.1 copy.38
  443.4 0.7 slice_bitcast_fusion.1
  444.1 0.1 slice_bitcast_fusion
  444.2 1.1 copy.42
  (6 shorter events, 0.1 us)
Async XLA Ops:
  0.6 8.5 %copy-start.1 = (bf16[2,577,1024]{2,0,1:T(2,128)(2,1)S(1)}, bf16[2,577,1024]{2,0,1:T(2,128)(2,1)}, u32[]{:S(2)}) copy-start(bf16[2,577,1024]{2,0,1:T(2,128)(2,1)} %param.10) | copy-start | bytes 7090180
  9.9 2.5 copy-start.2
  426.8 1.9 copy-start.4
  431.2 4.6 %copy-start.3 = (bf16[2,592,1024]{2,1,0:T(8,128)(2,1)S(1)}, bf16[2,592,1024]{2,1,0:T(8,128)(2,1)}, u32[]{:S(2)}) copy-start(bf16[2,592,1024]{2,1,0:T(8,128)(2,1)} %get-tuple-element.39) | copy-start | bytes 7274500
  436.0 4.6 %copy-start = (bf16[6,4,256,128]{3,2,1,0:T(8,128)(2,1)S(1)}, bf16[6,4,256,128]{3,2,1,0:T(8,128)(2,1)}, u32[]{:S(2)}) copy-start(bf16[6,4,256,128]{3,2,1,0:T(8,128)(2,1)} %get-tuple-element.40) | copy-start | bytes 4718596

commit v7 on v6

--- a/solution.py
+++ b/solution.py
@@ -298,7 +298,7 @@
 def forward_kernel(cfg, *refs):
     fsdp, head, tokens, rows, direct = cfg
     (
-        images, cotangents, attn_source, in_source, down_source, extras,
+        images, image_rest, cotangents, cot_rest, attn_source, in_source, down_source, extras,
         weights_out, vec_out, normed_out, unit_out, inverse_out, qkv_out, att_out, lse_out, hidden_out,
         stream_out, chip_out, cot_out,
         whole, extra, vec, pair, cots, stream, normed, unit, inverse, qkv, att_sum, att,
@@ -323,7 +323,11 @@
     small = Gather(spot, lambda g, role: extras, extra, *sems, groups, local_sem, direct)
     large = Gather(spot, source, whole, *sems, 0, local_sem, direct)
     large.blocks_first = (groups - 1,)
-    own_image, own_cot = images.at[spot.plane // 2], cotangents.at[spot.plane // 2]
+    whole_rows = tokens // 16 * 16
+    slot = spot.plane // 2
+    own_image, own_cot = [
+        (main.at[slot, 0:whole_rows], rest.at[slot]) for main, rest in ((images, image_rest), (cotangents, cot_rest))
+    ]
     exchange = Exchange(
         spot, sent, core_in, chip, side_in, full, (core_s, core_r), (side_s, side_r), (back_s, back_r)
     )
@@ -335,16 +339,19 @@
 
     def share(source, held, n):
         across = send(
-            source, held.at[x], (share_s, share_r), (n, 0), spot.at(role=flip2(spot.role))
+            held.at[x], held.at[x], (share_s, share_r), (n, 0), spot.at(role=flip2(spot.role))
         )
         across_in = send(
             held.at[other_x], held.at[other_x], (share_s, share_r), (n, 0), spot.at(role=flip2(spot.role))
         )
         down = [
-            send(src, held.at[at], (share_s, share_r), (n, 1 + k), spot.at(role=flip1(spot.role)))
-            for k, (src, at) in enumerate(((source, x), (held.at[other_x], other_x)))
+            send(held.at[at], held.at[at], (share_s, share_r), (n, 1 + k), spot.at(role=flip1(spot.role)))
+            for k, at in enumerate((x, other_x))
         ]
-        mine = pltpu.make_async_copy(source, held.at[x], store_sem.at[30 + n])
+        mine = [
+            pltpu.make_async_copy(source[0], held.at[x, 0:whole_rows], store_sem.at[30 + n]),
+            pltpu.make_async_copy(source[1], held.at[x, whole_rows:rows], store_sem.at[32 + n]),
+        ]
         return across, across_in, down, mine
 
     def share_begin(source, held, n):
@@ -352,8 +359,11 @@
 
         @pl.when(owner)
         def _():
+            for copy in mine:
+                copy.start()
+            for copy in mine:
+                copy.wait()
             across.start()
-            mine.start()
             down[0].start()
 
     def share_end(source, held, n):
@@ -364,7 +374,6 @@
             across_in.wait_recv()
             down[1].start()
             across.wait_send()
-            mine.wait()
             down[0].wait_send()
             down[1].wait_send()
 
@@ -390,6 +399,7 @@
     large.spread(2)
     large.spread(5)
     share_end(own_image, pair, 0)
+    share_begin(own_cot, cots, 1)
     small.complete(0)
 
     unit_picks(active, fsdp, spot.role)
@@ -561,7 +571,6 @@
 
             @pl.when(jnp.logical_and(l == 0, i == 0))
             def _():
-                share_begin(own_cot, cots, 1)
                 large.relay(2, 1)
                 large.spread(3)
 
@@ -677,7 +686,7 @@
         dma((2, 2)), dma((2, 2)),
         dma((2,)), dma((2,)),
         dma((2, 3)), dma((2, 3)),
-        dma((32,)),
+        dma((34,)),
     ]
     return pl.pallas_call(
         functools.partial(forward_kernel, (fsdp, head, tokens, rows, direct)),
@@ -1563,9 +1572,12 @@
     attn, inner, down, extras, direct = pack_inputs(
         places, w_qkv, w_out, w_in, w_down, qv_bias, in_bias, gains, shifts
     )
+    edge = tokens // 16 * 16
     pad = ((0, 0), (0, rows - tokens), (0, 0))
+    image_rest, cot_rest = [jnp.pad(v[:, edge:], pad) for v in (images, cotangent)]
     kept = forward_call(
-        fsdp, head, tokens, rows, direct, jnp.pad(images, pad), jnp.pad(cotangent, pad), attn, inner, down, extras
+        fsdp, head, tokens, rows, direct,
+        images, image_rest, cotangent, cot_rest, attn, inner, down, extras,
     )
     block_out, input_grad, grads, small = backward_call(fsdp, head, tokens, rows, direct, kept)
     if not direct:

time: 450 us -> 448 us (level)
    unnamed x16 -> x20, local copies, waits for them, and re-layouts: 13.2 us -> 14 us
where the time goes in v7:
time: 448 us; the launch traced here: 444 us
  Pallas kernels  412 us (92%)
  local copies, waits for them, and re-layouts  29.5 us (7%)
    pallas_call x1, Pallas kernels, backward_call(): pl.pallas_call(functools.partial(backward_kernel, (fsdp, head, tokens, ro...  231 us
    pallas_call x1, Pallas kernels, forward_call(): pl.pallas_call(functools.partial(forward_kernel, (fsdp, head, tokens, row...  181 us
    unnamed x20, local copies, waits for them, and re-layouts  14 us

profile of v7, /device:TPU:1, one launch (start us, length us, event | category | flops | bytes accessed | tf_op | source)
XLA Modules:
  0.0 444.3 jit_solution(10791710428535250680)
XLA Ops:
  0.6 0.0 copy-start.3
  0.7 0.9 reshape.68
  1.6 0.7 copy.38
  2.2 1.9 concatenate.14
  4.1 1.2 copy.36
  5.4 1.7 pad_maximum_fusion.refs_4_
  7.1 2.0 copy.37
  9.1 0.0 copy-start.4
  9.1 0.0 copy-done.3
  9.1 0.7 copy.40.refs_0_
  9.9 0.0 copy-start
  9.9 0.7 pad.11.refs_1_
  10.6 0.2 copy-done.4
  10.8 0.7 copy.41.refs_2_
  11.5 0.0 copy-start.1
  11.5 1.4 copy-done.1
  13.0 0.0 copy-done
  13.0 0.6 pad.12.refs_3_
  13.6 180.9 %forward_layers.1 = (bf16[6,4,4,64,1024]{4,3,2,1,0:T(8,128)(2,1)}, f32[2,8,1024]{2,1,0:T(8,128)}, bf16[2,2,2,592,1024]{4,3,2,1,0:T(8,128)(2,1)}, bf16[2,2,2,592,...) custom-call(bf16[2,577,1024]{2,1,0:T(8,128)(2,1)} %copy-done, ...), custom_call_target="tpu_custom_call" | custom-call | tf_op jit(solution)/shard_map/forward_layers/pallas_call | solution.py:691
  194.5 231.1 %backward_layers.1 = (bf16[2,592,1024]{2,1,0:T(8,128)(2,1)}, bf16[2,592,1024]{2,1,0:T(8,128)(2,1)}, bf16[6,4,256,128]{3,2,1,0:T(8,128)(2,1)}, bf16[1,4,32,128]{3,2,1,0:T(8,128)(2,1)}) custom-call(bf16[6,4,4,64,1024]{4,3,2,1,0:T(8,128)(2,1)} %get-tuple-element.26.refs_0_, f32[2,8,1024]{2,1,0:T(8,128)} %get-tuple-element.27.refs_1_, ...), custom_call_target="tpu_custom_call" | custom-call | tf_op jit(solution)/shard_map/backward_layers/pallas_call | solution.py:1477
  425.7 0.0 copy-start.6
  425.7 1.9 slice.47
  427.6 0.0 copy-done.6
  427.6 0.6 slice_bitcast_fusion.3
  428.2 0.7 reshape_squeeze.18
  428.9 0.6 slice.71
  429.4 0.6 slice.72
  430.0 0.0 copy-start.5
  430.0 4.6 %copy.44 = f32[2,577,1024]{2,0,1:T(2,128)} copy(bf16[2,577,1024]{2,1,0:T(8,128)(2,1)S(1)} %slice.47) | data formatting | bytes 7090176
  434.7 0.0 copy-done.5
  434.7 0.2 slice.48
  434.9 0.0 copy-start.2
  434.9 4.6 %copy.45 = f32[2,577,1024]{2,0,1:T(2,128)} copy(bf16[2,577,1024]{2,1,0:T(8,128)(2,1)S(1)} %slice.48) | data formatting | bytes 7090176
  439.5 0.0 copy-done.2
  439.5 1.3 fusion
  440.8 1.3 copy.49
  442.1 0.1 copy.42
  442.2 0.7 slice_bitcast_fusion.1
  442.9 0.1 slice_bitcast_fusion
  443.0 1.1 copy.46
  (8 shorter events, 0.1 us)
Async XLA Ops:
  0.6 8.5 %copy-start.3 = (bf16[2,577,1024]{2,0,1:T(2,128)(2,1)S(1)}, bf16[2,577,1024]{2,0,1:T(2,128)(2,1)}, u32[]{:S(2)}) copy-start(bf16[2,577,1024]{2,0,1:T(2,128)(2,1)} %param.10) | copy-start | bytes 7090180
  9.1 1.7 copy-start.4
  9.9 3.1 copy-start
  11.5 1.4 copy-start.1
  425.7 1.9 copy-start.6
  430.0 4.6 %copy-start.5 = (bf16[2,592,1024]{2,1,0:T(8,128)(2,1)S(1)}, bf16[2,592,1024]{2,1,0:T(8,128)(2,1)}, u32[]{:S(2)}) copy-start(bf16[2,592,1024]{2,1,0:T(8,128)(2,1)} %get-tuple-element.39) | copy-start | bytes 7274500
  434.9 4.6 %copy-start.2 = (bf16[6,4,256,128]{3,2,1,0:T(8,128)(2,1)S(1)}, bf16[6,4,256,128]{3,2,1,0:T(8,128)(2,1)}, u32[]{:S(2)}) copy-start(bf16[6,4,256,128]{3,2,1,0:T(8,128)(2,1)} %get-tuple-element.40) | copy-start | bytes 4718596
